TPU v7x, 128 devices: a whole 4x4x4 slice. The times are simulated.
128 devices in a mesh: view: 2 (over core), tile: 64 (over z, x, y).
Axes of the slice: x: 4, y: 4, z: 4, core: 2. Of those that a mesh axis runs over, the one named last changes fastest.
Arguments:
- params: float32 [59, 1048576], P(None, 'tile'), may hold values from -5 to 1032, as said below
- first_moment: float32 [59, 1048576], P(None, 'tile'), may hold values from -4 to 4
- second_moment: float32 [59, 1048576], P(None, 'tile'), may hold values from 0.1 to 10
- target: float32 [2, 3, 1024, 512], P('view', None, 'tile'), may hold values from 0 to 1
- view_shear: float32 [2, 2], replicated, may hold values from -1 to 1
- view_offset: float32 [2, 2], replicated, may hold values from -1.5 to 1.5
- cam_center: float32 [2, 3], replicated, may hold values from 40 to 200
- background: float32 [2, 3], replicated, may hold values from 0 to 1
- send_index: int32 [64, 64, 128], P('tile'), may hold values from 0 to 16383, as said below
- send_count: int32 [64, 64], P('tile'), may hold values from 0 to 128, as said below
- tile_list: int32 [2, 64, 32, 256], P('view', 'tile'), may hold values from 0 to 8191, as said below
- tile_count: int32 [64, 32], P('tile'), may hold values from 16 to 256, as said below
Outputs:
- new_params: float32 [59, 1048576], P(None, 'tile')
- new_first: float32 [59, 1048576], P(None, 'tile')
- new_second: float32 [59, 1048576], P(None, 'tile')
- mean_loss: float32 [], replicated
Inputs may be any that keep to these rules, and one draw needn't show every extreme that they name: `params`: row 2 lies in [-3, 3], row 6 in [0.6, 1.4], rows 7 to 9 in [-0.6, 0.6]. `send_index`: slot k of pair (o, d) holds a local index when k < send_count[o, d], else 0; no Gaussian of an owner is live in two slots. `send_count`: some pair fills all 128 slots. `tile_list`: a live entry of row d is o * 128 + k with k < send_count[o, d]; entries past tile_count are 0; in each view every live slot of row d appears in exactly one live entry of row d. `tile_count`: some tile holds all 256 entries.
All inputs are finite; a program needn't handle non-finite values.
Results may differ from a plain program's by a relative error of at most 0.0003.
Values sent between devices are 32-bit elements; how exact they have to be, the bound alone decides.
A program may use at most 256 MiB of HBM per device.

v0:
```python
import math

import jax
import jax.numpy as jnp
from jax import lax
from jax.sharding import PartitionSpec as P

STEP_COUNT = 20
LIST = 256


def extended(block, sides, width):
    for axis, dim in sides:
        count = lax.axis_size(axis)
        forward = [(i, i + 1) for i in range(count - 1)]
        backward = [(target, source) for source, target in forward]
        low = lax.ppermute(
            lax.slice_in_dim(block, block.shape[dim] - width, None, axis=dim), axis, forward
        )
        high = lax.ppermute(lax.slice_in_dim(block, 0, width, axis=dim), axis, backward)
        block = jnp.concatenate([low, block, high], axis=dim)
    return block


def window_taps():
    raw_taps = [math.exp(-(position - 5) * (position - 5) / 4.5) for position in range(11)]
    return [element / sum(raw_taps) for element in raw_taps]


def harmonics(unit_x, unit_y, unit_z):
    square_x = unit_x * unit_x
    square_y = unit_y * unit_y
    square_z = unit_z * unit_z
    return jnp.stack(
        [
            0.28209479177387814 * jnp.ones_like(unit_x),
            -0.4886025119029199 * unit_y,
            0.4886025119029199 * unit_z,
            -0.4886025119029199 * unit_x,
            1.0925484305920792 * unit_x * unit_y,
            -1.0925484305920792 * unit_y * unit_z,
            0.31539156525252005 * (2.0 * square_z - square_x - square_y),
            -1.0925484305920792 * unit_x * unit_z,
            0.5462742152960396 * (square_x - square_y),
            -0.5900435899266435 * unit_y * (3.0 * square_x - square_y),
            2.890611442640554 * unit_x * unit_y * unit_z,
            -0.4570457994644658 * unit_y * (4.0 * square_z - square_x - square_y),
            0.3731763325901154 * unit_z * (2.0 * square_z - 3.0 * square_x - 3.0 * square_y),
            -0.4570457994644658 * unit_x * (4.0 * square_z - square_x - square_y),
            1.445305721320277 * unit_z * (square_x - square_y),
            -0.5900435899266435 * unit_x * (square_x - 3.0 * square_y),
        ]
    )


def project(params, view_shear, view_offset, center):
    pos_x = params[0]
    pos_y = params[1]
    pos_z = params[2]
    scales = jnp.exp(params[3:6])
    quaternion = params[6:10]
    quaternion = quaternion / jnp.sqrt(jnp.sum(quaternion * quaternion, axis=0))
    quat_w = quaternion[0]
    quat_x = quaternion[1]
    quat_y = quaternion[2]
    quat_z = quaternion[3]
    rotation_matrix = [
        [
            1.0 - 2.0 * (quat_y * quat_y + quat_z * quat_z),
            2.0 * (quat_x * quat_y - quat_w * quat_z),
            2.0 * (quat_x * quat_z + quat_w * quat_y),
        ],
        [
            2.0 * (quat_x * quat_y + quat_w * quat_z),
            1.0 - 2.0 * (quat_x * quat_x + quat_z * quat_z),
            2.0 * (quat_y * quat_z - quat_w * quat_x),
        ],
        [
            2.0 * (quat_x * quat_z - quat_w * quat_y),
            2.0 * (quat_y * quat_z + quat_w * quat_x),
            1.0 - 2.0 * (quat_x * quat_x + quat_y * quat_y),
        ],
    ]
    shear_x = view_shear[0]
    shear_y = view_shear[1]
    row_first = [
        (rotation_matrix[0][column] + shear_x * rotation_matrix[2][column]) * scales[column]
        for column in range(3)
    ]
    row_second = [
        (rotation_matrix[1][column] + shear_y * rotation_matrix[2][column]) * scales[column]
        for column in range(3)
    ]
    cov_xx = (
        row_first[0] * row_first[0]
        + row_first[1] * row_first[1]
        + row_first[2] * row_first[2]
        + 0.3
    )
    cov_yy = (
        row_second[0] * row_second[0]
        + row_second[1] * row_second[1]
        + row_second[2] * row_second[2]
        + 0.3
    )
    cov_xy = (
        row_first[0] * row_second[0] + row_first[1] * row_second[1] + row_first[2] * row_second[2]
    )
    determinant = cov_xx * cov_yy - cov_xy * cov_xy
    screen_u = pos_x + shear_x * pos_z + view_offset[0]
    screen_v = pos_y + shear_y * pos_z + view_offset[1]
    opacity = jax.nn.sigmoid(params[10])
    toward_x = pos_x - center[0]
    toward_y = pos_y - center[1]
    toward_z = pos_z - center[2]
    length = jnp.sqrt(toward_x * toward_x + toward_y * toward_y + toward_z * toward_z)
    harmonic = harmonics(toward_x / length, toward_y / length, toward_z / length)
    coefficients = params[11:].reshape(16, 3, -1)
    splat_colors = 0.5 + jnp.sum(harmonic[:, None, :] * coefficients, axis=0)
    return jnp.stack(
        [
            screen_u,
            screen_v,
            cov_yy / determinant,
            -cov_xy / determinant,
            cov_xx / determinant,
            opacity,
            splat_colors[0],
            splat_colors[1],
            splat_colors[2],
        ]
    )


def blocked_prefix(log_keep):
    tile_total, length, pixels = log_keep.shape
    blocks = length // 128
    row_ids = lax.broadcasted_iota(jnp.int32, (128, 128), 0)
    column_ids = lax.broadcasted_iota(jnp.int32, (128, 128), 1)
    lower = (column_ids < row_ids).astype(jnp.float32)
    grouped = log_keep.reshape(tile_total, blocks, 128, pixels)
    inside = jnp.einsum("jk,tbkp->tbjp", lower, grouped, precision=lax.Precision.HIGHEST)
    block_sums = jnp.sum(grouped, axis=2)
    before = jnp.cumsum(block_sums, axis=1) - block_sums
    running_prefix = (inside + before[:, :, None, :]).reshape(tile_total, length, pixels)
    return (running_prefix, jnp.sum(block_sums, axis=1))


def render_band(entry_records, is_live, band_id, backdrop):
    tile_total = entry_records.shape[1]
    pixels = jnp.arange(256, dtype=jnp.int32)
    column_pos = (pixels % 16).astype(jnp.float32) + 0.5
    row_pos = (pixels // 16).astype(jnp.float32) + 0.5
    pixel_x = 16.0 * jnp.arange(tile_total, dtype=jnp.float32)[:, None] + column_pos[None, :]
    pixel_y = 16.0 * band_id.astype(jnp.float32) + row_pos
    delta_x = pixel_x[:, None, :] - entry_records[0][:, :, None]
    delta_y = pixel_y[None, None, :] - entry_records[1][:, :, None]
    exponent = (
        -0.5
        * (
            entry_records[2][:, :, None] * delta_x * delta_x
            + entry_records[4][:, :, None] * delta_y * delta_y
        )
        - entry_records[3][:, :, None] * delta_x * delta_y
    )
    coverage = jnp.where(is_live[:, :, None], entry_records[5][:, :, None] * jnp.exp(exponent), 0.0)
    log_keep = jnp.log1p(-coverage)
    running_prefix, log_total = blocked_prefix(log_keep)
    blend_weights = coverage * jnp.exp(running_prefix)
    splat_colors = jnp.einsum(
        "qvr,fqv->fqr", blend_weights, entry_records[6:9], precision=lax.Precision.HIGHEST
    )
    splat_colors = splat_colors + jnp.exp(log_total)[None] * backdrop[:, None, None]
    return (
        splat_colors.reshape(3, tile_total, 16, 16)
        .transpose(0, 2, 1, 3)
        .reshape(3, 16, tile_total * 16)
    )


def gaussian_blur(planes):
    taps = window_taps()
    rows_out = planes.shape[1] - 10
    vertical = taps[0] * planes[:, 0:rows_out]
    for position in range(1, 11):
        vertical = vertical + taps[position] * planes[:, position : position + rows_out]
    image_width = planes.shape[2]
    padded = jnp.pad(vertical, ((0, 0), (0, 0), (5, 5)))
    result = taps[0] * padded[:, :, 0:image_width]
    for position in range(1, 11):
        result = result + taps[position] * padded[:, :, position : position + image_width]
    return result


def ssim_map(level_x, level_y, energy_x, energy_y, product_xy):
    upper = (2.0 * level_x * level_y + 0.0001) * (2.0 * (product_xy - level_x * level_y) + 0.0009)
    lower = (level_x * level_x + level_y * level_y + 0.0001) * (
        energy_x - level_x * level_x + (energy_y - level_y * level_y) + 0.0009
    )
    return upper / lower


def window_stats(widened):
    shown = widened[0:3]
    truth = widened[3:6]
    mean_x = gaussian_blur(shown)
    mean_y = gaussian_blur(truth)
    power_x = gaussian_blur(shown * shown)
    power_y = gaussian_blur(truth * truth)
    cross_xy = gaussian_blur(shown * truth)
    return (mean_x, mean_y, power_x, power_y, cross_xy)


def adam_update(params, first_moment, second_moment, gradient):
    row_ids = jnp.arange(params.shape[0], dtype=jnp.int32)[:, None]
    learning = jnp.where(
        row_ids < 3,
        0.016,
        jnp.where(
            row_ids < 6,
            0.005,
            jnp.where(
                row_ids < 10,
                0.001,
                jnp.where(row_ids < 11, 0.05, jnp.where(row_ids < 14, 0.0025, 0.000125)),
            ),
        ),
    )
    new_first = 0.9 * first_moment + 0.1 * gradient
    new_second = 0.999 * second_moment + 0.001 * gradient * gradient
    corrected = new_first / (1.0 - 0.9**STEP_COUNT)
    scale_second = jnp.sqrt(new_second / (1.0 - 0.999**STEP_COUNT)) + 1e-15
    return (params - learning * corrected / scale_second, new_first, new_second)


def shards(
    params,
    first_moment,
    second_moment,
    target,
    view_shear,
    view_offset,
    cam_center,
    background,
    send_index,
    send_count,
    tile_list,
    tile_count,
):
    view_index = lax.axis_index("view")
    band_index = lax.axis_index("tile")
    band_total = lax.axis_size("tile")
    own_shear = lax.dynamic_index_in_dim(view_shear, view_index, 0, keepdims=False)
    own_offset = lax.dynamic_index_in_dim(view_offset, view_index, 0, keepdims=False)
    own_center = lax.dynamic_index_in_dim(cam_center, view_index, 0, keepdims=False)
    backdrop = lax.dynamic_index_in_dim(background, view_index, 0, keepdims=False)
    records, pull_back = jax.vjp(
        lambda values: project(values, own_shear, own_offset, own_center), params
    )
    slots_out = send_index[0]
    counts_out = send_count[0]
    capacity = slots_out.shape[1]
    was_dispatched = jnp.arange(capacity, dtype=jnp.int32)[None, :] < counts_out[:, None]
    outgoing = jnp.where(was_dispatched[None], records[:, slots_out], 0.0)
    incoming = lax.all_to_all(outgoing, "tile", split_axis=1, concat_axis=1, tiled=True)
    flat_slots = incoming.reshape(9, band_total * capacity)
    tile_lists = tile_list[0, 0]
    is_live = jnp.arange(LIST, dtype=jnp.int32)[None, :] < tile_count[0][:, None]
    entry_records = flat_slots[:, tile_lists]
    image_band, render_back = jax.vjp(
        lambda values: render_band(values, is_live, band_index, backdrop), entry_records
    )
    frame_band = target[0]
    image_width = frame_band.shape[2]
    stacked = jnp.concatenate([image_band, frame_band], axis=0)
    widened = extended(stacked, (("tile", 1),), 5)
    mean_x, mean_y, power_x, power_y, cross_xy = window_stats(widened)
    similarity, ssim_back = jax.vjp(
        lambda level_x, energy_x, product_xy: ssim_map(
            level_x, mean_y, energy_x, power_y, product_xy
        ),
        mean_x,
        power_x,
        cross_xy,
    )
    grad_mean, grad_power, grad_cross = ssim_back(jnp.full_like(similarity, -0.8))
    spread = extended(
        jnp.concatenate([grad_mean, grad_power, grad_cross], axis=0), (("tile", 1),), 5
    )
    blurred = gaussian_blur(spread)
    difference = image_band - frame_band
    smooth = jnp.sqrt(difference * difference + 0.0001)
    loss_part = jnp.sum(0.2 * smooth + 0.8 * (1.0 - similarity))
    pixel_grad = (
        0.2 * difference / smooth
        + blurred[0:3]
        + 2.0 * image_band * blurred[3:6]
        + frame_band * blurred[6:9]
    )
    mean_loss = lax.psum(loss_part, ("view", "tile")) / (
        lax.axis_size("view") * 3 * 16 * band_total * image_width
    )
    entry_grad = render_back(pixel_grad)[0]
    slot_grad = (
        jnp.zeros((9, band_total * capacity), jnp.float32)
        .at[:, tile_lists.reshape(-1)]
        .add(entry_grad.reshape(9, -1))
    )
    returned = lax.all_to_all(
        slot_grad.reshape(9, band_total, capacity), "tile", split_axis=1, concat_axis=1, tiled=True
    )
    returned = jnp.where(was_dispatched[None], returned, 0.0)
    screen_grad = (
        jnp.zeros((9, params.shape[1]), jnp.float32)
        .at[:, slots_out.reshape(-1)]
        .add(returned.reshape(9, -1))
    )
    gradient = lax.psum(pull_back(screen_grad)[0], "view")
    new_params, new_first, new_second = adam_update(params, first_moment, second_moment, gradient)
    return (new_params, new_first, new_second, mean_loss)


def solution(mesh):
    placed = (
        P(None, "tile"),
        P(None, "tile"),
        P(None, "tile"),
        P("view", None, "tile", None),
        P(),
        P(),
        P(),
        P(),
        P("tile", None, None),
        P("tile", None),
        P("view", "tile", None, None),
        P("tile", None),
    )
    return jax.shard_map(
        shards,
        mesh=mesh,
        in_specs=placed,
        out_specs=(P(None, "tile"), P(None, "tile"), P(None, "tile"), P()),
        check_vma=False,
    )
```

profile of v0, /device:TPU:1, one launch (start us, length us, event | category | flops | bytes accessed | tf_op | source)
XLA Modules:
  0.0 703.9 jit_solution(9548766106057801581)
XLA Ops:
  21.1 7.4 %multiply_multiply_fusion.8 = (f32[1,16384]{1,0:T(1,128)S(1)}, f32[1,16384]{1,0:T(1,128)S(1)}, f32[1,16384]{1,0:T(1,128)S(1)}, f32[1,16384]{1,0:T(1,128)S(1)}, f...) fusion(f32[1,16384]{1,0:T(1,128)S(1)} %get-tuple-element.61, ...), kind=kLoop, calls=%fused_computation.527 | loop fusion | flops 393216 | bytes 983068 | tf_op jit(solution)/shard_map/jvp()/mul | solution.py:50
  42.7 4.9 fusion.280
  54.0 31.3 %gather_fusion = f32[8192,9]{1,0:T(8,128)} fusion(f32[9,16384]{0,1:T(8,128)} %copy.423, s32[8192]{0:T(1024)S(1)} %fusion.262), kind=kCustom, calls=%fused_computation | custom fusion | bytes 622592 | tf_op jit(solution)/shard_map/gather | solution.py:264
  89.1 12.4 %all-to-all-start = ((f32[9,64,128]{2,0,1:T(8,128)}), f32[9,64,128]{2,0,1:T(8,128)S(1)}, u32[]{:S(2)}, u32[]{:S(2)}) async-start(f32[9,64,128]{2,0,1:T(8,128)} %select_bitcast_fusion), calls=%async_computation | async-start | bytes 1048576 | tf_op jit(solution)/shard_map/all_to_all | solution.py:265
  101.9 11.5 %all-to-all-done = f32[9,64,128]{2,0,1:T(8,128)S(1)} async-done(((f32[9,64,128]{2,0,1:T(8,128)}), f32[9,64,128]{2,0,1:T(8,128)S(1)}, u32[]{:S(2)}, u32[]{:S(2)}) %all-to-all-start) | async-done | bytes 294944 | tf_op jit(solution)/shard_map/all_to_all | solution.py:265
  116.2 30.1 %gather_fusion.1 = f32[8192,9]{1,0:T(8,128)} fusion(f32[9,8192]{0,1:T(8,128)} %bitcast.130, s32[8192]{0:T(1024)S(1)} %broadcast_clamp_fusion), kind=kCustom, calls=%fused_computation.1 | custom fusion | bytes 622592 | tf_op jit(solution)/shard_map/gather | solution.py:269
  149.4 9.4 %fusion.32 = (f32[32,256]{1,0:T(8,128)S(1)}, f32[32,2,256]{2,1,0:T(2,128)S(1)}) fusion(f32[32,2,128]{2,1,0:T(2,128)S(1)} %bitcast.182, f32[32,2,128]{2,1,0:T(2,128)S(1)} %bitcast.174, f32[256]{0:T(256)S(1)} %get-tuple-element.150, f32[32,2,128]{2,1,0:T(2,128)S(1)} %bitcast.176, f32[32,2,128]{2,1,0:T(2,128)S(1)} %bitcast.178, ...), kind=kLoop, calls=%fused_computation.70 | loop fusion | flops 33529856 | bytes 336896 | tf_op jit(solution)/shard_map/jvp()/reduce_sum | solution.py:146
  159.1 28.5 %add_exponential_fusion = f32[32,2,256,128]{2,3,1,0:T(8,128)S(1)} fusion(f32[32,2,256]{2,1,0:T(2,128)S(1)} %sub.377, f32[32,2,128]{2,1,0:T(2,128)S(1)} %bitcast.183, f32[32,2,128]{2,1,0:T(2,128)S(1)} %bitcast.175, f32[256]{0:T(256)S(1)} %get-tuple-element.150, f32[32,2,128]{2,1,0:T(2,128)S(1)} %bitcast.177, f32[32,2,128]{2,1,0:T(2,128)S(1)} %bitcast.179, ...), kind=kOutput, calls=%fused_computation.58 | convolution fusion | flops 3252699136 | bytes 8692736 | tf_op jit(solution)/shard_map/jvp(jk,tbkp->tbjp)/dot_general | solution.py:142
  187.7 8.9 %bitcast_multiply_fusion.2 = f32[32,256,256]{2,1,0:T(8,128)S(1)} fusion(f32[32,2,256,128]{2,3,1,0:T(8,128)S(1)} %add_exponential_fusion, f32[32,256]{1,0:T(8,128)S(1)} %bitcast.147, f32[32,256]{1,0:T(8,128)S(1)} %bitcast.151, f32[256]{0:T(256)S(1)} %get-tuple-element.150, f32[32,256]{1,0:T(8,128)S(1)} %bitcast.155, f32[32,256]{1,0:T(8,128)S(1)} %bitcast.159, ...), kind=kLoop, calls=%fused_computation.54 | loop fusion | flops 29360128 | bytes 17015808 | tf_op jit(solution)/shard_map/jvp()/mul | solution.py:169
  226.0 10.2 %convolution_bitcast_fusion = f32[3,32,256]{2,0,1:T(4,128)S(1)} fusion(f32[32,3,256]{2,1,0:T(4,128)S(1)} %copy.432, f32[32,256,256]{2,1,0:T(8,128)} %copy-done.2), kind=kOutput, calls=%fused_computation.76 | convolution fusion | flops 75497472 | bytes 8585216 | tf_op jit(solution)/shard_map/transpose(jvp(qvr,fqv->fqr))/dot_general | solution.py:170
  236.2 19.6 %bitcast_reduce_fusion = (f32[32,2,256]{2,1,0:T(2,128)S(1)}, f32[32,256,256]{2,1,0:T(8,128)}, f32[32,256,256]{2,1,0:T(8,128)}) fusion(f32[32,2,256,128]{2,3,1,0:T(8,128)} %copy-done.3, f32[32,256]{1,0:T(8,128)} %bitcast.148, f32[32,256]{1,0:T(8,128)} %bitcast.152, f32[256]{0:T(256)S(1)} %get-tuple-element.150, f32[32,256]{1,0:T(8,128)} %bitcast.156, ...), kind=kOutput, calls=%fused_computation.585 | convolution fusion | flops 109035520 | bytes 25732096 | tf_op jit(solution)/shard_map/transpose(jvp(qvr,fqv->fqr))/dot_general | solution.py:170
  256.0 9.0 %copy.436 = f32[32,2,128,256]{2,3,1,0:T(8,128)} copy(f32[32,2,128,256]{3,2,1,0:T(8,128)} %bitcast.131) | data formatting | bytes 16777216 | tf_op jit(solution)/shard_map/transpose(jvp())/reshape | solution.py:145
  265.5 9.0 %broadcast_add_fusion = f32[32,2,256,128]{2,3,1,0:T(8,128)S(1)} fusion(f32[32,2,256]{2,1,0:T(2,128)S(1)} %add_add_fusion.20, f32[32,2,128,256]{2,3,1,0:T(8,128)} %copy.436), kind=kOutput, calls=%fused_computation.66 | convolution fusion | flops 3223339008 | bytes 16842752 | tf_op jit(solution)/shard_map/transpose(jvp(jk,tbkp->tbjp))/dot_general | solution.py:142
  274.5 11.1 %fusion.26 = f32[32,256,256]{2,1,0:T(8,128)S(1)} fusion(f32[32,2,256,128]{2,3,1,0:T(8,128)S(1)} %broadcast_add_fusion, f32[32,256,256]{2,1,0:T(8,128)} %get-tuple-element.149, f32[32,2,256,128]{2,3,1,0:T(8,128)} %copy-done.3, f32[32,256]{1,0:T(8,128)S(1)} %bitcast.149, f32[32,256]{1,0:T(8,128)S(1)} %bitcast.153, f32[256]{0:T(256)S(1)} %get-tuple-element.150, ...), kind=kLoop, calls=%fused_computation.49 | loop fusion | flops 41943040 | bytes 33793024 | tf_op jit(solution)/shard_map/transpose(jvp(jit(_where)))/select_n | solution.py:166
  285.6 18.6 %fusion.21 = (f32[32,256]{1,0:T(8,128)S(1)}, f32[32,256]{1,0:T(8,128)S(1)}, f32[32,256]{1,0:T(8,128)S(1)}, f32[32,256]{1,0:T(8,128)S(1)}, f32[32,256]{1,0:T(8,128)S(1)}, /*index=5*/f32[32,256]{1,0:T(8,128)S(1)}) fusion(f32[32,256]{1,0:T(8,128)S(1)} %bitcast.154, f32[256]{0:T(256)S(1)} %get-tuple-element.150, f32[32,256]{1,0:T(8,128)S(1)} %bitcast.162, ...), kind=kLoop, calls=%fused_computation.43 | loop fusion | flops 79642624 | bytes 8815616 | tf_op jit(solution)/shard_map/transpose(jvp())/reduce_sum | solution.py:164
  308.1 54.6 %scatter_custom_fusion = f32[9,8192]{0,1:T(8,128)} fusion(s32[8192]{0:T(1024)} %bitcast.187, f32[8192,9]{1,0:T(8,128)} %copy.438, f32[]{:T(128)} %constant.43.clone.1), kind=kCustom, calls=%fused_computation.74 | custom fusion | flops 73728 | bytes 295424 | tf_op jit(solution)/shard_map/scatter-add | solution.py:307
  366.2 18.5 %all-to-all-start.1 = ((f32[9,64,128]{2,0,1:T(8,128)}), f32[9,64,128]{2,0,1:T(8,128)S(1)}, u32[]{:S(2)}, u32[]{:S(2)}) async-start(f32[9,64,128]{2,0,1:T(8,128)} %copy.439), calls=%async_computation.1 | async-start | bytes 1048576 | tf_op jit(solution)/shard_map/all_to_all | solution.py:309
  384.8 10.6 %all-to-all-done.1 = f32[9,64,128]{2,0,1:T(8,128)S(1)} async-done(((f32[9,64,128]{2,0,1:T(8,128)}), f32[9,64,128]{2,0,1:T(8,128)S(1)}, u32[]{:S(2)}, u32[]{:S(2)}) %all-to-all-start.1) | async-done | bytes 294944 | tf_op jit(solution)/shard_map/all_to_all | solution.py:309
  398.7 55.3 %scatter_custom_fusion.1 = f32[9,16384]{0,1:T(8,128)} fusion(s32[8192]{0:T(1024)S(1)} %bitcast.188, f32[8192,9]{1,0:T(8,128)} %copy.441, f32[]{:T(128)} %constant.43.clone.1), kind=kCustom, calls=%fused_computation.68 | custom fusion | flops 73728 | bytes 590336 | tf_op jit(solution)/shard_map/scatter-add | solution.py:316
  454.0 59.5 %fusion.281 = (f32[1,16384]{0,1:T(8,128)}, f32[1,16384]{0,1:T(8,128)}, f32[1,16384]{0,1:T(8,128)}, f32[1,16384]{0,1:T(8,128)}, f32[1,16384]{0,1:T(8,128)}, /*ind...) fusion(f32[9,16384]{0,1:T(8,128)} %scatter_custom_fusion.1), kind=kLoop, calls=%fused_computation.602 | loop fusion | bytes 1179648 | tf_op jit(solution)/shard_map/transpose(jvp())/unstack | solution.py:120
  513.4 5.3 copy.461
  518.8 5.4 copy.462
  524.2 5.3 copy.463
  538.7 13.3 %pad_add_fusion = f32[3,16384]{0,1:T(8,128)} fusion(f32[1,16384]{0,1:T(8,128)} %get-tuple-element.88, f32[1,16384]{0,1:T(8,128)} %get-tuple-element.89, f32[1,16384]{0,1:T(8,128)} %get-tuple-element.90), kind=kLoop, calls=%fused_computation.55 | loop fusion | flops 98304 | bytes 393216 | tf_op jit(solution)/shard_map/transpose(jvp())/add_any | solution.py:128
  552.0 5.5 copy.442
  557.5 6.8 broadcast_multiply_fusion
  578.8 5.9 copy.464
  584.7 5.9 copy.465
  590.6 5.9 copy.460
  597.4 10.7 %fusion.245 = (f32[1,16384]{1,0:T(1,128)S(1)}, f32[1,16384]{1,0:T(1,128)S(1)}, f32[1,16384]{1,0:T(1,128)S(1)}, f32[1,16384]{1,0:T(1,128)S(1)}) fusion(f32[1,16384]{1,0:T(1,128)} %copy.465, f32[1,16384]{1,0:T(1,128)} %copy.464, f32[]{:T(128)} %bitcast.9, f32[]{:T(128)} %bitcast.7, f32[1,16384]{1,0:T(1,128)S(1)} %copy-done.7, f32[]{:T(128)} %bitcast.2, ...), kind=kLoop, calls=%fused_computation.461 | loop fusion | flops 2359296 | bytes 1835028 | tf_op jit(solution)/shard_map/transpose(jvp())/add_any | solution.py:110
  615.5 68.0 %psum.15 = f32[]{:T(128)} all-reduce(f32[]{:T(128)} %get-tuple-element.32), channel_id=1, replica_groups=mesh['view'=2,'tile'=64] {'view','tile'}, use_global_device_ids=true, to_apply=%region_20.21 | all-reduce | flops 1 | bytes 8 | tf_op jit(solution)/shard_map/psum | solution.py:300
  684.2 11.6 %divide_subtract_fusion = (f32[59,16384]{1,0:T(8,128)}, f32[59,16384]{1,0:T(8,128)}, f32[59,16384]{1,0:T(8,128)}) fusion(f32[59,16384]{1,0:T(8,128)} %param.12, f32[59]{0:T(128)S(1)} %fusion.271, f32[59,16384]{1,0:T(8,128)} %all-reduce.35.cloned.1.call-done, f32[59,16384]{1,0:T(8,128)} %param.13, f32[59,16384]{1,0:T(8,128)} %param.14), kind=kLoop, calls=%fused_computation.62 | loop fusion | flops 11599872 | bytes 27066604 | tf_op jit(solution)/shard_map/sub | solution.py:233
  (234 shorter events, 115.3 us)
Async XLA Ops:
  10.9 29.8 %copy-start.20 = (f32[16384]{0:T(1024)}, f32[16384]{0:T(1024)S(1)}, u32[]{:S(2)}) copy-start(f32[16384]{0:T(1024)S(1)} %multiply_reduce_fusion.5) | copy-start | bytes 196612
  33.5 14.2 %copy-start.42 = (f32[1,16384]{1,0:T(1,128)S(1)}, f32[1,16384]{1,0:T(1,128)}, u32[]{:S(2)}) copy-start(f32[1,16384]{1,0:T(1,128)} %get-tuple-element.96) | copy-start | bytes 196612
  33.6 14.2 %copy-start.43 = (f32[1,16384]{1,0:T(1,128)S(1)}, f32[1,16384]{1,0:T(1,128)}, u32[]{:S(2)}) copy-start(f32[1,16384]{1,0:T(1,128)} %get-tuple-element.97) | copy-start | bytes 196612
  41.4 46.8 %copy-start.19 = (f32[16384]{0:T(1024)}, f32[16384]{0:T(1024)S(1)}, u32[]{:S(2)}) copy-start(f32[16384]{0:T(1024)S(1)} %get-tuple-element.139) | copy-start | bytes 196612
  49.2 39.0 %copy-start.52 = (s32[1,64]{1,0:T(1,128)S(1)}, s32[1,64]{1,0:T(1,128)}, u32[]{:S(2)}) copy-start(s32[1,64]{1,0:T(1,128)} %param.21) | copy-start | bytes 772
  49.2 52.4 %copy-start.46 = (s32[1,1,32,256]{3,2,1,0:T(8,128)S(1)}, s32[1,1,32,256]{3,2,1,0:T(8,128)}, u32[]{:S(2)}) copy-start(s32[1,1,32,256]{3,2,1,0:T(8,128)} %param.22) | copy-start | bytes 98308
  49.2 52.4 %copy-start.51 = (s32[1,32]{1,0:T(1,128)S(1)}, s32[1,32]{1,0:T(1,128)}, u32[]{:S(2)}) copy-start(s32[1,32]{1,0:T(1,128)} %param.23) | copy-start | bytes 388
  49.2 52.7 %copy-start.53 = (f32[2,3]{1,0:T(2,128)S(1)}, f32[2,3]{1,0:T(2,128)}, u32[]{:S(2)}) copy-start(f32[2,3]{1,0:T(2,128)} %param.19) | copy-start | bytes 76
  89.1 24.4 %all-to-all-start = ((f32[9,64,128]{2,0,1:T(8,128)}), f32[9,64,128]{2,0,1:T(8,128)S(1)}, u32[]{:S(2)}, u32[]{:S(2)}) async-start(f32[9,64,128]{2,0,1:T(8,128)} %select_bitcast_fusion), calls=%async_computation | async-start | bytes 1048576 | tf_op jit(solution)/shard_map/all_to_all | solution.py:265
  101.7 85.9 %copy-start.49 = (pred[32,256]{1,0:T(8,128)(4,1)}, pred[32,256]{1,0:T(8,128)(4,1)S(1)}, u32[]{:S(2)}) copy-start(pred[32,256]{1,0:T(8,128)(4,1)S(1)} %iota_compare_fusion.1) | copy-start | bytes 24580
  149.3 38.4 %copy-start.23 = (f32[1,32,256]{2,1,0:T(8,128)}, f32[1,32,256]{2,1,0:T(8,128)S(1)}, u32[]{:S(2)}) copy-start(f32[1,32,256]{2,1,0:T(8,128)S(1)} %copy.476) | copy-start | bytes 98308
  149.3 38.3 %copy-start.25 = (f32[1,32,256]{2,1,0:T(8,128)}, f32[1,32,256]{2,1,0:T(8,128)S(1)}, u32[]{:S(2)}) copy-start(f32[1,32,256]{2,1,0:T(8,128)S(1)} %copy.477) | copy-start | bytes 98308
  149.4 38.3 %copy-start.27 = (f32[1,32,256]{2,1,0:T(8,128)}, f32[1,32,256]{2,1,0:T(8,128)S(1)}, u32[]{:S(2)}) copy-start(f32[1,32,256]{2,1,0:T(8,128)S(1)} %copy.478) | copy-start | bytes 98308
  149.4 38.3 %copy-start.29 = (f32[1,32,256]{2,1,0:T(8,128)}, f32[1,32,256]{2,1,0:T(8,128)S(1)}, u32[]{:S(2)}) copy-start(f32[1,32,256]{2,1,0:T(8,128)S(1)} %copy.479) | copy-start | bytes 98308
  149.4 38.3 %copy-start.31 = (f32[1,32,256]{2,1,0:T(8,128)}, f32[1,32,256]{2,1,0:T(8,128)S(1)}, u32[]{:S(2)}) copy-start(f32[1,32,256]{2,1,0:T(8,128)S(1)} %copy.480) | copy-start | bytes 98308
  149.4 38.3 %copy-start.33 = (f32[1,32,256]{2,1,0:T(8,128)}, f32[1,32,256]{2,1,0:T(8,128)S(1)}, u32[]{:S(2)}) copy-start(f32[1,32,256]{2,1,0:T(8,128)S(1)} %copy.481) | copy-start | bytes 98308
  158.9 28.7 %copy-start.44 = (f32[32,256]{1,0:T(8,128)}, f32[32,256]{1,0:T(8,128)S(1)}, u32[]{:S(2)}) copy-start(f32[32,256]{1,0:T(8,128)S(1)} %get-tuple-element.30) | copy-start | bytes 98308
  204.9 4.4 collective-permute-start
  207.2 5.4 collective-permute-start.1
  215.7 4.4 collective-permute-start.2
  217.9 5.9 collective-permute-start.3
  305.0 79.8 %copy-start.48 = (s32[1,64,128]{2,1,0:T(8,128)S(1)}, s32[1,64,128]{2,1,0:T(8,128)}, u32[]{:S(2)}) copy-start(s32[1,64,128]{2,1,0:T(8,128)} %param.20) | copy-start | bytes 98308
  366.2 29.3 %all-to-all-start.1 = ((f32[9,64,128]{2,0,1:T(8,128)}), f32[9,64,128]{2,0,1:T(8,128)S(1)}, u32[]{:S(2)}, u32[]{:S(2)}) async-start(f32[9,64,128]{2,0,1:T(8,128)} %copy.439), calls=%async_computation.1 | async-start | bytes 1048576 | tf_op jit(solution)/shard_map/all_to_all | solution.py:309
  384.7 299.4 %all-reduce.35.cloned.1.call-start = ((), (), s32[]{:S(2)}) async-start(), calls=%async_computation.2 | async-start | bytes 8388608 | tf_op jit(solution)/shard_map/psum | solution.py:318
  533.3 18.7 %copy-start.11 = (f32[1,16384]{1,0:T(1,128)}, f32[1,16384]{1,0:T(1,128)S(1)}, u32[]{:S(2)}) copy-start(f32[1,16384]{1,0:T(1,128)S(1)} %get-tuple-element.41) | copy-start | bytes 196612
  533.3 18.7 %copy-start.12 = (f32[1,16384]{1,0:T(1,128)}, f32[1,16384]{1,0:T(1,128)S(1)}, u32[]{:S(2)}) copy-start(f32[1,16384]{1,0:T(1,128)S(1)} %get-tuple-element.42) | copy-start | bytes 196612
  533.3 18.7 %copy-start.13 = (f32[1,16384]{1,0:T(1,128)}, f32[1,16384]{1,0:T(1,128)S(1)}, u32[]{:S(2)}) copy-start(f32[1,16384]{1,0:T(1,128)S(1)} %get-tuple-element.43) | copy-start | bytes 196612
  533.3 18.7 %copy-start.14 = (f32[1,16384]{1,0:T(1,128)}, f32[1,16384]{1,0:T(1,128)S(1)}, u32[]{:S(2)}) copy-start(f32[1,16384]{1,0:T(1,128)S(1)} %get-tuple-element.44) | copy-start | bytes 196612
  533.3 18.7 %copy-start.15 = (f32[1,16384]{1,0:T(1,128)}, f32[1,16384]{1,0:T(1,128)S(1)}, u32[]{:S(2)}) copy-start(f32[1,16384]{1,0:T(1,128)S(1)} %get-tuple-element.46) | copy-start | bytes 196612
  533.3 18.7 %copy-start.16 = (f32[1,16384]{1,0:T(1,128)}, f32[1,16384]{1,0:T(1,128)S(1)}, u32[]{:S(2)}) copy-start(f32[1,16384]{1,0:T(1,128)S(1)} %get-tuple-element.47) | copy-start | bytes 196612
  533.3 18.7 %copy-start.17 = (f32[1,16384]{1,0:T(1,128)}, f32[1,16384]{1,0:T(1,128)S(1)}, u32[]{:S(2)}) copy-start(f32[1,16384]{1,0:T(1,128)S(1)} %get-tuple-element.49) | copy-start | bytes 196612
  533.3 18.7 %copy-start.18 = (f32[1,16384]{1,0:T(1,128)}, f32[1,16384]{1,0:T(1,128)S(1)}, u32[]{:S(2)}) copy-start(f32[1,16384]{1,0:T(1,128)S(1)} %get-tuple-element.50) | copy-start | bytes 196612
  (29 other events, 267.9 us)
Sparse Core Ops, SparseCore 0:
  615.6 35.6 all-reduce.34
where the time goes:
time: 714 us; the launch traced here: 704 us
  other arithmetic  261 us (37%)
  local copies, waits for them, and re-layouts  217 us (30%)
  matrix products  71.4 us (10%)
  blocking collectives  68 us (10%)
  starting transfers between devices  38.4 us (5%)
  waiting for transfers between devices  29.2 us (4%)
  between operations  18.7 us (3%)
    psum x1, blocking collectives, shards(): lax.psum(loss_part, ('view', 'tile'))  68 us
    another operation x3, local copies, waits for them, and re-layouts, project(): jnp.stack([screen_u, screen_v, cov_yy / determinant, -cov_xy / determinan...  65.6 us
    scatter-add x1, other arithmetic, shards(): screen_grad = jnp.zeros((9, params.shape[1]), jnp.float32).at[:, slots_ou...  55.3 us
    scatter-add x1, other arithmetic, shards(): slot_grad = jnp.zeros((9, band_total * capacity), jnp.float32).at[:, tile...  54.6 us
    unnamed x126, local copies, waits for them, and re-layouts  39.8 us
    dot_general x2, matrix products, blocked_prefix(): jnp.einsum('jk,tbkp->tbjp', lower, grouped, precision=lax.Precision.HIGHEST)  37.5 us
    gather x2, local copies, waits for them, and re-layouts, shards(): outgoing = jnp.where(was_dispatched[None], records[:, slots_out], 0.0)  34.2 us
    dot_general x3, matrix products, render_band(): jnp.einsum('qvr,fqv->fqr', blend_weights, entry_records[6:9], precision=l...  33.9 us
  transfers between devices with their start and end apart: 7, of which 4 were waited for; matrix products, arithmetic and copies ran while one was open for 0% of the time, Pallas kernels for 0%

commit v1 on v0

v1 whole, which is shorter than its diff:
```python
import functools
import math

import jax
import jax.numpy as jnp
from jax import lax
from jax.experimental import pallas as pl
from jax.experimental.pallas import tpu as pltpu
from jax.sharding import PartitionSpec as P

STEP_COUNT = 20
LIST = 256


def extended(block, sides, width):
    for axis, dim in sides:
        count = lax.axis_size(axis)
        forward = [(i, i + 1) for i in range(count - 1)]
        backward = [(target, source) for source, target in forward]
        low = lax.ppermute(
            lax.slice_in_dim(block, block.shape[dim] - width, None, axis=dim), axis, forward
        )
        high = lax.ppermute(lax.slice_in_dim(block, 0, width, axis=dim), axis, backward)
        block = jnp.concatenate([low, block, high], axis=dim)
    return block


def window_taps():
    raw_taps = [math.exp(-(position - 5) * (position - 5) / 4.5) for position in range(11)]
    return [element / sum(raw_taps) for element in raw_taps]


def harmonics(unit_x, unit_y, unit_z):
    square_x = unit_x * unit_x
    square_y = unit_y * unit_y
    square_z = unit_z * unit_z
    return [
        0.28209479177387814 * jnp.ones_like(unit_x),
        -0.4886025119029199 * unit_y,
        0.4886025119029199 * unit_z,
        -0.4886025119029199 * unit_x,
        1.0925484305920792 * unit_x * unit_y,
        -1.0925484305920792 * unit_y * unit_z,
        0.31539156525252005 * (2.0 * square_z - square_x - square_y),
        -1.0925484305920792 * unit_x * unit_z,
        0.5462742152960396 * (square_x - square_y),
        -0.5900435899266435 * unit_y * (3.0 * square_x - square_y),
        2.890611442640554 * unit_x * unit_y * unit_z,
        -0.4570457994644658 * unit_y * (4.0 * square_z - square_x - square_y),
        0.3731763325901154 * unit_z * (2.0 * square_z - 3.0 * square_x - 3.0 * square_y),
        -0.4570457994644658 * unit_x * (4.0 * square_z - square_x - square_y),
        1.445305721320277 * unit_z * (square_x - square_y),
        -0.5900435899266435 * unit_x * (square_x - 3.0 * square_y),
    ]


MESH = pl.DeviceIdType.MESH
VMEM_LIMIT = 56 * 1024 * 1024
NN = (((1,), (0,)), ((), ()))
NT = (((1,), (1,)), ((), ()))
TN = (((0,), (0,)), ((), ()))


def mxu(left, right, dims):
    return lax.dot_general(left, right, dims, preferred_element_type=jnp.float32)


def split2(value):
    high = value.astype(jnp.bfloat16)
    low = (value - high.astype(jnp.float32)).astype(jnp.bfloat16)
    return high, low


def split3(value):
    high = value.astype(jnp.bfloat16)
    rest = value - high.astype(jnp.float32)
    middle = rest.astype(jnp.bfloat16)
    low = (rest - middle.astype(jnp.float32)).astype(jnp.bfloat16)
    return high, middle, low


def project_rows(rows, cameras):
    pos_x, pos_y, pos_z = rows[0:3]
    scales = [jnp.exp(row) for row in rows[3:6]]
    quat_w, quat_x, quat_y, quat_z = rows[6:10]
    norm = 1.0 / jnp.sqrt(
        quat_w * quat_w + quat_x * quat_x + quat_y * quat_y + quat_z * quat_z
    )
    quat_w, quat_x, quat_y, quat_z = quat_w * norm, quat_x * norm, quat_y * norm, quat_z * norm
    rotation = [
        [
            1.0 - 2.0 * (quat_y * quat_y + quat_z * quat_z),
            2.0 * (quat_x * quat_y - quat_w * quat_z),
            2.0 * (quat_x * quat_z + quat_w * quat_y),
        ],
        [
            2.0 * (quat_x * quat_y + quat_w * quat_z),
            1.0 - 2.0 * (quat_x * quat_x + quat_z * quat_z),
            2.0 * (quat_y * quat_z - quat_w * quat_x),
        ],
        [
            2.0 * (quat_x * quat_z - quat_w * quat_y),
            2.0 * (quat_y * quat_z + quat_w * quat_x),
            1.0 - 2.0 * (quat_x * quat_x + quat_y * quat_y),
        ],
    ]
    opacity = 1.0 / (1.0 + jnp.exp(-rows[10]))
    records = []
    for shear_x, shear_y, offset_x, offset_y, center_x, center_y, center_z in cameras:
        first = [(rotation[0][k] + shear_x * rotation[2][k]) * scales[k] for k in range(3)]
        second = [(rotation[1][k] + shear_y * rotation[2][k]) * scales[k] for k in range(3)]
        cov_xx = first[0] * first[0] + first[1] * first[1] + first[2] * first[2] + 0.3
        cov_yy = second[0] * second[0] + second[1] * second[1] + second[2] * second[2] + 0.3
        cov_xy = first[0] * second[0] + first[1] * second[1] + first[2] * second[2]
        inverse = 1.0 / (cov_xx * cov_yy - cov_xy * cov_xy)
        toward_x = pos_x - center_x
        toward_y = pos_y - center_y
        toward_z = pos_z - center_z
        shrink = 1.0 / jnp.sqrt(toward_x * toward_x + toward_y * toward_y + toward_z * toward_z)
        basis = harmonics(toward_x * shrink, toward_y * shrink, toward_z * shrink)
        colors = []
        for c in range(3):
            total = basis[0] * rows[11 + c]
            for k in range(1, 16):
                total = total + basis[k] * rows[11 + 3 * k + c]
            colors.append(0.5 + total)
        records.append(
            [
                pos_x + shear_x * pos_z + offset_x,
                pos_y + shear_y * pos_z + offset_y,
                cov_yy * inverse,
                -cov_xy * inverse,
                cov_xx * inverse,
                opacity,
                *colors,
            ]
        )
    return records


def camera_of(refs, view):
    shear_ref, offset_ref, center_ref = refs
    return (
        shear_ref[view, 0],
        shear_ref[view, 1],
        offset_ref[view, 0],
        offset_ref[view, 1],
        center_ref[view, 0],
        center_ref[view, 1],
        center_ref[view, 2],
    )


def spread_rows(source_ref, dense_ref):
    count = source_ref.shape[0]
    for c in range(8):
        lanes = pl.ds(128 * c, 128)
        for first in range(0, count, 8):
            size = min(8, count - first)
            dense_ref[pl.ds(8 * first + c, size, stride=8), :] = source_ref[first : first + size, lanes]


def project_kernel(params_ref, index_ref, shear_ref, offset_ref, center_ref, out_ref, dense, table, parts):
    step = pl.program_id(0)
    spread_rows(params_ref, dense)
    rows = [dense[8 * r : 8 * r + 8, :] for r in range(59)]
    record = project_rows(rows, [camera_of((shear_ref, offset_ref, center_ref), 0)])[0]
    for q in range(9):
        table[q, pl.ds(pl.multiple_of(8 * step, 8), 8), :] = record[q]

    @pl.when(step == pl.num_programs(0) - 1)
    def _():
        for q in range(9):
            for half in range(2):
                for k, part in enumerate(split3(table[q, 64 * half : 64 * half + 64, :])):
                    parts[64 * q : 64 * q + 64, 256 * k + 128 * half : 256 * k + 128 * half + 128] = part
        low_ids = lax.broadcasted_iota(jnp.int32, (256, 256), 0)
        high_ids = lax.broadcasted_iota(jnp.int32, (64, 256), 0)

        def pick(pair, carry):
            index = jnp.concatenate(
                [index_ref[pl.ds(pair, 1), :], index_ref[pl.ds(pair + 32, 1), :]], axis=1
            )
            high = (index >> 7) & 63
            low = (index & 127) + ((index >> 13) << 7)
            hot = (low_ids == low).astype(jnp.float32).astype(jnp.bfloat16)
            found = mxu(parts[...], jnp.concatenate([hot, hot, hot], axis=0), NN)
            mask = high_ids == high
            for q in range(9):
                row = jnp.sum(jnp.where(mask, found[64 * q : 64 * q + 64], 0.0), axis=0, keepdims=True)
                out_ref[pair, q : q + 1, :] = row[:, 0:128]
                out_ref[pair + 32, q : q + 1, :] = row[:, 128:256]
            return carry

        lax.fori_loop(0, 32, pick, 0, unroll=2)


def project_and_pick(params, send_index, shear, offset, center):
    smem = pl.BlockSpec(memory_space=pltpu.SMEM)
    return pl.pallas_call(
        project_kernel,
        grid=(16,),
        out_shape=jax.ShapeDtypeStruct((64, 9, 128), jnp.float32),
        in_specs=[
            pl.BlockSpec((59, 1024), lambda i: (0, i)),
            pl.BlockSpec((64, 128), lambda i: (0, 0)),
            smem,
            smem,
            smem,
        ],
        out_specs=pl.BlockSpec((64, 9, 128), lambda i: (0, 0, 0)),
        scratch_shapes=[
            pltpu.VMEM((59 * 8, 128), jnp.float32),
            pltpu.VMEM((9, 128, 128), jnp.float32),
            pltpu.VMEM((576, 768), jnp.bfloat16),
        ],
        compiler_params=pltpu.CompilerParams(vmem_limit_bytes=VMEM_LIMIT),
        name="project_and_pick",
    )(params, send_index, shear, offset, center)


def exchange_kernel(in_ref, out_ref, send_sem, recv_sem, local_sem):
    total = lax.axis_size("tile")
    me = lax.axis_index("tile")
    barrier = pltpu.get_barrier_semaphore()

    def greet(p, carry):
        pl.semaphore_signal(
            barrier, inc=1, device_id={"tile": lax.rem(me + p, total)}, device_id_type=MESH
        )
        return carry

    lax.fori_loop(1, total, greet, 0)
    own = pltpu.make_async_copy(in_ref.at[me], out_ref.at[me], local_sem)
    own.start()
    pl.semaphore_wait(barrier, total - 1)

    def copy_to(p):
        peer = lax.rem(me + p, total)
        return pltpu.make_async_remote_copy(
            src_ref=in_ref.at[peer],
            dst_ref=out_ref.at[me],
            send_sem=send_sem.at[p],
            recv_sem=recv_sem.at[p],
            device_id={"tile": peer},
            device_id_type=MESH,
        )

    def send(p, carry):
        copy_to(p).start()
        return carry

    def finish(p, carry):
        copy_to(p).wait()
        return carry

    lax.fori_loop(1, total, send, 0)
    own.wait()
    lax.fori_loop(1, total, finish, 0)


def exchange(blocks, collective_id):
    vmem = pl.BlockSpec(memory_space=pltpu.VMEM)
    total = blocks.shape[0]
    return pl.pallas_call(
        exchange_kernel,
        out_shape=jax.ShapeDtypeStruct(blocks.shape, blocks.dtype),
        in_specs=[vmem],
        out_specs=vmem,
        scratch_shapes=[
            pltpu.SemaphoreType.DMA((total,)),
            pltpu.SemaphoreType.DMA((total,)),
            pltpu.SemaphoreType.DMA,
        ],
        compiler_params=pltpu.CompilerParams(
            collective_id=collective_id, has_side_effects=True, vmem_limit_bytes=VMEM_LIMIT
        ),
        name="exchange",
    )(blocks)


TILES_STEP = 4


def slot_place(index):
    return (index >> 7) & 31, (index & 127) + ((index >> 12) << 7)


def tile_deltas(tile, band, u_row, w_row):
    offsets = lax.broadcasted_iota(jnp.int32, (16, 256), 0)
    pixel_x = (offsets + 16 * tile).astype(jnp.float32) + 0.5
    pixel_y = (offsets + 16 * band).astype(jnp.float32) + 0.5
    return pixel_x - u_row, pixel_y - w_row


def forward_kernel(
    slots_ref, list_ref, count_ref, band_ref, back_ref, image_ref, entry_ref, cover_ref, keep_ref, parts, before
):
    step = pl.program_id(0)

    @pl.when(step == 0)
    def _():
        for q in range(9):
            for half in range(2):
                for k, part in enumerate(split3(slots_ref[32 * half : 32 * half + 32, q, :])):
                    parts[32 * q : 32 * q + 32, 256 * k + 128 * half : 256 * k + 128 * half + 128] = part
        row_ids = lax.broadcasted_iota(jnp.int32, (256, 256), 0)
        column_ids = lax.broadcasted_iota(jnp.int32, (256, 256), 1)
        before[...] = (row_ids < column_ids).astype(jnp.float32).astype(jnp.bfloat16)

    band = band_ref[0]
    low_ids = lax.broadcasted_iota(jnp.int32, (256, 256), 0)
    high_ids = lax.broadcasted_iota(jnp.int32, (32, 256), 0)
    lanes = lax.broadcasted_iota(jnp.int32, (1, 256), 1)

    def one(k, carry):
        tile = step * TILES_STEP + k
        high, low = slot_place(list_ref[pl.ds(tile, 1), :])
        hot = (low_ids == low).astype(jnp.float32).astype(jnp.bfloat16)
        found = mxu(parts[...], jnp.concatenate([hot, hot, hot], axis=0), NN)
        mask = high_ids == high
        rows = [
            jnp.sum(jnp.where(mask, found[32 * q : 32 * q + 32], 0.0), axis=0, keepdims=True)
            for q in range(9)
        ]
        rows[5] = jnp.where(lanes < count_ref[0, tile], rows[5], 0.0)
        for c in range(3):
            rows[6 + c] = rows[6 + c] - back_ref[c]
        for q in range(9):
            entry_ref[k, q : q + 1, :] = rows[q]
        delta_x, delta_y = tile_deltas(tile, band, rows[0], rows[1])
        along_x = -0.5 * rows[2] * delta_x * delta_x
        mixed = -rows[3] * delta_x
        along_y = -0.5 * rows[4] * delta_y * delta_y
        pieces = []
        for i in range(16):
            exponent = along_x + (mixed * delta_y[i : i + 1] + along_y[i : i + 1])
            pieces.append(rows[5] * jnp.exp(exponent))
        cover = jnp.concatenate(pieces, axis=0)
        kept_high, kept_low = split2(jnp.log(1.0 - cover))
        keep = jnp.exp(mxu(kept_high, before[...], NN) + mxu(kept_low, before[...], NN))
        cover_ref[k] = cover
        keep_ref[k] = keep
        weight_high, weight_low = split2(cover * keep)
        colors = jnp.concatenate(rows[6:9] + [jnp.zeros((5, 256), jnp.float32)], axis=0)
        color_high, color_low = split2(colors)
        shown = (
            mxu(color_high, weight_high, NT)
            + mxu(color_low, weight_high, NT)
            + mxu(color_high, weight_low, NT)
        )
        for c in range(3):
            image_ref[c, pl.ds(tile, 1), :] = shown[c : c + 1] + back_ref[c]
        return carry

    lax.fori_loop(0, TILES_STEP, one, 0)


def render_forward(slots, lists, counts, band, back):
    smem = pl.BlockSpec(memory_space=pltpu.SMEM)
    field = jax.ShapeDtypeStruct((32, 256, 256), jnp.float32)
    field_spec = pl.BlockSpec((TILES_STEP, 256, 256), lambda i: (i, 0, 0))
    return pl.pallas_call(
        forward_kernel,
        grid=(32 // TILES_STEP,),
        out_shape=(
            jax.ShapeDtypeStruct((3, 32, 256), jnp.float32),
            jax.ShapeDtypeStruct((32, 9, 256), jnp.float32),
            field,
            field,
        ),
        in_specs=[
            pl.BlockSpec((64, 9, 128), lambda i: (0, 0, 0)),
            pl.BlockSpec((32, 256), lambda i: (0, 0)),
            smem,
            smem,
            smem,
        ],
        out_specs=(
            pl.BlockSpec((3, 32, 256), lambda i: (0, 0, 0)),
            pl.BlockSpec((TILES_STEP, 9, 256), lambda i: (i, 0, 0)),
            field_spec,
            field_spec,
        ),
        scratch_shapes=[
            pltpu.VMEM((288, 768), jnp.bfloat16),
            pltpu.VMEM((256, 256), jnp.bfloat16),
        ],
        compiler_params=pltpu.CompilerParams(vmem_limit_bytes=VMEM_LIMIT),
        name="render_forward",
    )(slots, lists, counts, band, back)


def backward_kernel(
    entry_ref, cover_ref, keep_ref, grad_ref, list_ref, band_ref, out_ref, after, total
):
    step = pl.program_id(0)

    @pl.when(step == 0)
    def _():
        row_ids = lax.broadcasted_iota(jnp.int32, (256, 256), 0)
        column_ids = lax.broadcasted_iota(jnp.int32, (256, 256), 1)
        after[...] = (row_ids > column_ids).astype(jnp.float32).astype(jnp.bfloat16)
        total[...] = jnp.zeros_like(total)

    band = band_ref[0]
    low_ids = lax.broadcasted_iota(jnp.int32, (256, 256), 0)
    high_ids = lax.broadcasted_iota(jnp.int32, (32, 256), 0)

    def one(k, carry):
        tile = step * TILES_STEP + k
        rows = [entry_ref[k, q : q + 1, :] for q in range(9)]
        grads = jnp.concatenate([grad_ref[c, pl.ds(tile, 1), :] for c in range(3)], axis=0)
        colors = jnp.concatenate(rows[6:9], axis=0)
        grads_high = grads.astype(jnp.bfloat16).astype(jnp.float32)
        grads_low = grads - grads_high
        colors_high = colors.astype(jnp.bfloat16).astype(jnp.float32)
        colors_low = colors - colors_high
        blank = jnp.zeros((7, 256), jnp.float32)
        left = jnp.concatenate([grads_high, grads_high, grads_low, blank], axis=0).astype(jnp.bfloat16)
        right = jnp.concatenate([colors_high, colors_low, colors_high, blank], axis=0).astype(jnp.bfloat16)
        shade = mxu(left, right, TN)
        cover = cover_ref[k]
        weight = cover * keep_ref[k]
        weight_high, weight_low = split2(weight)
        both = jnp.concatenate([grads_high, grads_low, blank, blank[0:3]], axis=0).astype(jnp.bfloat16)
        color_grad = mxu(both, weight_high, NN)
        color_grad = color_grad[0:3] + color_grad[3:6] + mxu(both, weight_low, NN)[0:3]
        lit = weight * shade
        lit_high, lit_low = split2(lit)
        behind = mxu(lit_high, after[...], NN) + mxu(lit_low, after[...], NN)
        pull = lit - behind * (cover / (1.0 - cover))
        delta_x, delta_y = tile_deltas(tile, band, rows[0], rows[1])
        sum_0 = pull[0:16]
        sum_y = sum_0 * delta_y[0:1]
        sum_yy = sum_y * delta_y[0:1]
        for i in range(1, 16):
            piece = pull[16 * i : 16 * i + 16]
            piece_y = piece * delta_y[i : i + 1]
            sum_0 = sum_0 + piece
            sum_y = sum_y + piece_y
            sum_yy = sum_yy + piece_y * delta_y[i : i + 1]
        sum_x = sum_0 * delta_x

        def fold(value):
            return jnp.sum(value, axis=0, keepdims=True)

        moment_0 = fold(sum_0)
        moment_x = fold(sum_x)
        moment_xx = fold(sum_x * delta_x)
        moment_y = fold(sum_y)
        moment_xy = fold(sum_y * delta_x)
        moment_yy = fold(sum_yy)
        live = rows[5] > 0.0
        results = [
            rows[2] * moment_x + rows[3] * moment_y,
            rows[4] * moment_y + rows[3] * moment_x,
            -0.5 * moment_xx,
            -moment_xy,
            -0.5 * moment_yy,
            jnp.where(live, moment_0 / jnp.where(live, rows[5], 1.0), 0.0),
            color_grad[0:1],
            color_grad[1:2],
            color_grad[2:3],
        ]
        high, low = slot_place(list_ref[pl.ds(tile, 1), :])
        hot = (low_ids == low).astype(jnp.float32).astype(jnp.bfloat16)
        mask = high_ids == high
        placed = jnp.concatenate([jnp.where(mask, row, 0.0) for row in results], axis=0)
        placed_high, placed_low = split2(placed)
        total[...] += mxu(placed_high, hot, NT) + mxu(placed_low, hot, NT)
        return carry

    lax.fori_loop(0, TILES_STEP, one, 0)

    @pl.when(step == pl.num_programs(0) - 1)
    def _():
        for q in range(9):
            for half in range(2):
                out_ref[32 * half : 32 * half + 32, q, :] = total[
                    32 * q : 32 * q + 32, 128 * half : 128 * half + 128
                ]


def render_backward(entries, cover, keep, grads, lists, band):
    smem = pl.BlockSpec(memory_space=pltpu.SMEM)
    field_spec = pl.BlockSpec((TILES_STEP, 256, 256), lambda i: (i, 0, 0))
    return pl.pallas_call(
        backward_kernel,
        grid=(32 // TILES_STEP,),
        out_shape=jax.ShapeDtypeStruct((64, 9, 128), jnp.float32),
        in_specs=[
            pl.BlockSpec((TILES_STEP, 9, 256), lambda i: (i, 0, 0)),
            field_spec,
            field_spec,
            pl.BlockSpec((3, 32, 256), lambda i: (0, 0, 0)),
            pl.BlockSpec((32, 256), lambda i: (0, 0)),
            smem,
        ],
        out_specs=pl.BlockSpec((64, 9, 128), lambda i: (0, 0, 0)),
        scratch_shapes=[
            pltpu.VMEM((256, 256), jnp.bfloat16),
            pltpu.VMEM((288, 256), jnp.float32),
        ],
        compiler_params=pltpu.CompilerParams(vmem_limit_bytes=VMEM_LIMIT),
        name="render_backward",
    )(entries, cover, keep, grads, lists, band)


def place_kernel(returned_ref, index_ref, count_ref, out_ref, total):
    total[...] = jnp.zeros_like(total)
    low_ids = lax.broadcasted_iota(jnp.int32, (256, 256), 0)
    high_ids = lax.broadcasted_iota(jnp.int32, (64, 256), 0)
    lanes = lax.broadcasted_iota(jnp.int32, (1, 128), 1)

    def place(pair, carry):
        def joined(values):
            return jnp.concatenate(values, axis=1)

        bands = (pair, pair + 32)
        index = joined([index_ref[pl.ds(d, 1), :] for d in bands])
        live = joined([(lanes < count_ref[0, d]).astype(jnp.int32) for d in bands])
        high = jnp.where(live > 0, (index >> 7) & 63, -1)
        low = (index & 127) + ((index >> 13) << 7)
        hot = (low_ids == low).astype(jnp.float32).astype(jnp.bfloat16)
        mask = high_ids == high
        placed = jnp.concatenate(
            [
                jnp.where(mask, joined([returned_ref[d, q : q + 1, :] for d in bands]), 0.0)
                for q in range(9)
            ],
            axis=0,
        )
        placed_high, placed_low = split2(placed)
        total[...] += mxu(placed_high, hot, NT) + mxu(placed_low, hot, NT)
        return carry

    lax.fori_loop(0, 32, place, 0, unroll=2)
    for q in range(9):
        for half in range(2):
            out_ref[q, 64 * half : 64 * half + 64, :] = total[
                64 * q : 64 * q + 64, 128 * half : 128 * half + 128
            ]


def place_gradients(returned, send_index, send_count):
    vmem = pl.BlockSpec(memory_space=pltpu.VMEM)
    return pl.pallas_call(
        place_kernel,
        out_shape=jax.ShapeDtypeStruct((9, 128, 128), jnp.float32),
        in_specs=[vmem, vmem, pl.BlockSpec(memory_space=pltpu.SMEM)],
        out_specs=vmem,
        scratch_shapes=[pltpu.VMEM((576, 256), jnp.float32)],
        compiler_params=pltpu.CompilerParams(vmem_limit_bytes=VMEM_LIMIT),
        name="place_gradients",
    )(returned, send_index, send_count)


RATES = [0.016] * 3 + [0.005] * 3 + [0.001] * 4 + [0.05] + [0.0025] * 3 + [0.000125] * 45


def update_kernel(
    params_ref, first_ref, second_ref, own_ref, other_ref, view_ref, shear_ref, offset_ref, center_ref,
    params_out, first_out, second_out, dense,
):
    spread_rows(params_ref, dense)
    rows = [dense[8 * r : 8 * r + 8, :] for r in range(59)]
    refs = (shear_ref, offset_ref, center_ref)
    cameras = [camera_of(refs, 0), camera_of(refs, 1)]
    _, pull_back = jax.vjp(lambda *values: project_rows(values, cameras), *rows)
    is_first = view_ref[0] == 0
    own = [own_ref[q] for q in range(9)]
    other = [other_ref[q] for q in range(9)]
    gradient = pull_back(
        [
            [jnp.where(is_first, a, b) for a, b in zip(own, other)],
            [jnp.where(is_first, b, a) for a, b in zip(own, other)],
        ]
    )
    for r in range(59):
        dense[8 * r : 8 * r + 8, :] = gradient[r]
    for first in range(0, 59, 8):
        size = min(8, 59 - first)
        row_ids = lax.broadcasted_iota(jnp.int32, (size, 128), 0)
        rate = jnp.full((size, 128), RATES[first], jnp.float32)
        for r in range(1, size):
            if RATES[first + r] != RATES[first + r - 1]:
                rate = jnp.where(row_ids >= r, RATES[first + r], rate)
        for c in range(8):
            here = (slice(first, first + size), pl.ds(128 * c, 128))
            grad = dense[pl.ds(8 * first + c, size, stride=8), :]
            new_first = 0.9 * first_ref[here] + 0.1 * grad
            new_second = 0.999 * second_ref[here] + 0.001 * grad * grad
            corrected = new_first / (1.0 - 0.9**STEP_COUNT)
            scale = jnp.sqrt(new_second / (1.0 - 0.999**STEP_COUNT)) + 1e-15
            params_out[here] = params_ref[here] - rate * corrected / scale
            first_out[here] = new_first
            second_out[here] = new_second


def update(params, first_moment, second_moment, own, other, view, shear, offset, center):
    smem = pl.BlockSpec(memory_space=pltpu.SMEM)
    block = pl.BlockSpec((59, 1024), lambda i: (0, i))
    grads = pl.BlockSpec((9, 8, 128), lambda i: (0, i, 0))
    shape = jax.ShapeDtypeStruct(params.shape, jnp.float32)
    return pl.pallas_call(
        update_kernel,
        grid=(16,),
        out_shape=(shape, shape, shape),
        in_specs=[block, block, block, grads, grads, smem, smem, smem, smem],
        out_specs=(block, block, block),
        scratch_shapes=[pltpu.VMEM((59 * 8, 128), jnp.float32)],
        compiler_params=pltpu.CompilerParams(vmem_limit_bytes=VMEM_LIMIT),
        name="update",
    )(params, first_moment, second_moment, own, other, view, shear, offset, center)


def gaussian_blur(planes):
    taps = window_taps()
    rows_out = planes.shape[1] - 10
    vertical = taps[0] * planes[:, 0:rows_out]
    for position in range(1, 11):
        vertical = vertical + taps[position] * planes[:, position : position + rows_out]
    image_width = planes.shape[2]
    padded = jnp.pad(vertical, ((0, 0), (0, 0), (5, 5)))
    result = taps[0] * padded[:, :, 0:image_width]
    for position in range(1, 11):
        result = result + taps[position] * padded[:, :, position : position + image_width]
    return result


def ssim_map(level_x, level_y, energy_x, energy_y, product_xy):
    upper = (2.0 * level_x * level_y + 0.0001) * (2.0 * (product_xy - level_x * level_y) + 0.0009)
    lower = (level_x * level_x + level_y * level_y + 0.0001) * (
        energy_x - level_x * level_x + (energy_y - level_y * level_y) + 0.0009
    )
    return upper / lower


def window_stats(widened):
    shown = widened[0:3]
    truth = widened[3:6]
    mean_x = gaussian_blur(shown)
    mean_y = gaussian_blur(truth)
    power_x = gaussian_blur(shown * shown)
    power_y = gaussian_blur(truth * truth)
    cross_xy = gaussian_blur(shown * truth)
    return (mean_x, mean_y, power_x, power_y, cross_xy)


def shards(
    params,
    first_moment,
    second_moment,
    target,
    view_shear,
    view_offset,
    cam_center,
    background,
    send_index,
    send_count,
    tile_list,
    tile_count,
):
    view_index = lax.axis_index("view")
    band_index = lax.axis_index("tile")
    band_total = lax.axis_size("tile")

    def own_first(values):
        return jnp.where(view_index == 0, values, values[::-1])

    shear, offset, center = own_first(view_shear), own_first(view_offset), own_first(cam_center)
    backdrop = own_first(background)[0]
    band = band_index.astype(jnp.int32).reshape(1)
    outgoing = project_and_pick(params, send_index[0], shear, offset, center)
    incoming = exchange(outgoing, 0)
    shown, entries, cover, keep = render_forward(
        incoming, tile_list[0, 0], tile_count, band, backdrop
    )
    image_band = shown.reshape(3, 32, 16, 16).transpose(0, 2, 1, 3).reshape(3, 16, 512)
    frame_band = target[0]
    image_width = frame_band.shape[2]
    stacked = jnp.concatenate([image_band, frame_band], axis=0)
    widened = extended(stacked, (("tile", 1),), 5)
    mean_x, mean_y, power_x, power_y, cross_xy = window_stats(widened)
    similarity, ssim_back = jax.vjp(
        lambda level_x, energy_x, product_xy: ssim_map(
            level_x, mean_y, energy_x, power_y, product_xy
        ),
        mean_x,
        power_x,
        cross_xy,
    )
    grad_mean, grad_power, grad_cross = ssim_back(jnp.full_like(similarity, -0.8))
    spread = extended(
        jnp.concatenate([grad_mean, grad_power, grad_cross], axis=0), (("tile", 1),), 5
    )
    blurred = gaussian_blur(spread)
    difference = image_band - frame_band
    smooth = jnp.sqrt(difference * difference + 0.0001)
    loss_part = jnp.sum(0.2 * smooth + 0.8 * (1.0 - similarity))
    pixel_grad = (
        0.2 * difference / smooth
        + blurred[0:3]
        + 2.0 * image_band * blurred[3:6]
        + frame_band * blurred[6:9]
    )
    mean_loss = lax.psum(loss_part, ("view", "tile")) / (
        lax.axis_size("view") * 3 * 16 * band_total * image_width
    )
    grad_tiles = pixel_grad.reshape(3, 16, 32, 16).transpose(0, 2, 1, 3).reshape(3, 32, 256)
    slot_grad = render_backward(entries, cover, keep, grad_tiles, tile_list[0, 0], band)
    returned = exchange(slot_grad, 1)
    own_grad = place_gradients(returned, send_index[0], send_count)
    other_grad = lax.ppermute(own_grad, "view", [(0, 1), (1, 0)])
    new_params, new_first, new_second = update(
        params, first_moment, second_moment, own_grad, other_grad,
        view_index.astype(jnp.int32).reshape(1), view_shear, view_offset, cam_center,
    )
    return (new_params, new_first, new_second, mean_loss)


def solution(mesh):
    placed = (
        P(None, "tile"),
        P(None, "tile"),
        P(None, "tile"),
        P("view", None, "tile", None),
        P(),
        P(),
        P(),
        P(),
        P("tile", None, None),
        P("tile", None),
        P("view", "tile", None, None),
        P("tile", None),
    )
    return jax.shard_map(
        shards,
        mesh=mesh,
        in_specs=placed,
        out_specs=(P(None, "tile"), P(None, "tile"), P(None, "tile"), P()),
        check_vma=False,
    )
```

time: 714 us -> 250 us (0.35); the launches traced: 704 us -> 249 us
  other arithmetic: 261 us -> 5.48 us
  local copies, waits for them, and re-layouts: 217 us -> 7.18 us
  Pallas kernels: 0 us -> 145 us
  matrix products: 71.4 us -> 0 us
  starting transfers between devices: 38.4 us -> 15.4 us
  waiting for transfers between devices: 29.2 us -> 8.65 us
  between operations: 18.7 us -> 2.62 us
    pallas_call x0 -> x7, Pallas kernels: none -> 145 us  [the longest x2 38.8 us: exchange(): pl.pallas_call(exchange_kernel, out_shape=jax.ShapeDtypeStruct(blocks.sha...]
    scatter-add x2 -> x0, other arithmetic: 110 us -> none  [the longest x1 55.3 us: shards(): screen_grad = jnp.zeros((9, params.shape[1]), jnp.float32).at[:, slots_ou...]
    dot_general x5 -> x0, matrix products: 71.4 us -> none  [the longest x2 37.5 us: blocked_prefix(): jnp.einsum('jk,tbkp->tbjp', lower, grouped, precision=lax.Precision.HIGHEST)]
    another operation x5 -> x0, local copies, waits for them, and re-layouts: 68.9 us -> none  [the longest x3 65.6 us: project(): jnp.stack([screen_u, screen_v, cov_yy / determinant, -cov_xy / determinan...]
    gather x4 -> x0, local copies, waits for them, and re-layouts: 67.2 us -> none  [the longest x2 34.2 us: shards(): outgoing = jnp.where(was_dispatched[None], records[:, slots_out], 0.0)]
    add_any x13 -> x0, other arithmetic: 44.8 us -> none  [the longest x1 13.3 us: project(): splat_colors[0]]
    unnamed x126 -> x4, local copies, waits for them, and re-layouts: 39.8 us -> 0.81 us
    mul x13 -> x0, other arithmetic: 35.4 us -> none  [the longest x1 8.94 us: render_band(): blend_weights = coverage * jnp.exp(running_prefix)]
  transfers between devices with their start and end apart: 7 -> 5, of which waited for: 4 -> 4; matrix products, arithmetic and copies ran while one was open for 0% -> 0% of each run, Pallas kernels for 0% -> 0%
where the time goes in v1:
time: 250 us; the launch traced here: 249 us
  Pallas kernels  145 us (58%)
  blocking collectives  64.6 us (26%)
  starting transfers between devices  15.4 us (6%)
  waiting for transfers between devices  8.65 us (3%)
  local copies, waits for them, and re-layouts  7.18 us (3%)
  other arithmetic  5.48 us (2%)
  between operations  2.62 us (1%)
    psum x1, blocking collectives, shards(): lax.psum(loss_part, ('view', 'tile'))  64.6 us
    pallas_call x2, Pallas kernels, exchange(): pl.pallas_call(exchange_kernel, out_shape=jax.ShapeDtypeStruct(blocks.sha...  38.8 us
    pallas_call x1, Pallas kernels, render_forward(): pl.pallas_call(forward_kernel, grid=(32 // TILES_STEP,), out_shape=(jax.S...  32 us
    pallas_call x1, Pallas kernels, render_backward(): pl.pallas_call(backward_kernel, grid=(32 // TILES_STEP,), out_shape=jax.S...  26.1 us
    pallas_call x1, Pallas kernels, project_and_pick(): pl.pallas_call(project_kernel, grid=(16,), out_shape=jax.ShapeDtypeStruct...  20.2 us
    pallas_call x1, Pallas kernels, update(): pl.pallas_call(update_kernel, grid=(16,), out_shape=(shape, shape, shape)...  16.5 us
    pallas_call x1, Pallas kernels, place_gradients(): pl.pallas_call(place_kernel, out_shape=jax.ShapeDtypeStruct((9, 128, 128)...  11.1 us
    ppermute x2, waiting for transfers between devices, extended(): lax.ppermute(lax.slice_in_dim(block, 0, width, axis=dim), axis, backward)  7.55 us
  transfers between devices with their start and end apart: 5, of which 4 were waited for; matrix products, arithmetic and copies ran while one was open for 0% of the time, Pallas kernels for 0%

profile of v1, /device:TPU:1, one launch (start us, length us, event | category | flops | bytes accessed | tf_op | source)
XLA Modules:
  0.0 248.7 jit_solution(6775131982950261185)
XLA Ops:
  0.6 0.7 rev.15
  1.3 0.7 rev.12
  2.0 0.7 rev.13
  2.7 0.7 rev.14
  3.4 0.5 broadcast_select_fusion
  4.0 0.5 slice_bitcast_fusion.back_ref
  4.5 0.6 broadcast_select_fusion.2
  5.0 20.2 %project_and_pick.1.in_ref = f32[64,9,128]{2,1,0:T(8,128)} custom-call(f32[59,16384]{1,0:T(8,128)} %params_ref.3, s32[64,128]{1,0:T(8,128)} %bitcast.25, f32[2,2]{1,0:T(2,128)} %get-tuple-element.40.shear_ref, f32[2,2]{1,0:T(2,128)} %get-tuple-element.39.offset_ref, f32[2,3]{1,0:T(2,128)} %get-tuple-element.38.center_ref), custom_call_target="tpu_custom_call" | custom-call | tf_op jit(solution)/shard_map/project_and_pick/pallas_call | solution.py:200
  25.2 17.8 %exchange.2.slots_ref = f32[64,9,128]{2,1,0:T(8,128)} custom-call(f32[64,9,128]{2,1,0:T(8,128)} %project_and_pick.1.in_ref), custom_call_target="tpu_custom_call" | custom-call | tf_op jit(solution)/shard_map/exchange/pallas_call | solution.py:265
  43.0 32.0 %render_forward.1 = (f32[3,32,256]{2,1,0:T(8,128)}, f32[32,9,256]{2,1,0:T(8,128)}, f32[32,256,256]{2,1,0:T(8,128)}, f32[32,256,256]{2,1,0:T(8,128)}) custom-call(f32[64,9,128]{2,1,0:T(8,128)} %exchange.2.slots_ref, s32[32,256]{1,0:T(8,128)} %bitcast.23, s32[1,32]{1,0:T(1,128)} %count_ref.2, s32[1]{0:T(128)} %bitcast.2.band_ref, f32[3]{0:T(128)} %slice_bitcast_fusion.back_ref), custom_call_target="tpu_custom_call" | custom-call | tf_op jit(solution)/shard_map/render_forward/pallas_call | solution.py:363
  75.1 1.1 copy.18
  76.1 0.3 copy.19
  76.4 0.4 reshape.28
  76.8 2.5 collective-permute-start
  79.3 1.3 collective-permute-start.1
  80.6 0.3 collective-permute-done
  81.0 3.7 %collective-permute-done.1 = f32[6,5,512]{2,1,0:T(8,128)S(1)} collective-permute-done((f32[6,5,512]{2,1,0:T(8,128)S(1)}, f32[6,5,512]{2,1,0:T(8,128)S(1)}, u32[]{:S(2)}, u32[]{:S(2)}) %collective-permute-start.1) | collective-permute-done | bytes 61472 | tf_op jit(solution)/shard_map/ppermute | solution.py:23
  85.6 2.0 add_reduce_fusion
  87.8 3.4 %collective-permute-start.2 = (f32[9,5,512]{2,1,0:T(8,128)S(1)}, f32[9,5,512]{2,1,0:T(8,128)S(1)}, u32[]{:S(2)}, u32[]{:S(2)}) collective-permute-start(f32[9,5,512]{2,1,0:T(8,128)S(1)} %get-tuple-element.30), channel_id=1, source_target_pairs={{0,1},{1,2},{2,3},{3,4},{4,5},{5,6},{6,7},{7,8},{8,9},{9,10},{10,1... | collective-permute-start | bytes 276488 | tf_op jit(solution)/shard_map/ppermute | solution.py:20
  91.1 1.3 collective-permute-start.3
  92.4 0.8 collective-permute-done.2
  93.2 3.8 %collective-permute-done.3 = f32[9,5,512]{2,1,0:T(8,128)S(1)} collective-permute-done((f32[9,5,512]{2,1,0:T(8,128)S(1)}, f32[9,5,512]{2,1,0:T(8,128)S(1)}, u32[]{:S(2)}, u32[]{:S(2)}) %collective-permute-start.3) | collective-permute-done | bytes 92192 | tf_op jit(solution)/shard_map/ppermute | solution.py:23
  97.1 0.4 fusion.20
  97.5 0.8 fusion.10
  99.0 0.8 copy.21.grad_ref
  99.8 26.1 %render_backward.1.in_ref = f32[64,9,128]{2,1,0:T(8,128)} custom-call(f32[32,9,256]{2,1,0:T(8,128)} %get-tuple-element.11.entry_ref, f32[32,256,256]{2,1,0:T(8,128)} %get-tuple-element.12.cover_ref, f32[32,256,256]{2,1,0:T(8,128)} %get-tuple-element.13.keep_ref, f32[3,32,256]{2,1,0:T(8,128)} %copy.21.grad_ref, s32[32,256]{1,0:T(8,128)} %bitcast.24, ...), custom_call_target="tpu_custom_call" | custom-call | tf_op jit(solution)/shard_map/render_backward/pallas_call | solution.py:488
  125.9 21.0 %exchange.3.returned_ref = f32[64,9,128]{2,1,0:T(8,128)} custom-call(f32[64,9,128]{2,1,0:T(8,128)} %render_backward.1.in_ref), custom_call_target="tpu_custom_call" | custom-call | tf_op jit(solution)/shard_map/exchange/pallas_call | solution.py:265
  146.9 11.1 %place_gradients.1.own_ref = f32[9,128,128]{2,1,0:T(8,128)} custom-call(f32[64,9,128]{2,1,0:T(8,128)} %exchange.3.returned_ref, s32[64,128]{1,0:T(8,128)} %bitcast.26, s32[1,64]{1,0:T(1,128)} %count_ref.3), custom_call_target="tpu_custom_call" | custom-call | tf_op jit(solution)/shard_map/place_gradients/pallas_call | solution.py:548
  158.0 6.9 %collective-permute-start.4 = (f32[9,128,128]{2,1,0:T(8,128)}, f32[9,128,128]{2,1,0:T(8,128)S(1)}, u32[]{:S(2)}, u32[]{:S(2)}) collective-permute-start(f32[9,128,128]{2,1,0:T(8,128)} %place_gradients.1.own_ref), channel_id=1, source_target_pairs={{0,64},{64,0},{1,65},{65,1},{2,66},{66,2},{3,67},{67,3},{4,68},{68... | collective-permute-start | bytes 1769480 | tf_op jit(solution)/shard_map/ppermute | solution.py:715
  164.9 64.6 %psum.7 = f32[]{:T(128)} all-reduce(f32[]{:T(128)} %get-tuple-element.18), channel_id=1, replica_groups=mesh['view'=2,'tile'=64] {'view','tile'}, use_global_device_ids=true, to_apply=%region_1.2 | all-reduce | flops 1 | bytes 8 | tf_op jit(solution)/shard_map/psum | solution.py:708
  230.2 0.8 copy-done.1
  231.0 16.5 %update.1 = (f32[59,16384]{1,0:T(8,128)}, f32[59,16384]{1,0:T(8,128)}, f32[59,16384]{1,0:T(8,128)}) custom-call(f32[59,16384]{1,0:T(8,128)} %params_ref.3, f32[59,16384]{1,0:T(8,128)} %first_ref.1, f32[59,16384]{1,0:T(8,128)} %second_ref.1, f32[9,128,128]{2,1,0:T(8,128)} %place_gradients.1.own_ref, f32[9,128,128]{2,1,0:T(8,128)} %copy-done.1, ...), custom_call_target="tpu_custom_call" | custom-call | tf_op jit(solution)/shard_map/update/pallas_call | solution.py:606
  (20 shorter events, 1.7 us)
Async XLA Ops:
  5.0 71.8 %copy-start = (f32[1,3,16,512]{3,2,1,0:T(8,128)S(1)}, f32[1,3,16,512]{3,2,1,0:T(8,128)}, u32[]{:S(2)}) copy-start(f32[1,3,16,512]{3,2,1,0:T(8,128)} %param.15) | copy-start | bytes 294916
  76.8 4.1 %collective-permute-start = (f32[6,5,512]{2,1,0:T(8,128)S(1)}, f32[6,5,512]{2,1,0:T(8,128)S(1)}, u32[]{:S(2)}, u32[]{:S(2)}) collective-permute-start(f32[6,5,512]{2,1,0:T(8,128)S(1)} %get-tuple-element.35), channel_id=1, source_target_pairs={{0,1},{1,2},{2,3},{3,4},{4,5},{5,6},{6,7},{7,8},{8,9},{9,10},{10,1... | collective-permute-start | bytes 184328 | tf_op jit(solution)/shard_map/ppermute | solution.py:20
  79.3 5.4 %collective-permute-start.1 = (f32[6,5,512]{2,1,0:T(8,128)S(1)}, f32[6,5,512]{2,1,0:T(8,128)S(1)}, u32[]{:S(2)}, u32[]{:S(2)}) collective-permute-start(f32[6,5,512]{2,1,0:T(8,128)S(1)} %get-tuple-element.36), channel_id=1, source_target_pairs={{1,0},{2,1},{3,2},{4,3},{5,4},{6,5},{7,6},{8,7},{9,8},{10,9},{11,1... | collective-permute-start | bytes 184328 | tf_op jit(solution)/shard_map/ppermute | solution.py:23
  87.8 5.5 %collective-permute-start.2 = (f32[9,5,512]{2,1,0:T(8,128)S(1)}, f32[9,5,512]{2,1,0:T(8,128)S(1)}, u32[]{:S(2)}, u32[]{:S(2)}) collective-permute-start(f32[9,5,512]{2,1,0:T(8,128)S(1)} %get-tuple-element.30), channel_id=1, source_target_pairs={{0,1},{1,2},{2,3},{3,4},{4,5},{5,6},{6,7},{7,8},{8,9},{9,10},{10,1... | collective-permute-start | bytes 276488 | tf_op jit(solution)/shard_map/ppermute | solution.py:20
  91.1 5.9 %collective-permute-start.3 = (f32[9,5,512]{2,1,0:T(8,128)S(1)}, f32[9,5,512]{2,1,0:T(8,128)S(1)}, u32[]{:S(2)}, u32[]{:S(2)}) collective-permute-start(f32[9,5,512]{2,1,0:T(8,128)S(1)} %get-tuple-element.31), channel_id=1, source_target_pairs={{1,0},{2,1},{3,2},{4,3},{5,4},{6,5},{7,6},{8,7},{9,8},{10,9},{11,1... | collective-permute-start | bytes 276488 | tf_op jit(solution)/shard_map/ppermute | solution.py:23
  158.0 72.2 %collective-permute-start.4 = (f32[9,128,128]{2,1,0:T(8,128)}, f32[9,128,128]{2,1,0:T(8,128)S(1)}, u32[]{:S(2)}, u32[]{:S(2)}) collective-permute-start(f32[9,128,128]{2,1,0:T(8,128)} %place_gradients.1.own_ref), channel_id=1, source_target_pairs={{0,64},{64,0},{1,65},{65,1},{2,66},{66,2},{3,67},{67,3},{4,68},{68... | collective-permute-start | bytes 1769480 | tf_op jit(solution)/shard_map/ppermute | solution.py:715
  230.2 0.8 copy-start.1

commit v2 on v1

v2 whole, which is shorter than its diff:
```python
import functools
import math

import jax
import jax.numpy as jnp
from jax import lax
from jax.experimental import pallas as pl
from jax.experimental.pallas import tpu as pltpu
from jax.sharding import PartitionSpec as P

STEP_COUNT = 20
LIST = 256


def extended(block, sides, width):
    for axis, dim in sides:
        count = lax.axis_size(axis)
        forward = [(i, i + 1) for i in range(count - 1)]
        backward = [(target, source) for source, target in forward]
        low = lax.ppermute(
            lax.slice_in_dim(block, block.shape[dim] - width, None, axis=dim), axis, forward
        )
        high = lax.ppermute(lax.slice_in_dim(block, 0, width, axis=dim), axis, backward)
        block = jnp.concatenate([low, block, high], axis=dim)
    return block


def window_taps():
    raw_taps = [math.exp(-(position - 5) * (position - 5) / 4.5) for position in range(11)]
    return [element / sum(raw_taps) for element in raw_taps]


def harmonics(unit_x, unit_y, unit_z):
    square_x = unit_x * unit_x
    square_y = unit_y * unit_y
    square_z = unit_z * unit_z
    return [
        0.28209479177387814 * jnp.ones_like(unit_x),
        -0.4886025119029199 * unit_y,
        0.4886025119029199 * unit_z,
        -0.4886025119029199 * unit_x,
        1.0925484305920792 * unit_x * unit_y,
        -1.0925484305920792 * unit_y * unit_z,
        0.31539156525252005 * (2.0 * square_z - square_x - square_y),
        -1.0925484305920792 * unit_x * unit_z,
        0.5462742152960396 * (square_x - square_y),
        -0.5900435899266435 * unit_y * (3.0 * square_x - square_y),
        2.890611442640554 * unit_x * unit_y * unit_z,
        -0.4570457994644658 * unit_y * (4.0 * square_z - square_x - square_y),
        0.3731763325901154 * unit_z * (2.0 * square_z - 3.0 * square_x - 3.0 * square_y),
        -0.4570457994644658 * unit_x * (4.0 * square_z - square_x - square_y),
        1.445305721320277 * unit_z * (square_x - square_y),
        -0.5900435899266435 * unit_x * (square_x - 3.0 * square_y),
    ]


MESH = pl.DeviceIdType.MESH
VMEM_LIMIT = 56 * 1024 * 1024
NN = (((1,), (0,)), ((), ()))
NT = (((1,), (1,)), ((), ()))
TN = (((0,), (0,)), ((), ()))


def mxu(left, right, dims):
    return lax.dot_general(left, right, dims, preferred_element_type=jnp.float32)


def split2(value):
    high = value.astype(jnp.bfloat16)
    low = (value - high.astype(jnp.float32)).astype(jnp.bfloat16)
    return high, low


def split3(value):
    high = value.astype(jnp.bfloat16)
    rest = value - high.astype(jnp.float32)
    middle = rest.astype(jnp.bfloat16)
    low = (rest - middle.astype(jnp.float32)).astype(jnp.bfloat16)
    return high, middle, low


def project_rows(rows, cameras):
    pos_x, pos_y, pos_z = rows[0:3]
    scales = [jnp.exp(row) for row in rows[3:6]]
    quat_w, quat_x, quat_y, quat_z = rows[6:10]
    norm = 1.0 / jnp.sqrt(
        quat_w * quat_w + quat_x * quat_x + quat_y * quat_y + quat_z * quat_z
    )
    quat_w, quat_x, quat_y, quat_z = quat_w * norm, quat_x * norm, quat_y * norm, quat_z * norm
    rotation = [
        [
            1.0 - 2.0 * (quat_y * quat_y + quat_z * quat_z),
            2.0 * (quat_x * quat_y - quat_w * quat_z),
            2.0 * (quat_x * quat_z + quat_w * quat_y),
        ],
        [
            2.0 * (quat_x * quat_y + quat_w * quat_z),
            1.0 - 2.0 * (quat_x * quat_x + quat_z * quat_z),
            2.0 * (quat_y * quat_z - quat_w * quat_x),
        ],
        [
            2.0 * (quat_x * quat_z - quat_w * quat_y),
            2.0 * (quat_y * quat_z + quat_w * quat_x),
            1.0 - 2.0 * (quat_x * quat_x + quat_y * quat_y),
        ],
    ]
    opacity = 1.0 / (1.0 + jnp.exp(-rows[10]))
    records = []
    for shear_x, shear_y, offset_x, offset_y, center_x, center_y, center_z in cameras:
        first = [(rotation[0][k] + shear_x * rotation[2][k]) * scales[k] for k in range(3)]
        second = [(rotation[1][k] + shear_y * rotation[2][k]) * scales[k] for k in range(3)]
        cov_xx = first[0] * first[0] + first[1] * first[1] + first[2] * first[2] + 0.3
        cov_yy = second[0] * second[0] + second[1] * second[1] + second[2] * second[2] + 0.3
        cov_xy = first[0] * second[0] + first[1] * second[1] + first[2] * second[2]
        inverse = 1.0 / (cov_xx * cov_yy - cov_xy * cov_xy)
        toward_x = pos_x - center_x
        toward_y = pos_y - center_y
        toward_z = pos_z - center_z
        shrink = 1.0 / jnp.sqrt(toward_x * toward_x + toward_y * toward_y + toward_z * toward_z)
        basis = harmonics(toward_x * shrink, toward_y * shrink, toward_z * shrink)
        colors = []
        for c in range(3):
            total = basis[0] * rows[11 + c]
            for k in range(1, 16):
                total = total + basis[k] * rows[11 + 3 * k + c]
            colors.append(0.5 + total)
        records.append(
            [
                pos_x + shear_x * pos_z + offset_x,
                pos_y + shear_y * pos_z + offset_y,
                cov_yy * inverse,
                -cov_xy * inverse,
                cov_xx * inverse,
                opacity,
                *colors,
            ]
        )
    return records


def camera_of(refs, view):
    shear_ref, offset_ref, center_ref = refs
    return (
        shear_ref[view, 0],
        shear_ref[view, 1],
        offset_ref[view, 0],
        offset_ref[view, 1],
        center_ref[view, 0],
        center_ref[view, 1],
        center_ref[view, 2],
    )


BLOCK = 4096


def dense_rows(source_ref, sub):
    count = source_ref.shape[0]
    columns = pl.ds(pl.multiple_of(1024 * sub, 1024), 1024)
    rows = []
    for first in range(0, count, 8):
        size = min(8, count - first)
        block = source_ref[first : first + size, columns].reshape(size, 8, 128)
        rows += [block[r] for r in range(size)]
    return rows


def project_kernel(
    params_ref, index_ref, view_ref, shear_ref, offset_ref, center_ref, out_ref, table, high_parts, low_parts
):
    step = pl.program_id(0)
    camera = camera_of((shear_ref, offset_ref, center_ref), view_ref[0])

    def part(sub, carry):
        record = project_rows(dense_rows(params_ref, sub), [camera])[0]
        first = pl.multiple_of(step * (BLOCK // 128) + 8 * sub, 8)
        for q in range(9):
            table[q, pl.ds(first, 8), :] = record[q]
        return carry

    lax.fori_loop(0, BLOCK // 1024, part, 0, unroll=2)

    @pl.when(step == pl.num_programs(0) - 1)
    def _():
        for q in range(9):
            for half in range(2):
                store_parts(
                    table[q, 64 * half : 64 * half + 64, :],
                    high_parts, low_parts, q, pl.ds(128 * half, 128),
                )
        low_ids = lax.broadcasted_iota(jnp.int32, (256, 256), 0)
        high_ids = lax.broadcasted_iota(jnp.int32, (64, 256), 0)

        def pick(pair, carry):
            index = jnp.concatenate(
                [index_ref[pl.ds(pair, 1), :], index_ref[pl.ds(pair + 32, 1), :]], axis=1
            )
            high = (index >> 7) & 63
            low = (index & 127) + ((index >> 13) << 7)
            rows = pick_rows(high_parts, low_parts, one_hot(low_ids, low), high_ids == high)
            for q in range(9):
                out_ref[pair, q : q + 1, :] = rows[q][:, 0:128]
                out_ref[pair + 32, q : q + 1, :] = rows[q][:, 128:256]
            return carry

        lax.fori_loop(0, 32, pick, 0, unroll=4)


def project_and_pick(params, send_index, view, shear, offset, center):
    smem = pl.BlockSpec(memory_space=pltpu.SMEM)
    return pl.pallas_call(
        project_kernel,
        grid=(16384 // BLOCK,),
        out_shape=jax.ShapeDtypeStruct((64, 9, 128), jnp.float32),
        in_specs=[
            pl.BlockSpec((59, BLOCK), lambda i: (0, i)),
            pl.BlockSpec((64, 128), lambda i: (0, 0)),
            smem,
            smem,
            smem,
            smem,
        ],
        out_specs=pl.BlockSpec((64, 9, 128), lambda i: (0, 0, 0)),
        scratch_shapes=[
            pltpu.VMEM((9, 128, 128), jnp.float32),
            pltpu.VMEM((576, 512), jnp.bfloat16),
            pltpu.VMEM((128, 256), jnp.bfloat16),
        ],
        compiler_params=pltpu.CompilerParams(vmem_limit_bytes=VMEM_LIMIT),
        name="project_and_pick",
    )(params, send_index, view, shear, offset, center)


def axis_peers(me, stride):
    place = lax.rem(me // stride, 4)
    return [me + (lax.rem(place + j, 4) - place) * stride for j in range(1, 4)]


def signal_all(semaphore, peers):
    for peer in peers:
        pl.semaphore_signal(semaphore, inc=1, device_id={"tile": peer}, device_id_type=MESH)


def exchange_kernel(in_ref, out_ref, send_sem, recv_sem, local_sem, plane_sem, cube_sem):
    total = lax.axis_size("tile")
    me = lax.axis_index("tile")
    barrier = pltpu.get_barrier_semaphore()
    lines = [axis_peers(me, stride) for stride in (1, 4, 16)]
    for line in lines:
        signal_all(barrier, line)
    own = pltpu.make_async_copy(in_ref.at[me], out_ref.at[me], local_sem)
    own.start()
    pl.semaphore_wait(barrier, 9)
    signal_all(plane_sem, lines[1])
    pl.semaphore_wait(plane_sem, 3)
    signal_all(cube_sem, lines[2])
    pl.semaphore_wait(cube_sem, 3)

    def copy_to(p):
        peer = lax.rem(me + p, total)
        return pltpu.make_async_remote_copy(
            src_ref=in_ref.at[peer],
            dst_ref=out_ref.at[me],
            send_sem=send_sem.at[p],
            recv_sem=recv_sem.at[p],
            device_id={"tile": peer},
            device_id_type=MESH,
        )

    def send(p, carry):
        copy_to(p).start()
        return carry

    def finish(p, carry):
        copy_to(p).wait()
        return carry

    lax.fori_loop(1, total, send, 0)
    own.wait()
    lax.fori_loop(1, total, finish, 0)


def exchange(blocks, collective_id):
    vmem = pl.BlockSpec(memory_space=pltpu.VMEM)
    total = blocks.shape[0]
    return pl.pallas_call(
        exchange_kernel,
        out_shape=jax.ShapeDtypeStruct(blocks.shape, blocks.dtype),
        in_specs=[vmem],
        out_specs=vmem,
        scratch_shapes=[
            pltpu.SemaphoreType.DMA((total,)),
            pltpu.SemaphoreType.DMA((total,)),
            pltpu.SemaphoreType.DMA,
            pltpu.SemaphoreType.REGULAR,
            pltpu.SemaphoreType.REGULAR,
        ],
        compiler_params=pltpu.CompilerParams(
            collective_id=collective_id, has_side_effects=True, vmem_limit_bytes=VMEM_LIMIT
        ),
        name="exchange",
    )(blocks)


TILES_STEP = 8
CHUNK = 16
UNROLL = 4


def slot_place(index):
    return (index >> 7) & 31, (index & 127) + ((index >> 12) << 7)


def one_hot(ids, values):
    return (ids == values).astype(jnp.float32).astype(jnp.bfloat16)


def store_parts(rows, high_parts, low_parts, q, columns):
    count = rows.shape[0]
    high, middle, low = split3(rows)
    here = pl.ds(count * q, count)
    width = columns.size
    high_parts[here, columns] = high
    high_parts[here, pl.ds(columns.start + 256, width)] = middle
    if q < 2:
        low_parts[here, columns] = low


def both_parts(value, right, dims):
    sums = mxu(jnp.concatenate(split2(value), axis=0), right, dims)
    return sums[: value.shape[0]] + sums[value.shape[0] :]


def pick_rows(high_parts, low_parts, hot, mask):
    count = mask.shape[0]
    found = mxu(high_parts[...], jnp.concatenate([hot, hot], axis=0), NN)
    found_low = mxu(low_parts[...], hot, NN)
    rows = []
    for q in range(9):
        part = found[count * q : count * q + count]
        if q < 2:
            part = part + found_low[count * q : count * q + count]
        rows.append(jnp.sum(jnp.where(mask, part, 0.0), axis=0, keepdims=True))
    return rows


def tile_deltas(tile, band, u_row, w_row):
    offsets = lax.broadcasted_iota(jnp.int32, (16, 256), 0)
    pixel_x = (offsets + 16 * tile).astype(jnp.float32) + 0.5
    pixel_y = (offsets + 16 * band).astype(jnp.float32) + 0.5
    return pixel_x - u_row, pixel_y - w_row


def forward_kernel(
    slots_ref, list_ref, count_ref, band_ref, view_ref, back_ref,
    image_ref, entry_ref, cover_ref, keep_ref,
    high_parts, low_parts, before, picked, total,
):
    step = pl.program_id(0)
    view = view_ref[0]
    band = band_ref[0]
    lanes = lax.broadcasted_iota(jnp.int32, (1, 256), 1)

    @pl.when(step == 0)
    def _():
        for q in range(9):
            for half in range(2):
                store_parts(
                    slots_ref[32 * half : 32 * half + 32, q, :],
                    high_parts, low_parts, q, pl.ds(128 * half, 128),
                )
        row_ids = lax.broadcasted_iota(jnp.int32, (256, 256), 0)
        column_ids = lax.broadcasted_iota(jnp.int32, (256, 256), 1)
        before[...] = (row_ids < column_ids).astype(jnp.float32).astype(jnp.bfloat16)
        total[...] = jnp.zeros_like(total)
        high_ids = lax.broadcasted_iota(jnp.int32, (32, 256), 0)

        def pick(tile, carry):
            high, low = slot_place(list_ref[pl.ds(tile, 1), :])
            rows = pick_rows(high_parts, low_parts, one_hot(row_ids, low), high_ids == high)
            rows[5] = jnp.where(lanes < count_ref[0, tile], rows[5], 0.0)
            for c in range(3):
                rows[6 + c] = rows[6 + c] - back_ref[view, c]
            for q in range(9):
                picked[tile, q : q + 1, :] = rows[q]
            return carry

        lax.fori_loop(0, 32, pick, 0, unroll=4)

    color_ids = lax.broadcasted_iota(jnp.int32, (128, 256), 0)

    def one(k, carry):
        tile = step * TILES_STEP + k
        rows = [picked[tile, q : q + 1, :] for q in range(9)]
        for q in range(9):
            entry_ref[k, q : q + 1, :] = rows[q]
        delta_x, delta_y = tile_deltas(tile, band, rows[0], rows[1])
        along_x = -0.5 * rows[2] * delta_x * delta_x
        mixed = -rows[3] * delta_x
        along_y = -0.5 * rows[4] * delta_y * delta_y
        colors = jnp.zeros((128, 256), jnp.float32)
        for c in range(3):
            colors = jnp.where(color_ids == 3 * tile + c, rows[6 + c], colors)
        colors = jnp.concatenate(split2(colors), axis=0)
        for first in range(0, 16, CHUNK):
            pieces = []
            for i in range(first, first + CHUNK):
                exponent = along_x + (mixed * delta_y[i : i + 1] + along_y[i : i + 1])
                pieces.append(rows[5] * jnp.exp(exponent))
            cover = jnp.concatenate(pieces, axis=0)
            keep = jnp.exp(both_parts(jnp.log(1.0 - cover), before[...], NN))
            here = slice(16 * first, 16 * (first + CHUNK))
            cover_ref[k, here] = cover
            keep_ref[k, here] = keep
            shown = mxu(jnp.concatenate(split2(cover * keep), axis=0), colors, NT)
            size = 16 * CHUNK
            total[here] += shown[0:size, 0:128] + shown[0:size, 128:256] + shown[size:, 0:128]
        return carry

    lax.fori_loop(0, TILES_STEP, one, 0, unroll=UNROLL)

    @pl.when(step == pl.num_programs(0) - 1)
    def _():
        image_ref[...] = jnp.transpose(total[...])


def render_forward(slots, lists, counts, band, view, back):
    smem = pl.BlockSpec(memory_space=pltpu.SMEM)
    field = jax.ShapeDtypeStruct((32, 256, 256), jnp.float32)
    field_spec = pl.BlockSpec((TILES_STEP, 256, 256), lambda i: (i, 0, 0))
    return pl.pallas_call(
        forward_kernel,
        grid=(32 // TILES_STEP,),
        out_shape=(
            jax.ShapeDtypeStruct((128, 256), jnp.float32),
            jax.ShapeDtypeStruct((32, 9, 256), jnp.float32),
            field,
            field,
        ),
        in_specs=[
            pl.BlockSpec((64, slots.shape[1], 128), lambda i: (0, 0, 0)),
            pl.BlockSpec((32, 256), lambda i: (0, 0)),
            smem,
            smem,
            smem,
            smem,
        ],
        out_specs=(
            pl.BlockSpec((128, 256), lambda i: (0, 0)),
            pl.BlockSpec((TILES_STEP, 9, 256), lambda i: (i, 0, 0)),
            field_spec,
            field_spec,
        ),
        scratch_shapes=[
            pltpu.VMEM((288, 512), jnp.bfloat16),
            pltpu.VMEM((64, 256), jnp.bfloat16),
            pltpu.VMEM((256, 256), jnp.bfloat16),
            pltpu.VMEM((32, 9, 256), jnp.float32),
            pltpu.VMEM((256, 128), jnp.float32),
        ],
        compiler_params=pltpu.CompilerParams(vmem_limit_bytes=VMEM_LIMIT),
        name="render_forward",
    )(slots, lists, counts, band, view, back)


def backward_kernel(
    entry_ref, cover_ref, keep_ref, grad_ref, list_ref, band_ref, loss_ref, out_ref,
    after, total, results, high_weights, low_weights,
):
    step = pl.program_id(0)

    @pl.when(step == 0)
    def _():
        row_ids = lax.broadcasted_iota(jnp.int32, (256, 256), 0)
        column_ids = lax.broadcasted_iota(jnp.int32, (256, 256), 1)
        after[...] = (row_ids > column_ids).astype(jnp.float32).astype(jnp.bfloat16)

    band = band_ref[0]

    def fold(value):
        return jnp.sum(value, axis=0, keepdims=True)

    def one(k, carry):
        tile = step * TILES_STEP + k
        rows = [entry_ref[k, q : q + 1, :] for q in range(9)]
        grads = jnp.concatenate([grad_ref[c, pl.ds(tile, 1), :] for c in range(3)], axis=0)
        colors = jnp.concatenate(rows[6:9], axis=0)
        grads_high = grads.astype(jnp.bfloat16).astype(jnp.float32)
        grads_low = grads - grads_high
        colors_high = colors.astype(jnp.bfloat16).astype(jnp.float32)
        colors_low = colors - colors_high
        blank = jnp.zeros((7, 256), jnp.float32)
        left = jnp.concatenate([grads_high, grads_high, grads_low, blank], axis=0).astype(jnp.bfloat16)
        right = jnp.concatenate([colors_high, colors_low, colors_high, blank], axis=0).astype(jnp.bfloat16)
        both = jnp.concatenate([grads_high, grads_low, blank, blank[0:3]], axis=0).astype(jnp.bfloat16)
        delta_x, delta_y = tile_deltas(tile, band, rows[0], rows[1])
        sum_0 = jnp.zeros((16, 256), jnp.float32)
        sum_y = sum_0
        sum_yy = sum_0
        for first in range(0, 16, CHUNK):
            here = slice(16 * first, 16 * (first + CHUNK))
            shade = mxu(left[:, here], right, TN)
            cover = cover_ref[k, here]
            weight = cover * keep_ref[k, here]
            weight_high, weight_low = split2(weight)
            high_weights[k % 2, here] = weight_high
            low_weights[k % 2, here] = weight_low
            lit = weight * shade
            behind = both_parts(lit, after[...], NN)
            pull = lit - behind * (cover / (1.0 - cover))
            for i in range(CHUNK):
                piece = pull[16 * i : 16 * i + 16]
                level = delta_y[first + i : first + i + 1]
                piece_y = piece * level
                sum_0 = sum_0 + piece
                sum_y = sum_y + piece_y
                sum_yy = sum_yy + piece_y * level
        color_grad = mxu(both, high_weights[k % 2], NN)
        color_grad = color_grad[0:3] + color_grad[3:6] + mxu(both, low_weights[k % 2], NN)[0:3]
        sum_x = sum_0 * delta_x
        moment_0 = fold(sum_0)
        moment_x = fold(sum_x)
        moment_xx = fold(sum_x * delta_x)
        moment_y = fold(sum_y)
        moment_xy = fold(sum_y * delta_x)
        moment_yy = fold(sum_yy)
        live = rows[5] > 0.0
        values = [
            rows[2] * moment_x + rows[3] * moment_y,
            rows[4] * moment_y + rows[3] * moment_x,
            -0.5 * moment_xx,
            -moment_xy,
            -0.5 * moment_yy,
            jnp.where(live, moment_0 / jnp.where(live, rows[5], 1.0), 0.0),
            color_grad[0:1],
            color_grad[1:2],
            color_grad[2:3],
        ]
        for q in range(9):
            results[tile, q : q + 1, :] = values[q]
        return carry

    lax.fori_loop(0, TILES_STEP, one, 0, unroll=UNROLL)

    @pl.when(step == pl.num_programs(0) - 1)
    def _():
        low_ids = lax.broadcasted_iota(jnp.int32, (256, 256), 0)
        high_ids = lax.broadcasted_iota(jnp.int32, (32, 256), 0)
        total[...] = jnp.zeros_like(total)

        def place(tile, carry):
            high, low = slot_place(list_ref[pl.ds(tile, 1), :])
            place_rows([results[tile, q : q + 1, :] for q in range(9)], total, one_hot(low_ids, low), high_ids == high)
            return carry

        lax.fori_loop(0, 32, place, 0, unroll=4)
        for q in range(9):
            for half in range(2):
                out_ref[32 * half : 32 * half + 32, q, :] = total[
                    32 * q : 32 * q + 32, 128 * half : 128 * half + 128
                ]
        out_ref[:, 9, :] = jnp.broadcast_to(loss_ref[...], (64, 128))


def place_rows(rows, total, hot, mask):
    count = mask.shape[0]
    high_rows, low_rows = [], []
    for row in rows:
        high = row.astype(jnp.bfloat16).astype(jnp.float32)
        high_rows.append(jnp.where(mask, high, 0.0))
        low_rows.append(jnp.where(mask, row - high, 0.0))
    placed = jnp.concatenate(high_rows + low_rows, axis=0).astype(jnp.bfloat16)
    sums = mxu(placed, hot, NT)
    total[...] += sums[: 9 * count] + sums[9 * count :]


def render_backward(entries, cover, keep, grads, lists, band, loss):
    smem = pl.BlockSpec(memory_space=pltpu.SMEM)
    field_spec = pl.BlockSpec((TILES_STEP, 256, 256), lambda i: (i, 0, 0))
    return pl.pallas_call(
        backward_kernel,
        grid=(32 // TILES_STEP,),
        out_shape=jax.ShapeDtypeStruct((64, 10, 128), jnp.float32),
        in_specs=[
            pl.BlockSpec((TILES_STEP, 9, 256), lambda i: (i, 0, 0)),
            field_spec,
            field_spec,
            pl.BlockSpec((3, 32, 256), lambda i: (0, 0, 0)),
            pl.BlockSpec((32, 256), lambda i: (0, 0)),
            smem,
            pl.BlockSpec((1, 128), lambda i: (0, 0)),
        ],
        out_specs=pl.BlockSpec((64, 10, 128), lambda i: (0, 0, 0)),
        scratch_shapes=[
            pltpu.VMEM((256, 256), jnp.bfloat16),
            pltpu.VMEM((288, 256), jnp.float32),
            pltpu.VMEM((32, 9, 256), jnp.float32),
            pltpu.VMEM((2, 256, 256), jnp.bfloat16),
            pltpu.VMEM((2, 256, 256), jnp.bfloat16),
        ],
        compiler_params=pltpu.CompilerParams(vmem_limit_bytes=VMEM_LIMIT),
        name="render_backward",
    )(entries, cover, keep, grads, lists, band, loss)
def place_kernel(returned_ref, index_ref, count_ref, out_ref, total):
    total[...] = jnp.zeros_like(total)
    low_ids = lax.broadcasted_iota(jnp.int32, (256, 256), 0)
    high_ids = lax.broadcasted_iota(jnp.int32, (64, 256), 0)
    lanes = lax.broadcasted_iota(jnp.int32, (1, 128), 1)

    def place(pair, carry):
        def joined(values):
            return jnp.concatenate(values, axis=1)

        bands = (pair, pair + 32)
        index = joined([index_ref[pl.ds(d, 1), :] for d in bands])
        live = joined([(lanes < count_ref[0, d]).astype(jnp.int32) for d in bands])
        high = jnp.where(live > 0, (index >> 7) & 63, -1)
        low = (index & 127) + ((index >> 13) << 7)
        rows = [joined([returned_ref[d, q : q + 1, :] for d in bands]) for q in range(9)]
        place_rows(rows, total, one_hot(low_ids, low), high_ids == high)
        return carry

    lax.fori_loop(0, 32, place, 0, unroll=4)
    for q in range(9):
        for half in range(2):
            out_ref[q, 64 * half : 64 * half + 64, :] = total[
                64 * q : 64 * q + 64, 128 * half : 128 * half + 128
            ]
    loss = jnp.sum(returned_ref[:, 9, :], axis=0, keepdims=True)
    out_ref[9] = jnp.broadcast_to(loss, (128, 128))


def place_gradients(returned, send_index, send_count):
    vmem = pl.BlockSpec(memory_space=pltpu.VMEM)
    return pl.pallas_call(
        place_kernel,
        out_shape=jax.ShapeDtypeStruct((10, 128, 128), jnp.float32),
        in_specs=[vmem, vmem, pl.BlockSpec(memory_space=pltpu.SMEM)],
        out_specs=vmem,
        scratch_shapes=[pltpu.VMEM((576, 256), jnp.float32)],
        compiler_params=pltpu.CompilerParams(vmem_limit_bytes=VMEM_LIMIT),
        name="place_gradients",
    )(returned, send_index, send_count)


RATES = [0.016] * 3 + [0.005] * 3 + [0.001] * 4 + [0.05] + [0.0025] * 3 + [0.000125] * 45
LOSS_TERMS = 2 * 3 * 1024 * 512


def update_kernel(
    params_ref, first_ref, second_ref, own_ref, other_ref, view_ref, shear_ref, offset_ref, center_ref,
    params_out, first_out, second_out, loss_out, dense,
):
    refs = (shear_ref, offset_ref, center_ref)
    cameras = [camera_of(refs, 0), camera_of(refs, 1)]
    is_first = view_ref[0] == 0
    loss_out[...] = (own_ref[9, 0:1, 0:1] + other_ref[9, 0:1, 0:1]) / LOSS_TERMS

    def part(sub, carry):
        rows = dense_rows(params_ref, sub)
        _, pull_back = jax.vjp(lambda *values: project_rows(values, cameras), *rows)
        here = pl.ds(pl.multiple_of(8 * sub, 8), 8)
        own = [own_ref[q, here, :] for q in range(9)]
        other = [other_ref[q, here, :] for q in range(9)]
        gradient = pull_back(
            [
                [jnp.where(is_first, a, b) for a, b in zip(own, other)],
                [jnp.where(is_first, b, a) for a, b in zip(own, other)],
            ]
        )
        for r in range(59):
            dense[8 * r : 8 * r + 8, :] = gradient[r]
        for first in range(0, 59, 8):
            size = min(8, 59 - first)
            row_ids = lax.broadcasted_iota(jnp.int32, (size, 128), 0)
            rate = jnp.full((size, 128), RATES[first], jnp.float32)
            for r in range(1, size):
                if RATES[first + r] != RATES[first + r - 1]:
                    rate = jnp.where(row_ids >= r, RATES[first + r], rate)
            rate = rate / (1.0 - 0.9**STEP_COUNT)
            for c in range(8):
                columns = pl.ds(pl.multiple_of(1024 * sub + 128 * c, 128), 128)
                here = (slice(first, first + size), columns)
                grad = dense[pl.ds(8 * first + c, size, stride=8), :]
                new_first = 0.9 * first_ref[here] + 0.1 * grad
                new_second = 0.999 * second_ref[here] + 0.001 * grad * grad
                scale = jnp.sqrt(new_second * (1.0 / (1.0 - 0.999**STEP_COUNT))) + 1e-15
                params_out[here] = params_ref[here] - rate * new_first / scale
                first_out[here] = new_first
                second_out[here] = new_second
        return carry

    lax.fori_loop(0, BLOCK // 1024, part, 0)


def update(params, first_moment, second_moment, own, other, view, shear, offset, center):
    smem = pl.BlockSpec(memory_space=pltpu.SMEM)
    block = pl.BlockSpec((59, BLOCK), lambda i: (0, i))
    grads = pl.BlockSpec((10, BLOCK // 128, 128), lambda i: (0, i, 0))
    shape = jax.ShapeDtypeStruct(params.shape, jnp.float32)
    return pl.pallas_call(
        update_kernel,
        grid=(16384 // BLOCK,),
        out_shape=(shape, shape, shape, jax.ShapeDtypeStruct((1, 1), jnp.float32)),
        in_specs=[block, block, block, grads, grads, smem, smem, smem, smem],
        out_specs=(block, block, block, pl.BlockSpec((1, 1), lambda i: (0, 0))),
        scratch_shapes=[pltpu.VMEM((59 * 8, 128), jnp.float32)],
        compiler_params=pltpu.CompilerParams(vmem_limit_bytes=VMEM_LIMIT),
        name="update",
    )(params, first_moment, second_moment, own, other, view, shear, offset, center)


def gaussian_blur(planes):
    taps = window_taps()
    rows_out = planes.shape[1] - 10
    vertical = taps[0] * planes[:, 0:rows_out]
    for position in range(1, 11):
        vertical = vertical + taps[position] * planes[:, position : position + rows_out]
    image_width = planes.shape[2]
    padded = jnp.pad(vertical, ((0, 0), (0, 0), (5, 5)))
    result = taps[0] * padded[:, :, 0:image_width]
    for position in range(1, 11):
        result = result + taps[position] * padded[:, :, position : position + image_width]
    return result


def ssim_map(level_x, level_y, energy_x, energy_y, product_xy):
    upper = (2.0 * level_x * level_y + 0.0001) * (2.0 * (product_xy - level_x * level_y) + 0.0009)
    lower = (level_x * level_x + level_y * level_y + 0.0001) * (
        energy_x - level_x * level_x + (energy_y - level_y * level_y) + 0.0009
    )
    return upper / lower


def window_stats(widened):
    shown = widened[0:3]
    truth = widened[3:6]
    mean_x = gaussian_blur(shown)
    mean_y = gaussian_blur(truth)
    power_x = gaussian_blur(shown * shown)
    power_y = gaussian_blur(truth * truth)
    cross_xy = gaussian_blur(shown * truth)
    return (mean_x, mean_y, power_x, power_y, cross_xy)


def shards(
    params,
    first_moment,
    second_moment,
    target,
    view_shear,
    view_offset,
    cam_center,
    background,
    send_index,
    send_count,
    tile_list,
    tile_count,
):
    view_index = lax.axis_index("view")
    band_index = lax.axis_index("tile")

    view = view_index.astype(jnp.int32).reshape(1)
    band = band_index.astype(jnp.int32).reshape(1)
    backdrop = lax.dynamic_index_in_dim(background, view_index, 0, keepdims=False)
    outgoing = project_and_pick(params, send_index[0], view, view_shear, view_offset, cam_center)
    incoming = exchange(outgoing, 0)
    shown, entries, cover, keep = render_forward(
        incoming, tile_list[0, 0], tile_count, band, view, background
    )
    image_band = shown[:96].reshape(32, 3, 16, 16).transpose(1, 2, 0, 3).reshape(3, 16, 512)
    image_band = image_band + backdrop[:, None, None]
    frame_band = target[0]
    stacked = jnp.concatenate([image_band, frame_band], axis=0)
    widened = extended(stacked, (("tile", 1),), 5)
    mean_x, mean_y, power_x, power_y, cross_xy = window_stats(widened)
    similarity, ssim_back = jax.vjp(
        lambda level_x, energy_x, product_xy: ssim_map(
            level_x, mean_y, energy_x, power_y, product_xy
        ),
        mean_x,
        power_x,
        cross_xy,
    )
    grad_mean, grad_power, grad_cross = ssim_back(jnp.full_like(similarity, -0.8))
    spread = extended(
        jnp.concatenate([grad_mean, grad_power, grad_cross], axis=0), (("tile", 1),), 5
    )
    blurred = gaussian_blur(spread)
    difference = image_band - frame_band
    smooth = jnp.sqrt(difference * difference + 0.0001)
    loss_part = jnp.sum(0.2 * smooth + 0.8 * (1.0 - similarity))
    pixel_grad = (
        0.2 * difference / smooth
        + blurred[0:3]
        + 2.0 * image_band * blurred[3:6]
        + frame_band * blurred[6:9]
    )
    grad_tiles = pixel_grad.reshape(3, 16, 32, 16).transpose(0, 2, 1, 3).reshape(3, 32, 256)
    loss_row = jnp.broadcast_to(loss_part, (1, 128))
    slot_grad = render_backward(entries, cover, keep, grad_tiles, tile_list[0, 0], band, loss_row)
    returned = exchange(slot_grad, 1)
    own_grad = place_gradients(returned, send_index[0], send_count)
    other_grad = lax.ppermute(own_grad, "view", [(0, 1), (1, 0)])
    new_params, new_first, new_second, mean_loss = update(
        params, first_moment, second_moment, own_grad, other_grad, view, view_shear, view_offset, cam_center
    )
    return (new_params, new_first, new_second, mean_loss[0, 0])


def solution(mesh):
    placed = (
        P(None, "tile"),
        P(None, "tile"),
        P(None, "tile"),
        P("view", None, "tile", None),
        P(),
        P(),
        P(),
        P(),
        P("tile", None, None),
        P("tile", None),
        P("view", "tile", None, None),
        P("tile", None),
    )
    return jax.shard_map(
        shards,
        mesh=mesh,
        in_specs=placed,
        out_specs=(P(None, "tile"), P(None, "tile"), P(None, "tile"), P()),
        check_vma=False,
    )
```

time: 250 us -> 147 us (0.59)
  blocking collectives: 64.6 us -> 0 us
  Pallas kernels: 145 us -> 112 us
    psum x1 -> x0, blocking collectives: 64.6 us -> none  [shards(): lax.psum(loss_part, ('view', 'tile'))]
    pallas_call x3, Pallas kernels: 47.8 us -> 33.6 us  [the longest x1 12.8 us: update(): pl.pallas_call(update_kernel, grid=(16384 // BLOCK,), out_shape=(shape, s...]
    pallas_call x1, Pallas kernels: 32 us -> 18.4 us  [render_forward(): pl.pallas_call(forward_kernel, grid=(32 // TILES_STEP,), out_shape=(jax.S...]
    pallas_call x1, Pallas kernels: 26.1 us -> 17.1 us  [render_backward(): pl.pallas_call(backward_kernel, grid=(32 // TILES_STEP,), out_shape=jax.S...]
    pallas_call x2, Pallas kernels: 38.8 us -> 42.6 us  [exchange(): pl.pallas_call(exchange_kernel, out_shape=jax.ShapeDtypeStruct(blocks.sha...]
    rev x4 -> x0, local copies, waits for them, and re-layouts: 2.8 us -> none  [own_first(): return jnp.where(view_index == 0, values, values[::-1])]
  transfers between devices with their start and end apart: 5 -> 5, of which waited for: 4 -> 5; matrix products, arithmetic and copies ran while one was open for 0% -> 0% of each run, Pallas kernels for 0% -> 0%
where the time goes in v2:
time: 147 us
  Pallas kernels  112 us (76%)
  starting transfers between devices  14.2 us (10%)
  waiting for transfers between devices  10.4 us (7%)
  local copies, waits for them, and re-layouts  5.18 us (4%)
  other arithmetic  4.45 us (3%)
    pallas_call x2, Pallas kernels, exchange(): pl.pallas_call(exchange_kernel, out_shape=jax.ShapeDtypeStruct(blocks.sha...  42.6 us
    pallas_call x1, Pallas kernels, render_forward(): pl.pallas_call(forward_kernel, grid=(32 // TILES_STEP,), out_shape=(jax.S...  18.4 us
    pallas_call x1, Pallas kernels, render_backward(): pl.pallas_call(backward_kernel, grid=(32 // TILES_STEP,), out_shape=jax.S...  17.1 us
    pallas_call x1, Pallas kernels, update(): pl.pallas_call(update_kernel, grid=(16384 // BLOCK,), out_shape=(shape, s...  12.8 us
    pallas_call x1, Pallas kernels, project_and_pick(): pl.pallas_call(project_kernel, grid=(16384 // BLOCK,), out_shape=jax.Shap...  12.2 us
    pallas_call x1, Pallas kernels, place_gradients(): pl.pallas_call(place_kernel, out_shape=jax.ShapeDtypeStruct((10, 128, 128...  8.53 us
    ppermute x2, waiting for transfers between devices, extended(): lax.ppermute(lax.slice_in_dim(block, 0, width, axis=dim), axis, backward)  7.55 us
    ppermute x1, starting transfers between devices, shards(): other_grad = lax.ppermute(own_grad, 'view', [(0, 1), (1, 0)])  6.46 us
  transfers between devices with their start and end apart: 5, of which 5 were waited for; matrix products, arithmetic and copies ran while one was open for 0% of the time, Pallas kernels for 0%

profile of v2, /device:TPU:1, one launch (start us, length us, event | category | flops | bytes accessed | tf_op | source)
XLA Modules:
  0.0 146.7 jit_solution(11094186819970214543)
XLA Ops:
  0.7 12.2 %project_and_pick.1.in_ref = f32[64,9,128]{2,1,0:T(8,128)} custom-call(f32[59,16384]{1,0:T(8,128)} %params_ref.3, s32[64,128]{1,0:T(8,128)} %bitcast.24, s32[1]{0:T(128)} %bitcast.1.view_ref, f32[2,2]{1,0:T(2,128)} %shear_ref.3, f32[2,2]{1,0:T(2,128)} %offset_ref.3, f32[2,3]{1,0:T(2,128)} %center_ref.3), custom_call_target="tpu_custom_call" | custom-call | tf_op jit(solution)/shard_map/project_and_pick/pallas_call | solution.py:211
  12.8 18.8 %exchange.2.slots_ref = f32[64,9,128]{2,1,0:T(8,128)} custom-call(f32[64,9,128]{2,1,0:T(8,128)} %project_and_pick.1.in_ref), custom_call_target="tpu_custom_call" | custom-call | tf_op jit(solution)/shard_map/exchange/pallas_call | solution.py:286
  31.6 18.4 %render_forward.1 = (f32[128,256]{1,0:T(8,128)}, f32[32,9,256]{2,1,0:T(8,128)}, f32[32,256,256]{2,1,0:T(8,128)}, f32[32,256,256]{2,1,0:T(8,128)}) custom-call(f32[64,9,128]{2,1,0:T(8,128)} %exchange.2.slots_ref, s32[32,256]{1,0:T(8,128)} %bitcast.22, s32[1,32]{1,0:T(1,128)} %count_ref.2, s32[1]{0:T(128)} %bitcast.3.band_ref, s32[1]{0:T(128)} %bitcast.1.view_ref, ...), custom_call_target="tpu_custom_call" | custom-call | tf_op jit(solution)/shard_map/render_forward/pallas_call | solution.py:431
  50.0 0.9 slice.461
  50.9 0.3 reshape.30
  51.2 0.3 copy.18
  51.4 0.4 reshape.31
  51.9 2.4 %collective-permute-start = (f32[6,5,512]{2,1,0:T(8,128)S(1)}, f32[6,5,512]{2,1,0:T(8,128)S(1)}, u32[]{:S(2)}, u32[]{:S(2)}) collective-permute-start(f32[6,5,512]{2,1,0:T(8,128)S(1)} %get-tuple-element.37), channel_id=1, source_target_pairs={{0,1},{1,2},{2,3},{3,4},{4,5},{5,6},{6,7},{7,8},{8,9},{9,10},{10,1... | collective-permute-start | bytes 184328 | tf_op jit(solution)/shard_map/ppermute | solution.py:20
  54.3 1.3 collective-permute-start.1
  55.6 0.3 collective-permute-done
  56.0 3.7 %collective-permute-done.1 = f32[6,5,512]{2,1,0:T(8,128)S(1)} collective-permute-done((f32[6,5,512]{2,1,0:T(8,128)S(1)}, f32[6,5,512]{2,1,0:T(8,128)S(1)}, u32[]{:S(2)}, u32[]{:S(2)}) %collective-permute-start.1) | collective-permute-done | bytes 61472 | tf_op jit(solution)/shard_map/ppermute | solution.py:23
  59.8 0.1 fusion.172
  59.9 0.1 fusion.182
  60.6 1.9 %add_reduce_fusion = (f32[]{:T(128)}, f32[3,16,512]{2,1,0:T(8,128)S(1)}, f32[3,16,512]{2,1,0:T(8,128)S(1)}, f32[3,16,512]{2,1,0:T(8,128)S(1)}, f32[3,16,512]{2,1,0:T(8,128)S(1)}) fusion(f32[1,3,16,512]{3,2,1,0:T(8,128)S(1)} %copy-done, f32[3,16,512]{2,1,0:T(8,128)S(1)} %fusion.142, f32[3,16,512]{2,1,0:T(8,128)S(1)} %fusion.152, ...), kind=kLoop, calls=%fused_computation.331 | loop fusion | flops 3244031 | bytes 1081360 | tf_op jit(solution)/shard_map/reduce_sum | solution.py:792
  62.7 2.6 %collective-permute-start.2 = (f32[9,5,512]{2,1,0:T(8,128)S(1)}, f32[9,5,512]{2,1,0:T(8,128)S(1)}, u32[]{:S(2)}, u32[]{:S(2)}) collective-permute-start(f32[9,5,512]{2,1,0:T(8,128)S(1)} %get-tuple-element.32), channel_id=1, source_target_pairs={{0,1},{1,2},{2,3},{3,4},{4,5},{5,6},{6,7},{7,8},{8,9},{9,10},{10,1... | collective-permute-start | bytes 276488 | tf_op jit(solution)/shard_map/ppermute | solution.py:20
  65.3 1.5 %collective-permute-start.3 = (f32[9,5,512]{2,1,0:T(8,128)S(1)}, f32[9,5,512]{2,1,0:T(8,128)S(1)}, u32[]{:S(2)}, u32[]{:S(2)}) collective-permute-start(f32[9,5,512]{2,1,0:T(8,128)S(1)} %get-tuple-element.33), channel_id=1, source_target_pairs={{1,0},{2,1},{3,2},{4,3},{5,4},{6,5},{7,6},{8,7},{9,8},{10,9},{11,1... | collective-permute-start | bytes 276488 | tf_op jit(solution)/shard_map/ppermute | solution.py:23
  66.8 0.6 collective-permute-done.2
  67.3 3.8 %collective-permute-done.3 = f32[9,5,512]{2,1,0:T(8,128)S(1)} collective-permute-done((f32[9,5,512]{2,1,0:T(8,128)S(1)}, f32[9,5,512]{2,1,0:T(8,128)S(1)}, u32[]{:S(2)}, u32[]{:S(2)}) %collective-permute-start.3) | collective-permute-done | bytes 92192 | tf_op jit(solution)/shard_map/ppermute | solution.py:23
  71.3 0.4 fusion.20
  71.7 0.8 fusion.10
  72.5 0.1 fusion.140
  72.6 0.3 reshape.32
  72.9 0.3 copy.19
  73.2 0.8 copy.20.grad_ref
  74.0 1.2 broadcast_in_dim.8.loss_ref
  75.1 17.1 %render_backward.1.in_ref = f32[64,10,128]{2,1,0:T(8,128)} custom-call(f32[32,9,256]{2,1,0:T(8,128)} %get-tuple-element.12.entry_ref, f32[32,256,256]{2,1,0:T(8,128)} %get-tuple-element.13.cover_ref, f32[32,256,256]{2,1,0:T(8,128)} %get-tuple-element.14.keep_ref, f32[3,32,256]{2,1,0:T(8,128)} %copy.20.grad_ref, s32[32,256]{1,0:T(8,128)} %bitcast.23, ...), custom_call_target="tpu_custom_call" | custom-call | tf_op jit(solution)/shard_map/render_backward/pallas_call | solution.py:580
  92.2 23.8 %exchange.3.returned_ref = f32[64,10,128]{2,1,0:T(8,128)} custom-call(f32[64,10,128]{2,1,0:T(8,128)} %render_backward.1.in_ref), custom_call_target="tpu_custom_call" | custom-call | tf_op jit(solution)/shard_map/exchange/pallas_call | solution.py:286
  116.0 8.5 %place_gradients.1.own_ref = f32[10,128,128]{2,1,0:T(8,128)} custom-call(f32[64,10,128]{2,1,0:T(8,128)} %exchange.3.returned_ref, s32[64,128]{1,0:T(8,128)} %bitcast.25, s32[1,64]{1,0:T(1,128)} %count_ref.3), custom_call_target="tpu_custom_call" | custom-call | tf_op jit(solution)/shard_map/place_gradients/pallas_call | solution.py:635
  124.6 6.5 %collective-permute-start.4 = (f32[10,128,128]{2,1,0:T(8,128)}, f32[10,128,128]{2,1,0:T(8,128)S(1)}, u32[]{:S(2)}, u32[]{:S(2)}) collective-permute-start(f32[10,128,128]{2,1,0:T(8,128)} %place_gradients.1.own_ref), channel_id=1, source_target_pairs={{0,64},{64,0},{1,65},{65,1},{2,66},{66,2},{3,67},{67,3},{4,68},{68... | collective-permute-start | bytes 1966088 | tf_op jit(solution)/shard_map/ppermute | solution.py:804
  131.0 1.9 %collective-permute-done.4.other_ref = f32[10,128,128]{2,1,0:T(8,128)S(1)} collective-permute-done((f32[10,128,128]{2,1,0:T(8,128)}, f32[10,128,128]{2,1,0:T(8,128)S(1)}, u32[]{:S(2)}, u32[]{:S(2)}) %collective-permute-start.4) | collective-permute-done | bytes 655392 | tf_op jit(solution)/shard_map/ppermute | solution.py:804
  133.0 0.8 copy-done.1
  133.8 12.8 %update.1 = (f32[59,16384]{1,0:T(8,128)}, f32[59,16384]{1,0:T(8,128)}, f32[59,16384]{1,0:T(8,128)}, f32[1,1]{1,0:T(1,128)}) custom-call(f32[59,16384]{1,0:T(8,128)} %params_ref.3, f32[59,16384]{1,0:T(8,128)} %first_ref.1, f32[59,16384]{1,0:T(8,128)} %second_ref.1, f32[10,128,128]{2,1,0:T(8,128)} %place_gradients.1.own_ref, f32[10,128,128]{2,1,0:T(8,128)} %copy-done.1, ...), custom_call_target="tpu_custom_call" | custom-call | tf_op jit(solution)/shard_map/update/pallas_call | solution.py:701
  (18 shorter events, 0.9 us)
Async XLA Ops:
  0.6 31.0 %copy-start.2 = (f32[2,3]{1,0:T(2,128)S(1)}, f32[2,3]{1,0:T(2,128)}, u32[]{:S(2)}) copy-start(f32[2,3]{1,0:T(2,128)} %back_ref.1) | copy-start | bytes 76
  0.6 51.3 %copy-start = (f32[1,3,16,512]{3,2,1,0:T(8,128)S(1)}, f32[1,3,16,512]{3,2,1,0:T(8,128)}, u32[]{:S(2)}) copy-start(f32[1,3,16,512]{3,2,1,0:T(8,128)} %param.15) | copy-start | bytes 294916
  51.9 4.0 %collective-permute-start = (f32[6,5,512]{2,1,0:T(8,128)S(1)}, f32[6,5,512]{2,1,0:T(8,128)S(1)}, u32[]{:S(2)}, u32[]{:S(2)}) collective-permute-start(f32[6,5,512]{2,1,0:T(8,128)S(1)} %get-tuple-element.37), channel_id=1, source_target_pairs={{0,1},{1,2},{2,3},{3,4},{4,5},{5,6},{6,7},{7,8},{8,9},{9,10},{10,1... | collective-permute-start | bytes 184328 | tf_op jit(solution)/shard_map/ppermute | solution.py:20
  54.3 5.4 %collective-permute-start.1 = (f32[6,5,512]{2,1,0:T(8,128)S(1)}, f32[6,5,512]{2,1,0:T(8,128)S(1)}, u32[]{:S(2)}, u32[]{:S(2)}) collective-permute-start(f32[6,5,512]{2,1,0:T(8,128)S(1)} %get-tuple-element.38), channel_id=1, source_target_pairs={{1,0},{2,1},{3,2},{4,3},{5,4},{6,5},{7,6},{8,7},{9,8},{10,9},{11,1... | collective-permute-start | bytes 184328 | tf_op jit(solution)/shard_map/ppermute | solution.py:23
  62.7 4.7 %collective-permute-start.2 = (f32[9,5,512]{2,1,0:T(8,128)S(1)}, f32[9,5,512]{2,1,0:T(8,128)S(1)}, u32[]{:S(2)}, u32[]{:S(2)}) collective-permute-start(f32[9,5,512]{2,1,0:T(8,128)S(1)} %get-tuple-element.32), channel_id=1, source_target_pairs={{0,1},{1,2},{2,3},{3,4},{4,5},{5,6},{6,7},{7,8},{8,9},{9,10},{10,1... | collective-permute-start | bytes 276488 | tf_op jit(solution)/shard_map/ppermute | solution.py:20
  65.3 5.9 %collective-permute-start.3 = (f32[9,5,512]{2,1,0:T(8,128)S(1)}, f32[9,5,512]{2,1,0:T(8,128)S(1)}, u32[]{:S(2)}, u32[]{:S(2)}) collective-permute-start(f32[9,5,512]{2,1,0:T(8,128)S(1)} %get-tuple-element.33), channel_id=1, source_target_pairs={{1,0},{2,1},{3,2},{4,3},{5,4},{6,5},{7,6},{8,7},{9,8},{10,9},{11,1... | collective-permute-start | bytes 276488 | tf_op jit(solution)/shard_map/ppermute | solution.py:23
  124.6 8.4 %collective-permute-start.4 = (f32[10,128,128]{2,1,0:T(8,128)}, f32[10,128,128]{2,1,0:T(8,128)S(1)}, u32[]{:S(2)}, u32[]{:S(2)}) collective-permute-start(f32[10,128,128]{2,1,0:T(8,128)} %place_gradients.1.own_ref), channel_id=1, source_target_pairs={{0,64},{64,0},{1,65},{65,1},{2,66},{66,2},{3,67},{67,3},{4,68},{68... | collective-permute-start | bytes 1966088 | tf_op jit(solution)/shard_map/ppermute | solution.py:804
  133.0 0.9 copy-start.1

commit v3 on v2

--- a/solution.py
+++ b/solution.py
@@ -10,19 +10,6 @@
 
 STEP_COUNT = 20
 LIST = 256
-
-
-def extended(block, sides, width):
-    for axis, dim in sides:
-        count = lax.axis_size(axis)
-        forward = [(i, i + 1) for i in range(count - 1)]
-        backward = [(target, source) for source, target in forward]
-        low = lax.ppermute(
-            lax.slice_in_dim(block, block.shape[dim] - width, None, axis=dim), axis, forward
-        )
-        high = lax.ppermute(lax.slice_in_dim(block, 0, width, axis=dim), axis, backward)
-        block = jnp.concatenate([low, block, high], axis=dim)
-    return block
 
 
 def window_taps():
@@ -165,10 +152,97 @@
     return rows
 
 
+def axis_peers(me, stride):
+    place = lax.rem(me // stride, 4)
+    return [me + (lax.rem(place + j, 4) - place) * stride for j in range(1, 4)]
+
+
+def signal_all(semaphore, peers):
+    for peer in peers:
+        pl.semaphore_signal(semaphore, inc=1, device_id={"tile": peer}, device_id_type=MESH)
+
+
+def greet_all(step, semaphores):
+    plane_sem, cube_sem = semaphores
+    me = lax.axis_index("tile")
+    lines = [axis_peers(me, stride) for stride in (1, 4, 16)]
+    barrier = pltpu.get_barrier_semaphore()
+
+    @pl.when(step == 0)
+    def _():
+        for line in lines:
+            signal_all(barrier, line)
+
+    @pl.when(step == 1)
+    def _():
+        pl.semaphore_wait(barrier, 9)
+        signal_all(plane_sem, lines[1])
+
+    @pl.when(step == 2)
+    def _():
+        pl.semaphore_wait(plane_sem, 3)
+        signal_all(cube_sem, lines[2])
+
+    @pl.when(step == 3)
+    def _():
+        pl.semaphore_wait(cube_sem, 3)
+
+
+def block_copy(outgoing, incoming, send_sem, recv_sem, peer):
+    me = lax.axis_index("tile")
+    return pltpu.make_async_remote_copy(
+        src_ref=outgoing.at[peer],
+        dst_ref=incoming.at[me],
+        send_sem=send_sem.at[peer],
+        recv_sem=recv_sem.at[me],
+        device_id={"tile": peer},
+        device_id_type=MESH,
+    )
+
+
+def send_block(outgoing, incoming, send_sem, recv_sem, peer):
+    @pl.when(peer != lax.axis_index("tile"))
+    def _():
+        block_copy(outgoing, incoming, send_sem, recv_sem, peer).start()
+
+
+def finish_blocks(outgoing, incoming, send_sem, recv_sem):
+    me = lax.axis_index("tile")
+    incoming[me] = outgoing[me]
+
+    def finish(p, carry):
+        peer = lax.rem(me + p, 64)
+        block_copy(outgoing, incoming, send_sem, recv_sem, peer).wait_send()
+        pltpu.make_async_remote_copy(
+            src_ref=outgoing.at[peer],
+            dst_ref=incoming.at[peer],
+            send_sem=send_sem.at[peer],
+            recv_sem=recv_sem.at[peer],
+            device_id={"tile": peer},
+            device_id_type=MESH,
+        ).wait_recv()
+        return carry
+
+    lax.fori_loop(1, 64, finish, 0)
+
+
+def exchange_scratch(rows):
+    return [
+        pltpu.VMEM((64, rows, 128), jnp.float32),
+        pltpu.VMEM((64, rows, 128), jnp.float32),
+        pltpu.SemaphoreType.DMA((64,)),
+        pltpu.SemaphoreType.DMA((64,)),
+        pltpu.SemaphoreType.REGULAR,
+        pltpu.SemaphoreType.REGULAR,
+    ]
+
+
 def project_kernel(
-    params_ref, index_ref, view_ref, shear_ref, offset_ref, center_ref, out_ref, table, high_parts, low_parts
+    params_ref, index_ref, view_ref, shear_ref, offset_ref, center_ref, out_ref,
+    table, high_parts, low_parts, outgoing, incoming, send_sem, recv_sem, *greetings,
 ):
     step = pl.program_id(0)
+    greet_all(step, greetings)
     camera = camera_of((shear_ref, offset_ref, center_ref), view_ref[0])
 
     def part(sub, carry):
@@ -199,11 +273,27 @@
             low = (index & 127) + ((index >> 13) << 7)
             rows = pick_rows(high_parts, low_parts, one_hot(low_ids, low), high_ids == high)
             for q in range(9):
-                out_ref[pair, q : q + 1, :] = rows[q][:, 0:128]
-                out_ref[pair + 32, q : q + 1, :] = rows[q][:, 128:256]
+                outgoing[pair, q : q + 1, :] = rows[q][:, 0:128]
+                outgoing[pair + 32, q : q + 1, :] = rows[q][:, 128:256]
             return carry
 
-        lax.fori_loop(0, 32, pick, 0, unroll=4)
+        me = lax.axis_index("tile")
+
+        def group(part, carry):
+            first = lax.rem(part + me, 4) * 8
+            lax.fori_loop(0, 8, lambda k, carry: pick(first + k, carry), 0, unroll=4)
+
+            def send(k, carry):
+                for peer in (first + k, first + k + 32):
+                    send_block(outgoing, incoming, send_sem, recv_sem, peer)
+                return carry
+
+            lax.fori_loop(0, 8, send, 0)
+            return carry
+
+        lax.fori_loop(0, 4, group, 0)
+        finish_blocks(outgoing, incoming, send_sem, recv_sem)
+        out_ref[...] = incoming[...]
 
 
 def project_and_pick(params, send_index, view, shear, offset, center):
@@ -225,81 +315,63 @@
             pltpu.VMEM((9, 128, 128), jnp.float32),
             pltpu.VMEM((576, 512), jnp.bfloat16),
             pltpu.VMEM((128, 256), jnp.bfloat16),
+            *exchange_scratch(9),
         ],
-        compiler_params=pltpu.CompilerParams(vmem_limit_bytes=VMEM_LIMIT),
+        compiler_params=pltpu.CompilerParams(
+            collective_id=0, has_side_effects=True, vmem_limit_bytes=VMEM_LIMIT
+        ),
         name="project_and_pick",
     )(params, send_index, view, shear, offset, center)
 
 
-def axis_peers(me, stride):
-    place = lax.rem(me // stride, 4)
-    return [me + (lax.rem(place + j, 4) - place) * stride for j in range(1, 4)]
-
-
-def signal_all(semaphore, peers):
-    for peer in peers:
-        pl.semaphore_signal(semaphore, inc=1, device_id={"tile": peer}, device_id_type=MESH)
-
-
-def exchange_kernel(in_ref, out_ref, send_sem, recv_sem, local_sem, plane_sem, cube_sem):
+def halo_kernel(planes_ref, low_ref, high_ref, low_send, high_send, send_sem, recv_sem):
     total = lax.axis_size("tile")
     me = lax.axis_index("tile")
+    following, previous = lax.rem(me + 1, total), lax.rem(me + total - 1, total)
     barrier = pltpu.get_barrier_semaphore()
-    lines = [axis_peers(me, stride) for stride in (1, 4, 16)]
-    for line in lines:
-        signal_all(barrier, line)
-    own = pltpu.make_async_copy(in_ref.at[me], out_ref.at[me], local_sem)
-    own.start()
-    pl.semaphore_wait(barrier, 9)
-    signal_all(plane_sem, lines[1])
-    pl.semaphore_wait(plane_sem, 3)
-    signal_all(cube_sem, lines[2])
-    pl.semaphore_wait(cube_sem, 3)
-
-    def copy_to(p):
-        peer = lax.rem(me + p, total)
-        return pltpu.make_async_remote_copy(
-            src_ref=in_ref.at[peer],
-            dst_ref=out_ref.at[me],
-            send_sem=send_sem.at[p],
-            recv_sem=recv_sem.at[p],
+    signal_all(barrier, (following, previous))
+    low_send[...] = planes_ref[:, 6:16, :]
+    high_send[...] = planes_ref[:, 0:10, :]
+    pl.semaphore_wait(barrier, 2)
+    copies = [
+        pltpu.make_async_remote_copy(
+            src_ref=source,
+            dst_ref=target,
+            send_sem=send_sem.at[k],
+            recv_sem=recv_sem.at[k],
             device_id={"tile": peer},
             device_id_type=MESH,
         )
-
-    def send(p, carry):
-        copy_to(p).start()
-        return carry
-
-    def finish(p, carry):
-        copy_to(p).wait()
-        return carry
-
-    lax.fori_loop(1, total, send, 0)
-    own.wait()
-    lax.fori_loop(1, total, finish, 0)
-
-
-def exchange(blocks, collective_id):
+        for k, (source, target, peer) in enumerate(
+            ((low_send, low_ref, following), (high_send, high_ref, previous))
+        )
+    ]
+    for copy in copies:
+        copy.start()
+    for copy in copies:
+        copy.wait()
+
+
+def halo_rows(planes):
     vmem = pl.BlockSpec(memory_space=pltpu.VMEM)
-    total = blocks.shape[0]
+    part = (planes.shape[0], 10, planes.shape[2])
+    shape = jax.ShapeDtypeStruct(part, jnp.float32)
     return pl.pallas_call(
-        exchange_kernel,
-        out_shape=jax.ShapeDtypeStruct(blocks.shape, blocks.dtype),
+        halo_kernel,
+        out_shape=(shape, shape),
         in_specs=[vmem],
-        out_specs=vmem,
+        out_specs=(vmem, vmem),
         scratch_shapes=[
-            pltpu.SemaphoreType.DMA((total,)),
-            pltpu.SemaphoreType.DMA((total,)),
-            pltpu.SemaphoreType.DMA,
-            pltpu.SemaphoreType.REGULAR,
-            pltpu.SemaphoreType.REGULAR,
+            pltpu.VMEM(part, jnp.float32),
+            pltpu.VMEM(part, jnp.float32),
+            pltpu.SemaphoreType.DMA((2,)),
+            pltpu.SemaphoreType.DMA((2,)),
         ],
         compiler_params=pltpu.CompilerParams(
-            collective_id=collective_id, has_side_effects=True, vmem_limit_bytes=VMEM_LIMIT
+            collective_id=2, has_side_effects=True, vmem_limit_bytes=VMEM_LIMIT
         ),
-        name="exchange",
-    )(blocks)
+        name="halo_rows",
+    )(planes)
 
 
 TILES_STEP = 8
@@ -465,9 +537,10 @@
 
 def backward_kernel(
     entry_ref, cover_ref, keep_ref, grad_ref, list_ref, band_ref, loss_ref, out_ref,
-    after, total, results, high_weights, low_weights,
+    after, total, results, high_weights, low_weights, outgoing, incoming, send_sem, recv_sem, *greetings,
 ):
     step = pl.program_id(0)
+    greet_all(step, greetings)
 
     @pl.when(step == 0)
     def _():
@@ -556,10 +629,19 @@
         lax.fori_loop(0, 32, place, 0, unroll=4)
         for q in range(9):
             for half in range(2):
-                out_ref[32 * half : 32 * half + 32, q, :] = total[
+                outgoing[32 * half : 32 * half + 32, q, :] = total[
                     32 * q : 32 * q + 32, 128 * half : 128 * half + 128
                 ]
-        out_ref[:, 9, :] = jnp.broadcast_to(loss_ref[...], (64, 128))
+        outgoing[:, 9, :] = jnp.broadcast_to(loss_ref[...], (64, 128))
+        me = lax.axis_index("tile")
+
+        def send(p, carry):
+            block_copy(outgoing, incoming, send_sem, recv_sem, lax.rem(me + p, 64)).start()
+            return carry
+
+        lax.fori_loop(1, 64, send, 0)
+        finish_blocks(outgoing, incoming, send_sem, recv_sem)
+        out_ref[...] = incoming[...]
 
 
 def place_rows(rows, total, hot, mask):
@@ -597,8 +679,11 @@
             pltpu.VMEM((32, 9, 256), jnp.float32),
             pltpu.VMEM((2, 256, 256), jnp.bfloat16),
             pltpu.VMEM((2, 256, 256), jnp.bfloat16),
+            *exchange_scratch(10),
         ],
-        compiler_params=pltpu.CompilerParams(vmem_limit_bytes=VMEM_LIMIT),
+        compiler_params=pltpu.CompilerParams(
+            collective_id=1, has_side_effects=True, vmem_limit_bytes=VMEM_LIMIT
+        ),
         name="render_backward",
     )(entries, cover, keep, grads, lists, band, loss)
 def place_kernel(returned_ref, index_ref, count_ref, out_ref, total):
@@ -763,8 +848,7 @@
     view = view_index.astype(jnp.int32).reshape(1)
     band = band_index.astype(jnp.int32).reshape(1)
     backdrop = lax.dynamic_index_in_dim(background, view_index, 0, keepdims=False)
-    outgoing = project_and_pick(params, send_index[0], view, view_shear, view_offset, cam_center)
-    incoming = exchange(outgoing, 0)
+    incoming = project_and_pick(params, send_index[0], view, view_shear, view_offset, cam_center)
     shown, entries, cover, keep = render_forward(
         incoming, tile_list[0, 0], tile_count, band, view, background
     )
@@ -772,7 +856,11 @@
     image_band = image_band + backdrop[:, None, None]
     frame_band = target[0]
     stacked = jnp.concatenate([image_band, frame_band], axis=0)
-    widened = extended(stacked, (("tile", 1),), 5)
+    low, high = halo_rows(stacked)
+    last_band = lax.axis_size("tile") - 1
+    low = jnp.where(band_index > 0, low, 0.0)
+    high = jnp.where(band_index < last_band, high, 0.0)
+    widened = jnp.concatenate([low, stacked, high], axis=1)
     mean_x, mean_y, power_x, power_y, cross_xy = window_stats(widened)
     similarity, ssim_back = jax.vjp(
         lambda level_x, energy_x, product_xy: ssim_map(
@@ -782,10 +870,11 @@
         power_x,
         cross_xy,
     )
-    grad_mean, grad_power, grad_cross = ssim_back(jnp.full_like(similarity, -0.8))
-    spread = extended(
-        jnp.concatenate([grad_mean, grad_power, grad_cross], axis=0), (("tile", 1),), 5
-    )
+    rows = jnp.arange(26, dtype=jnp.int32) - 5 + 16 * band_index
+    inside = (rows >= 0) & (rows < 16 * (last_band + 1))
+    seed = jnp.where(inside, -0.8, 0.0)[None, :, None]
+    spread = jnp.concatenate(ssim_back(jnp.broadcast_to(seed, similarity.shape)), axis=0)
+    similarity = similarity[:, 5:21]
     blurred = gaussian_blur(spread)
     difference = image_band - frame_band
     smooth = jnp.sqrt(difference * difference + 0.0001)
@@ -798,8 +887,7 @@
     )
     grad_tiles = pixel_grad.reshape(3, 16, 32, 16).transpose(0, 2, 1, 3).reshape(3, 32, 256)
     loss_row = jnp.broadcast_to(loss_part, (1, 128))
-    slot_grad = render_backward(entries, cover, keep, grad_tiles, tile_list[0, 0], band, loss_row)
-    returned = exchange(slot_grad, 1)
+    returned = render_backward(entries, cover, keep, grad_tiles, tile_list[0, 0], band, loss_row)
     own_grad = place_gradients(returned, send_index[0], send_count)
     other_grad = lax.ppermute(own_grad, "view", [(0, 1), (1, 0)])
     new_params, new_first, new_second, mean_loss = update(

time: 147 us -> 124 us (0.84)
  starting transfers between devices: 14.2 us -> 4.17 us
  Pallas kernels: 112 us -> 103 us
  waiting for transfers between devices: 10.4 us -> 1.93 us
  other arithmetic: 4.45 us -> 8.02 us
    pallas_call x2 -> x1, Pallas kernels: 42.6 us -> 11.7 us  [halo_rows(): pl.pallas_call(halo_kernel, out_shape=(shape, shape), in_specs=[vmem], ou...]
    pallas_call x1, Pallas kernels: 12.2 us -> 25.6 us  [project_and_pick(): pl.pallas_call(project_kernel, grid=(16384 // BLOCK,), out_shape=jax.Shap...]
    pallas_call x1, Pallas kernels: 17.1 us -> 26.3 us  [render_backward(): pl.pallas_call(backward_kernel, grid=(32 // TILES_STEP,), out_shape=jax.S...]
    ppermute x4 -> x0, waiting for transfers between devices: 8.47 us -> none  [the longest x2 7.55 us: extended(): lax.ppermute(lax.slice_in_dim(block, 0, width, axis=dim), axis, backward)]
    ppermute x4 -> x0, starting transfers between devices: 7.72 us -> none  [the longest x2 4.96 us: extended(): lax.ppermute(lax.slice_in_dim(block, block.shape[dim] - width, None, axis...]
    mul x0 -> x2, other arithmetic: none -> 2.67 us  [the longest x1 1.59 us: ssim_map(): (2.0 * level_x * level_y + 0.0001) * (2.0 * (product_xy - level_x * level...]
    ppermute x1, starting transfers between devices: 6.46 us -> 4.17 us  [shards(): other_grad = lax.ppermute(own_grad, 'view', [(0, 1), (1, 0)])]
  transfers between devices with their start and end apart: 5 -> 1, of which waited for: 5 -> 1; matrix products, arithmetic and copies ran while one was open for 0% -> 0% of each run, Pallas kernels for 0% -> 0%
where the time goes in v3:
time: 124 us
  Pallas kernels  103 us (83%)
  other arithmetic  8.02 us (6%)
  local copies, waits for them, and re-layouts  5.85 us (5%)
  starting transfers between devices  4.17 us (3%)
  waiting for transfers between devices  1.93 us (2%)
    pallas_call x1, Pallas kernels, render_backward(): pl.pallas_call(backward_kernel, grid=(32 // TILES_STEP,), out_shape=jax.S...  26.3 us
    pallas_call x1, Pallas kernels, project_and_pick(): pl.pallas_call(project_kernel, grid=(16384 // BLOCK,), out_shape=jax.Shap...  25.6 us
    pallas_call x1, Pallas kernels, render_forward(): pl.pallas_call(forward_kernel, grid=(32 // TILES_STEP,), out_shape=(jax.S...  18.4 us
    pallas_call x1, Pallas kernels, update(): pl.pallas_call(update_kernel, grid=(16384 // BLOCK,), out_shape=(shape, s...  12.8 us
    pallas_call x1, Pallas kernels, halo_rows(): pl.pallas_call(halo_kernel, out_shape=(shape, shape), in_specs=[vmem], ou...  11.7 us
    pallas_call x1, Pallas kernels, place_gradients(): pl.pallas_call(place_kernel, out_shape=jax.ShapeDtypeStruct((10, 128, 128...  8.54 us
    ppermute x1, starting transfers between devices, shards(): other_grad = lax.ppermute(own_grad, 'view', [(0, 1), (1, 0)])  4.17 us
  transfers between devices with their start and end apart: 1, of which 1 were waited for; matrix products, arithmetic and copies ran while one was open for 0% of the time, Pallas kernels for 0%

profile of v3, /device:TPU:1, one launch (start us, length us, event | category | flops | bytes accessed | tf_op | source)
XLA Modules:
  0.0 124.1 jit_solution(12129435075852728251)
XLA Ops:
  0.6 0.7 dynamic-slice_bitcast_fusion
  1.3 25.6 %project_and_pick.1.slots_ref = f32[64,9,128]{2,1,0:T(8,128)} custom-call(f32[59,16384]{1,0:T(8,128)} %params_ref.3, s32[64,128]{1,0:T(8,128)} %bitcast.23, s32[1]{0:T(128)} %bitcast.1.view_ref, f32[2,2]{1,0:T(2,128)} %shear_ref.3, f32[2,2]{1,0:T(2,128)} %offset_ref.3, f32[2,3]{1,0:T(2,128)} %center_ref.3), custom_call_target="tpu_custom_call" | custom-call | tf_op jit(solution)/shard_map/project_and_pick/pallas_call | solution.py:301
  26.9 18.4 %render_forward.1 = (f32[128,256]{1,0:T(8,128)}, f32[32,9,256]{2,1,0:T(8,128)}, f32[32,256,256]{2,1,0:T(8,128)}, f32[32,256,256]{2,1,0:T(8,128)}) custom-call(f32[64,9,128]{2,1,0:T(8,128)} %project_and_pick.1.slots_ref, s32[32,256]{1,0:T(8,128)} %bitcast.21, s32[1,32]{1,0:T(1,128)} %count_ref.2, s32[1]{0:T(128)} %bitcast.3.band_ref, s32[1]{0:T(128)} %bitcast.1.view_ref, ...), custom_call_target="tpu_custom_call" | custom-call | tf_op jit(solution)/shard_map/render_forward/pallas_call | solution.py:503
  45.3 0.9 slice.431
  46.2 0.3 reshape.39
  46.5 0.3 copy.18
  46.7 0.4 reshape.40
  47.2 0.7 pad_maximum_fusion.3.planes_ref
  47.9 11.7 %halo_rows.1 = (f32[6,10,512]{2,1,0:T(8,128)}, f32[6,10,512]{2,1,0:T(8,128)}) custom-call(f32[6,16,512]{2,1,0:T(8,128)} %pad_maximum_fusion.3.planes_ref), custom_call_target="tpu_custom_call" | custom-call | tf_op jit(solution)/shard_map/halo_rows/pallas_call | solution.py:359
  59.6 1.0 broadcast_select_fusion
  60.6 0.1 maximum_maximum_fusion
  60.7 0.2 fusion.169
  61.0 0.2 fusion.179
  61.3 0.2 fusion.159
  61.5 0.2 fusion.139
  61.8 0.2 fusion.149
  62.0 1.6 %fusion.195 = (f32[3,26,512]{2,1,0:T(8,128)S(1)}, f32[3,26,512]{2,1,0:T(8,128)S(1)}, f32[3,26,512]{2,1,0:T(8,128)S(1)}, f32[3,26,512]{2,1,0:T(8,128)S(1)}) fusion(f32[3,26,512]{2,1,0:T(8,128)S(1)} %fusion.139, f32[3,26,512]{2,1,0:T(8,128)S(1)} %fusion.179, f32[3,26,512]{2,1,0:T(8,128)S(1)} %fusion.169), kind=kLoop, calls=%fused_computation.338 | loop fusion | flops 2835456 | bytes 1118208 | tf_op jit(solution)/shard_map/jvp()/mul | solution.py:813
  63.6 1.1 fusion.196
  64.7 0.3 fusion.31
  65.0 0.4 fusion.20
  65.4 0.8 fusion.10
  66.2 0.7 fusion.197
  66.9 0.3 reshape.41
  67.2 0.3 copy.19
  67.5 0.8 copy.20.grad_ref
  68.3 1.2 broadcast_in_dim.31.loss_ref
  69.4 26.3 %render_backward.1.returned_ref = f32[64,10,128]{2,1,0:T(8,128)} custom-call(f32[32,9,256]{2,1,0:T(8,128)} %get-tuple-element.14.entry_ref, f32[32,256,256]{2,1,0:T(8,128)} %get-tuple-element.15.cover_ref, f32[32,256,256]{2,1,0:T(8,128)} %get-tuple-element.16.keep_ref, f32[3,32,256]{2,1,0:T(8,128)} %copy.20.grad_ref, s32[32,256]{1,0:T(8,128)} %bitcast.22, ...), custom_call_target="tpu_custom_call" | custom-call | tf_op jit(solution)/shard_map/render_backward/pallas_call | solution.py:662
  95.7 8.5 %place_gradients.1.own_ref = f32[10,128,128]{2,1,0:T(8,128)} custom-call(f32[64,10,128]{2,1,0:T(8,128)} %render_backward.1.returned_ref, s32[64,128]{1,0:T(8,128)} %bitcast.24, s32[1,64]{1,0:T(1,128)} %count_ref.3), custom_call_target="tpu_custom_call" | custom-call | tf_op jit(solution)/shard_map/place_gradients/pallas_call | solution.py:720
  104.3 4.2 %collective-permute-start = (f32[10,128,128]{2,1,0:T(8,128)}, f32[10,128,128]{2,1,0:T(8,128)S(1)}, u32[]{:S(2)}, u32[]{:S(2)}) collective-permute-start(f32[10,128,128]{2,1,0:T(8,128)} %place_gradients.1.own_ref), channel_id=1, source_target_pairs={{0,64},{64,0},{1,65},{65,1},{2,66},{66,2},{3,67},{67,3},{4,68},{68... | collective-permute-start | bytes 1966088 | tf_op jit(solution)/shard_map/ppermute | solution.py:892
  108.5 1.9 %collective-permute-done.other_ref = f32[10,128,128]{2,1,0:T(8,128)S(1)} collective-permute-done((f32[10,128,128]{2,1,0:T(8,128)}, f32[10,128,128]{2,1,0:T(8,128)S(1)}, u32[]{:S(2)}, u32[]{:S(2)}) %collective-permute-start) | collective-permute-done | bytes 655392 | tf_op jit(solution)/shard_map/ppermute | solution.py:892
  110.4 0.9 copy-done.1
  111.3 12.8 %update.1 = (f32[59,16384]{1,0:T(8,128)}, f32[59,16384]{1,0:T(8,128)}, f32[59,16384]{1,0:T(8,128)}, f32[1,1]{1,0:T(1,128)}) custom-call(f32[59,16384]{1,0:T(8,128)} %params_ref.3, f32[59,16384]{1,0:T(8,128)} %first_ref.1, f32[59,16384]{1,0:T(8,128)} %second_ref.1, f32[10,128,128]{2,1,0:T(8,128)} %place_gradients.1.own_ref, f32[10,128,128]{2,1,0:T(8,128)} %copy-done.1, ...), custom_call_target="tpu_custom_call" | custom-call | tf_op jit(solution)/shard_map/update/pallas_call | solution.py:786
  (8 shorter events, 0.3 us)
Async XLA Ops:
  1.3 45.9 %copy-start = (f32[1,3,16,512]{3,2,1,0:T(8,128)S(1)}, f32[1,3,16,512]{3,2,1,0:T(8,128)}, u32[]{:S(2)}) copy-start(f32[1,3,16,512]{3,2,1,0:T(8,128)} %param.15) | copy-start | bytes 294916
  104.3 6.1 %collective-permute-start = (f32[10,128,128]{2,1,0:T(8,128)}, f32[10,128,128]{2,1,0:T(8,128)S(1)}, u32[]{:S(2)}, u32[]{:S(2)}) collective-permute-start(f32[10,128,128]{2,1,0:T(8,128)} %place_gradients.1.own_ref), channel_id=1, source_target_pairs={{0,64},{64,0},{1,65},{65,1},{2,66},{66,2},{3,67},{67,3},{4,68},{68... | collective-permute-start | bytes 1966088 | tf_op jit(solution)/shard_map/ppermute | solution.py:892
  110.4 0.9 copy-start.1

commit v4 on v3

v4 whole, which is shorter than its diff:
```python
import functools
import math

import jax
import jax.numpy as jnp
from jax import lax
from jax.experimental import pallas as pl
from jax.experimental.pallas import tpu as pltpu
from jax.sharding import PartitionSpec as P

STEP_COUNT = 20
LIST = 256


def window_taps():
    raw_taps = [math.exp(-(position - 5) * (position - 5) / 4.5) for position in range(11)]
    return [element / sum(raw_taps) for element in raw_taps]


def harmonics(unit_x, unit_y, unit_z):
    square_x = unit_x * unit_x
    square_y = unit_y * unit_y
    square_z = unit_z * unit_z
    return [
        0.28209479177387814 * jnp.ones_like(unit_x),
        -0.4886025119029199 * unit_y,
        0.4886025119029199 * unit_z,
        -0.4886025119029199 * unit_x,
        1.0925484305920792 * unit_x * unit_y,
        -1.0925484305920792 * unit_y * unit_z,
        0.31539156525252005 * (2.0 * square_z - square_x - square_y),
        -1.0925484305920792 * unit_x * unit_z,
        0.5462742152960396 * (square_x - square_y),
        -0.5900435899266435 * unit_y * (3.0 * square_x - square_y),
        2.890611442640554 * unit_x * unit_y * unit_z,
        -0.4570457994644658 * unit_y * (4.0 * square_z - square_x - square_y),
        0.3731763325901154 * unit_z * (2.0 * square_z - 3.0 * square_x - 3.0 * square_y),
        -0.4570457994644658 * unit_x * (4.0 * square_z - square_x - square_y),
        1.445305721320277 * unit_z * (square_x - square_y),
        -0.5900435899266435 * unit_x * (square_x - 3.0 * square_y),
    ]


def ssim_map(level_x, level_y, energy_x, energy_y, product_xy):
    upper = (2.0 * level_x * level_y + 0.0001) * (2.0 * (product_xy - level_x * level_y) + 0.0009)
    lower = (level_x * level_x + level_y * level_y + 0.0001) * (
        energy_x - level_x * level_x + (energy_y - level_y * level_y) + 0.0009
    )
    return upper / lower


MESH = pl.DeviceIdType.MESH
VMEM_LIMIT = 56 * 1024 * 1024
NN = (((1,), (0,)), ((), ()))
NT = (((1,), (1,)), ((), ()))
TN = (((0,), (0,)), ((), ()))


def mxu(left, right, dims):
    return lax.dot_general(left, right, dims, preferred_element_type=jnp.float32)


def split2(value):
    high = value.astype(jnp.bfloat16)
    low = (value - high.astype(jnp.float32)).astype(jnp.bfloat16)
    return high, low


def split3(value):
    high = value.astype(jnp.bfloat16)
    rest = value - high.astype(jnp.float32)
    middle = rest.astype(jnp.bfloat16)
    low = (rest - middle.astype(jnp.float32)).astype(jnp.bfloat16)
    return high, middle, low


def project_rows(rows, cameras):
    pos_x, pos_y, pos_z = rows[0:3]
    scales = [jnp.exp(row) for row in rows[3:6]]
    quat_w, quat_x, quat_y, quat_z = rows[6:10]
    norm = 1.0 / jnp.sqrt(
        quat_w * quat_w + quat_x * quat_x + quat_y * quat_y + quat_z * quat_z
    )
    quat_w, quat_x, quat_y, quat_z = quat_w * norm, quat_x * norm, quat_y * norm, quat_z * norm
    rotation = [
        [
            1.0 - 2.0 * (quat_y * quat_y + quat_z * quat_z),
            2.0 * (quat_x * quat_y - quat_w * quat_z),
            2.0 * (quat_x * quat_z + quat_w * quat_y),
        ],
        [
            2.0 * (quat_x * quat_y + quat_w * quat_z),
            1.0 - 2.0 * (quat_x * quat_x + quat_z * quat_z),
            2.0 * (quat_y * quat_z - quat_w * quat_x),
        ],
        [
            2.0 * (quat_x * quat_z - quat_w * quat_y),
            2.0 * (quat_y * quat_z + quat_w * quat_x),
            1.0 - 2.0 * (quat_x * quat_x + quat_y * quat_y),
        ],
    ]
    opacity = 1.0 / (1.0 + jnp.exp(-rows[10]))
    records = []
    for shear_x, shear_y, offset_x, offset_y, center_x, center_y, center_z in cameras:
        first = [(rotation[0][k] + shear_x * rotation[2][k]) * scales[k] for k in range(3)]
        second = [(rotation[1][k] + shear_y * rotation[2][k]) * scales[k] for k in range(3)]
        cov_xx = first[0] * first[0] + first[1] * first[1] + first[2] * first[2] + 0.3
        cov_yy = second[0] * second[0] + second[1] * second[1] + second[2] * second[2] + 0.3
        cov_xy = first[0] * second[0] + first[1] * second[1] + first[2] * second[2]
        inverse = 1.0 / (cov_xx * cov_yy - cov_xy * cov_xy)
        toward_x = pos_x - center_x
        toward_y = pos_y - center_y
        toward_z = pos_z - center_z
        shrink = 1.0 / jnp.sqrt(toward_x * toward_x + toward_y * toward_y + toward_z * toward_z)
        basis = harmonics(toward_x * shrink, toward_y * shrink, toward_z * shrink)
        colors = []
        for c in range(3):
            total = basis[0] * rows[11 + c]
            for k in range(1, 16):
                total = total + basis[k] * rows[11 + 3 * k + c]
            colors.append(0.5 + total)
        records.append(
            [
                pos_x + shear_x * pos_z + offset_x,
                pos_y + shear_y * pos_z + offset_y,
                cov_yy * inverse,
                -cov_xy * inverse,
                cov_xx * inverse,
                opacity,
                *colors,
            ]
        )
    return records


def camera_of(refs, view):
    shear_ref, offset_ref, center_ref = refs
    return (
        shear_ref[view, 0],
        shear_ref[view, 1],
        offset_ref[view, 0],
        offset_ref[view, 1],
        center_ref[view, 0],
        center_ref[view, 1],
        center_ref[view, 2],
    )


BLOCK = 4096


def dense_rows(source_ref, sub):
    count = source_ref.shape[0]
    columns = pl.ds(pl.multiple_of(1024 * sub, 1024), 1024)
    rows = []
    for first in range(0, count, 8):
        size = min(8, count - first)
        block = source_ref[first : first + size, columns].reshape(size, 8, 128)
        rows += [block[r] for r in range(size)]
    return rows


def axis_peers(me, stride):
    place = lax.rem(me // stride, 4)
    return [me + (lax.rem(place + j, 4) - place) * stride for j in range(1, 4)]


def signal_all(semaphore, peers):
    for peer in peers:
        pl.semaphore_signal(semaphore, inc=1, device_id={"tile": peer}, device_id_type=MESH)


def greet_all(step, semaphores):
    plane_sem, cube_sem = semaphores
    me = lax.axis_index("tile")
    lines = [axis_peers(me, stride) for stride in (1, 4, 16)]
    barrier = pltpu.get_barrier_semaphore()

    @pl.when(step == 0)
    def _():
        for line in lines:
            signal_all(barrier, line)

    @pl.when(step == 1)
    def _():
        pl.semaphore_wait(barrier, 9)
        signal_all(plane_sem, lines[1])

    @pl.when(step == 2)
    def _():
        pl.semaphore_wait(plane_sem, 3)
        signal_all(cube_sem, lines[2])

    @pl.when(step == 3)
    def _():
        pl.semaphore_wait(cube_sem, 3)


def block_copy(outgoing, incoming, send_sem, recv_sem, peer):
    me = lax.axis_index("tile")
    return pltpu.make_async_remote_copy(
        src_ref=outgoing.at[peer],
        dst_ref=incoming.at[me],
        send_sem=send_sem.at[peer],
        recv_sem=recv_sem.at[me],
        device_id={"tile": peer},
        device_id_type=MESH,
    )


def send_block(outgoing, incoming, send_sem, recv_sem, peer):
    @pl.when(peer != lax.axis_index("tile"))
    def _():
        block_copy(outgoing, incoming, send_sem, recv_sem, peer).start()


def finish_blocks(outgoing, incoming, send_sem, recv_sem):
    me = lax.axis_index("tile")
    incoming[me] = outgoing[me]

    def finish(p, carry):
        peer = lax.rem(me + p, 64)
        block_copy(outgoing, incoming, send_sem, recv_sem, peer).wait_send()
        pltpu.make_async_remote_copy(
            src_ref=outgoing.at[peer],
            dst_ref=incoming.at[peer],
            send_sem=send_sem.at[peer],
            recv_sem=recv_sem.at[peer],
            device_id={"tile": peer},
            device_id_type=MESH,
        ).wait_recv()
        return carry

    lax.fori_loop(1, 64, finish, 0)


def exchange_scratch(rows):
    return [
        pltpu.VMEM((64, rows, 128), jnp.float32),
        pltpu.VMEM((64, rows, 128), jnp.float32),
        pltpu.SemaphoreType.DMA((64,)),
        pltpu.SemaphoreType.DMA((64,)),
        pltpu.SemaphoreType.REGULAR,
        pltpu.SemaphoreType.REGULAR,
    ]


def project_kernel(
    params_ref, index_ref, view_ref, shear_ref, offset_ref, center_ref, out_ref,
    table, high_parts, low_parts, outgoing, incoming, send_sem, recv_sem, *greetings,
):
    step = pl.program_id(0)
    greet_all(step, greetings)
    camera = camera_of((shear_ref, offset_ref, center_ref), view_ref[0])

    def part(sub, carry):
        record = project_rows(dense_rows(params_ref, sub), [camera])[0]
        first = pl.multiple_of(step * (BLOCK // 128) + 8 * sub, 8)
        for q in range(9):
            table[q, pl.ds(first, 8), :] = record[q]
        return carry

    lax.fori_loop(0, BLOCK // 1024, part, 0, unroll=2)

    @pl.when(step == pl.num_programs(0) - 1)
    def _():
        for q in range(9):
            for half in range(2):
                store_parts(
                    table[q, 64 * half : 64 * half + 64, :],
                    high_parts, low_parts, q, pl.ds(128 * half, 128),
                )
        low_ids = lax.broadcasted_iota(jnp.int32, (256, 256), 0)
        high_ids = lax.broadcasted_iota(jnp.int32, (64, 256), 0)

        def pick(pair, carry):
            index = jnp.concatenate(
                [index_ref[pl.ds(pair, 1), :], index_ref[pl.ds(pair + 32, 1), :]], axis=1
            )
            high = (index >> 7) & 63
            low = (index & 127) + ((index >> 13) << 7)
            rows = pick_rows(high_parts, low_parts, one_hot(low_ids, low), high_ids == high)
            for q in range(9):
                outgoing[pair, q : q + 1, :] = rows[q][:, 0:128]
                outgoing[pair + 32, q : q + 1, :] = rows[q][:, 128:256]
            return carry

        me = lax.axis_index("tile")

        def group(part, carry):
            first = lax.rem(part + me, 4) * 8
            lax.fori_loop(0, 8, lambda k, carry: pick(first + k, carry), 0, unroll=4)

            def send(k, carry):
                for peer in (first + k, first + k + 32):
                    send_block(outgoing, incoming, send_sem, recv_sem, peer)
                return carry

            lax.fori_loop(0, 8, send, 0)
            return carry

        lax.fori_loop(0, 4, group, 0)
        finish_blocks(outgoing, incoming, send_sem, recv_sem)
        out_ref[...] = incoming[...]


def project_and_pick(params, send_index, view, shear, offset, center):
    smem = pl.BlockSpec(memory_space=pltpu.SMEM)
    return pl.pallas_call(
        project_kernel,
        grid=(16384 // BLOCK,),
        out_shape=jax.ShapeDtypeStruct((64, 9, 128), jnp.float32),
        in_specs=[
            pl.BlockSpec((59, BLOCK), lambda i: (0, i)),
            pl.BlockSpec((64, 128), lambda i: (0, 0)),
            smem,
            smem,
            smem,
            smem,
        ],
        out_specs=pl.BlockSpec((64, 9, 128), lambda i: (0, 0, 0)),
        scratch_shapes=[
            pltpu.VMEM((9, 128, 128), jnp.float32),
            pltpu.VMEM((576, 512), jnp.bfloat16),
            pltpu.VMEM((128, 256), jnp.bfloat16),
            *exchange_scratch(9),
        ],
        compiler_params=pltpu.CompilerParams(
            collective_id=0, has_side_effects=True, vmem_limit_bytes=VMEM_LIMIT
        ),
        name="project_and_pick",
    )(params, send_index, view, shear, offset, center)


def slot_place(index):
    return (index >> 7) & 31, (index & 127) + ((index >> 12) << 7)


def one_hot(ids, values):
    return (ids == values).astype(jnp.float32).astype(jnp.bfloat16)


def store_parts(rows, high_parts, low_parts, q, columns):
    count = rows.shape[0]
    high, middle, low = split3(rows)
    here = pl.ds(count * q, count)
    width = columns.size
    high_parts[here, columns] = high
    high_parts[here, pl.ds(columns.start + 256, width)] = middle
    if q < 2:
        low_parts[here, columns] = low


def both_parts(value, right, dims):
    sums = mxu(jnp.concatenate(split2(value), axis=0), right, dims)
    return sums[: value.shape[0]] + sums[value.shape[0] :]


def pick_rows(high_parts, low_parts, hot, mask):
    count = mask.shape[0]
    found = mxu(high_parts[...], jnp.concatenate([hot, hot], axis=0), NN)
    found_low = mxu(low_parts[...], hot, NN)
    rows = []
    for q in range(9):
        part = found[count * q : count * q + count]
        if q < 2:
            part = part + found_low[count * q : count * q + count]
        rows.append(jnp.sum(jnp.where(mask, part, 0.0), axis=0, keepdims=True))
    return rows


def place_rows(rows, total, hot, mask):
    count = mask.shape[0]
    high_rows, low_rows = [], []
    for row in rows:
        high = row.astype(jnp.bfloat16).astype(jnp.float32)
        high_rows.append(jnp.where(mask, high, 0.0))
        low_rows.append(jnp.where(mask, row - high, 0.0))
    placed = jnp.concatenate(high_rows + low_rows, axis=0).astype(jnp.bfloat16)
    sums = mxu(placed, hot, NT)
    total[...] += sums[: 9 * count] + sums[9 * count :]


def tile_deltas(tile, band, u_row, w_row):
    offsets = lax.broadcasted_iota(jnp.int32, (16, 256), 0)
    pixel_x = (offsets + 16 * tile).astype(jnp.float32) + 0.5
    pixel_y = (offsets + 16 * band).astype(jnp.float32) + 0.5
    return pixel_x - u_row, pixel_y - w_row


def forward_tile(tile, band, picked, before, cover_ref, keep_ref, total):
    rows = [picked[tile, q : q + 1, :] for q in range(9)]
    delta_x, delta_y = tile_deltas(tile, band, rows[0], rows[1])
    along_x = -0.5 * rows[2] * delta_x * delta_x
    mixed = -rows[3] * delta_x
    along_y = -0.5 * rows[4] * delta_y * delta_y
    color_ids = lax.broadcasted_iota(jnp.int32, (128, 256), 0)
    colors = jnp.zeros((128, 256), jnp.float32)
    for c in range(3):
        colors = jnp.where(color_ids == 3 * tile + c, rows[6 + c], colors)
    colors = jnp.concatenate(split2(colors), axis=0)
    pieces = []
    for i in range(16):
        exponent = along_x + (mixed * delta_y[i : i + 1] + along_y[i : i + 1])
        pieces.append(rows[5] * jnp.exp(exponent))
    cover = jnp.concatenate(pieces, axis=0)
    keep = jnp.exp(both_parts(jnp.log(1.0 - cover), before[...], NN))
    cover_ref[tile] = cover
    keep_ref[tile] = keep
    shown = mxu(jnp.concatenate(split2(cover * keep), axis=0), colors, NT)
    total[...] += shown[0:256, 0:128] + shown[0:256, 128:256] + shown[256:512, 0:128]


def backward_tile(tile, slot, band, picked, after, cover_ref, keep_ref, grad_ref, results, high_weights, low_weights):
    rows = [picked[tile, q : q + 1, :] for q in range(9)]
    grads = jnp.concatenate([grad_ref[pl.ds(3 * tile + c, 1), :] for c in range(3)], axis=0)
    colors = jnp.concatenate(rows[6:9], axis=0)
    grads_high = grads.astype(jnp.bfloat16).astype(jnp.float32)
    grads_low = grads - grads_high
    colors_high = colors.astype(jnp.bfloat16).astype(jnp.float32)
    colors_low = colors - colors_high
    blank = jnp.zeros((7, 256), jnp.float32)
    left = jnp.concatenate([grads_high, grads_high, grads_low, blank], axis=0).astype(jnp.bfloat16)
    right = jnp.concatenate([colors_high, colors_low, colors_high, blank], axis=0).astype(jnp.bfloat16)
    both = jnp.concatenate([grads_high, grads_low, blank, blank[0:3]], axis=0).astype(jnp.bfloat16)
    delta_x, delta_y = tile_deltas(tile, band, rows[0], rows[1])
    shade = mxu(left, right, TN)
    cover = cover_ref[tile]
    weight = cover * keep_ref[tile]
    weight_high, weight_low = split2(weight)
    high_weights[slot] = weight_high
    low_weights[slot] = weight_low
    lit = weight * shade
    behind = both_parts(lit, after[...], NN)
    pull = lit - behind * (cover / (1.0 - cover))
    sum_0 = jnp.zeros((16, 256), jnp.float32)
    sum_y = sum_0
    sum_yy = sum_0
    for i in range(16):
        piece = pull[16 * i : 16 * i + 16]
        level = delta_y[i : i + 1]
        piece_y = piece * level
        sum_0 = sum_0 + piece
        sum_y = sum_y + piece_y
        sum_yy = sum_yy + piece_y * level
    color_grad = mxu(both, high_weights[slot], NN)
    color_grad = color_grad[0:3] + color_grad[3:6] + mxu(both, low_weights[slot], NN)[0:3]
    sum_x = sum_0 * delta_x

    def fold(value):
        return jnp.sum(value, axis=0, keepdims=True)

    moment_x = fold(sum_x)
    moment_y = fold(sum_y)
    live = rows[5] > 0.0
    values = [
        rows[2] * moment_x + rows[3] * moment_y,
        rows[4] * moment_y + rows[3] * moment_x,
        -0.5 * fold(sum_x * delta_x),
        -fold(sum_y * delta_x),
        -0.5 * fold(sum_yy),
        jnp.where(live, fold(sum_0) / jnp.where(live, rows[5], 1.0), 0.0),
        color_grad[0:1],
        color_grad[1:2],
        color_grad[2:3],
    ]
    for q in range(9):
        results[tile, q : q + 1, :] = values[q]


def blurred_down(planes, count):
    taps = window_taps()
    result = taps[5] * planes[5 : 5 + count]
    for k in range(5):
        result = result + taps[k] * (planes[k : k + count] + planes[10 - k : 10 - k + count])
    return result


def blurred_across(planes, spread):
    taps = window_taps()
    spread[:, 0:8, :] = pltpu.roll(planes[:, 8:16], 3, 2)
    spread[:, 8:24, :] = planes
    spread[:, 24:32, :] = pltpu.roll(planes[:, 0:8], 125, 2)
    result = taps[5] * planes
    for k in range(5):
        result = result + taps[k] * (spread[:, 3 + k : 19 + k, :] + spread[:, 13 - k : 29 - k, :])
    return result


def window_step(band, last_band, image_ref, truth_ref, grad_ref, spread):
    image = image_ref[...].reshape(36, 16, 128)
    truth = truth_ref[...].reshape(36, 16, 128)
    stage = lax.broadcasted_iota(jnp.int32, (36, 16, 128), 0) - 10 + 16 * band
    within = (stage >= 0) & (stage < 16 * (last_band + 1))
    image = jnp.where(within, image, 0.0)
    truth = jnp.where(within, truth, 0.0)
    stats = []
    for k, plane in enumerate((image, truth, image * image, truth * truth, image * truth)):
        stats.append(blurred_across(blurred_down(plane, 26), spread.at[k]))
    mean_x, mean_y, power_x, power_y, cross_xy = stats
    similarity, ssim_back = jax.vjp(
        lambda level_x, energy_x, product_xy: ssim_map(
            level_x, mean_y, energy_x, power_y, product_xy
        ),
        mean_x,
        power_x,
        cross_xy,
    )
    lanes = lax.broadcasted_iota(jnp.int32, (26, 16, 128), 2)
    counted = within[5:31] & (lanes < 96)
    pulled = []
    for k, plane in enumerate(ssim_back(jnp.where(counted, -0.8, 0.0))):
        pulled.append(blurred_across(blurred_down(plane, 16), spread.at[k, 0:16]))
    shown = image[10:26]
    wanted = truth[10:26]
    difference = shown - wanted
    smooth = jnp.sqrt(difference * difference + 0.0001)
    loss = jnp.where(lanes[0:16] < 96, 0.2 * smooth + 0.8 * (1.0 - similarity[5:21]), 0.0)
    pixel_grad = 0.2 * difference / smooth + pulled[0] + 2.0 * shown * pulled[1] + wanted * pulled[2]
    grad_ref[...] = jnp.transpose(pixel_grad.reshape(256, 128))
    return jnp.sum(jnp.sum(loss, axis=0), axis=0, keepdims=True)


def render_kernel(
    slots_ref, list_ref, count_ref, view_ref, back_ref, target_ref, index_ref, sent_ref,
    own_ref, other_ref,
    high_parts, low_parts, before, after, picked, cover_ref, keep_ref, results, total, slot_total, owner_total,
    target_rows, image_ref, truth_ref, grad_ref, spread, high_weights, low_weights,
    outgoing, incoming, send_sem, recv_sem, plane_sem, cube_sem, halo_send, halo_recv, swap_send, swap_recv,
):
    me = lax.axis_index("tile")
    pair = 1 - lax.axis_index("view")
    band = me
    last_band = lax.axis_size("tile") - 1
    view = view_ref[0]
    barrier = pltpu.get_barrier_semaphore()
    lines = [axis_peers(me, stride) for stride in (1, 4, 16)]
    for line in lines:
        signal_all(barrier, line)
    pl.semaphore_signal(barrier, inc=1, device_id={"view": pair}, device_id_type=MESH)

    for q in range(9):
        for half in range(2):
            store_parts(
                slots_ref[32 * half : 32 * half + 32, q, :], high_parts, low_parts, q, pl.ds(128 * half, 128)
            )
    row_ids = lax.broadcasted_iota(jnp.int32, (256, 256), 0)
    column_ids = lax.broadcasted_iota(jnp.int32, (256, 256), 1)
    before[...] = (row_ids < column_ids).astype(jnp.float32).astype(jnp.bfloat16)
    after[...] = (row_ids > column_ids).astype(jnp.float32).astype(jnp.bfloat16)
    own_pixels = slice(160, 416)
    target_rows[0:96, :] = target_ref[...]
    target_rows[96:128, :] = jnp.zeros((32, 256), jnp.float32)
    truth_ref[own_pixels, :] = jnp.transpose(target_rows[...])
    lanes = lax.broadcasted_iota(jnp.int32, (1, 256), 1)
    high_ids = lax.broadcasted_iota(jnp.int32, (32, 256), 0)

    def pick(tile, carry):
        high, low = slot_place(list_ref[pl.ds(tile, 1), :])
        low_ids = lax.broadcasted_iota(jnp.int32, (256, 256), 0)
        rows = pick_rows(high_parts, low_parts, one_hot(low_ids, low), high_ids == high)
        rows[5] = jnp.where(lanes < count_ref[0, tile], rows[5], 0.0)
        for c in range(3):
            rows[6 + c] = rows[6 + c] - back_ref[view, c]
        for q in range(9):
            picked[tile, q : q + 1, :] = rows[q]
        return carry

    lax.fori_loop(0, 32, pick, 0, unroll=4)
    pl.semaphore_wait(barrier, 10)
    signal_all(plane_sem, lines[1])
    total[...] = jnp.zeros_like(total)

    def forward(tile, carry):
        forward_tile(tile, band, picked, before, cover_ref, keep_ref, total)
        return carry

    lax.fori_loop(0, 12, forward, 0, unroll=4)
    pl.semaphore_wait(plane_sem, 3)
    signal_all(cube_sem, lines[2])
    lax.fori_loop(12, 24, forward, 0, unroll=4)
    pl.semaphore_wait(cube_sem, 3)

    following, previous = lax.rem(me + 1, 64), lax.rem(me + 63, 64)

    def halo(field, k, peer, source, target):
        return pltpu.make_async_remote_copy(
            src_ref=field.at[pl.ds(source, 160), :],
            dst_ref=field.at[pl.ds(target, 160), :],
            send_sem=halo_send.at[k],
            recv_sem=halo_recv.at[k],
            device_id={"tile": peer},
            device_id_type=MESH,
        )

    copies = [halo(truth_ref, 0, following, 256, 0), halo(truth_ref, 1, previous, 160, 416)]
    for copy in copies:
        copy.start()
    lax.fori_loop(24, 32, forward, 0, unroll=4)
    color_lanes = lax.broadcasted_iota(jnp.int32, (1, 128), 1)
    backdrop = jnp.zeros((1, 128), jnp.float32)
    for c in range(3):
        here = (lax.rem(color_lanes, 3) == c) & (color_lanes < 96)
        backdrop = jnp.where(here, back_ref[view, c], backdrop)
    image_ref[own_pixels, :] = total[...] + backdrop
    shown = [halo(image_ref, 2, following, 256, 0), halo(image_ref, 3, previous, 160, 416)]
    for copy in shown:
        copy.start()
    for copy in copies + shown:
        copy.wait()
    loss = window_step(band, last_band, image_ref, truth_ref, grad_ref, spread)

    def backward(group, carry):
        for slot in range(4):
            backward_tile(
                4 * group + slot, slot, band, picked, after, cover_ref, keep_ref, grad_ref, results,
                high_weights, low_weights,
            )
        return carry

    lax.fori_loop(0, 8, backward, 0)
    slot_total[...] = jnp.zeros_like(slot_total)

    def place_slots(tile, carry):
        high, low = slot_place(list_ref[pl.ds(tile, 1), :])
        low_ids = lax.broadcasted_iota(jnp.int32, (256, 256), 0)
        rows = [results[tile, q : q + 1, :] for q in range(9)]
        place_rows(rows, slot_total, one_hot(low_ids, low), high_ids == high)
        return carry

    lax.fori_loop(0, 32, place_slots, 0, unroll=4)
    for q in range(9):
        for half in range(2):
            outgoing[32 * half : 32 * half + 32, q, :] = slot_total[
                32 * q : 32 * q + 32, 128 * half : 128 * half + 128
            ]
    outgoing[:, 9, :] = jnp.broadcast_to(loss, (64, 128))

    def send(p, carry):
        block_copy(outgoing, incoming, send_sem, recv_sem, lax.rem(me + p, 64)).start()
        return carry

    lax.fori_loop(1, 64, send, 0)
    owner_total[...] = jnp.zeros_like(owner_total)
    owner_ids = lax.broadcasted_iota(jnp.int32, (64, 256), 0)
    finish_blocks(outgoing, incoming, send_sem, recv_sem)

    def place_owned(first, carry):
        def joined(values):
            return jnp.concatenate(values, axis=1)

        bands = (first, first + 32)
        index = joined([index_ref[pl.ds(d, 1), :] for d in bands])
        live = joined([(color_lanes < sent_ref[0, d]).astype(jnp.int32) for d in bands])
        high = jnp.where(live > 0, (index >> 7) & 63, -1)
        low = (index & 127) + ((index >> 13) << 7)
        low_ids = lax.broadcasted_iota(jnp.int32, (256, 256), 0)
        rows = [joined([incoming[d, q : q + 1, :] for d in bands]) for q in range(9)]
        place_rows(rows, owner_total, one_hot(low_ids, low), owner_ids == high)
        return carry

    lax.fori_loop(0, 32, place_owned, 0, unroll=4)
    for q in range(9):
        for half in range(2):
            own_ref[q, 64 * half : 64 * half + 64, :] = owner_total[
                64 * q : 64 * q + 64, 128 * half : 128 * half + 128
            ]
    losses = jnp.sum(incoming[:, 9, :], axis=0, keepdims=True)
    own_ref[9] = jnp.broadcast_to(losses, (128, 128))
    swap = pltpu.make_async_remote_copy(
        src_ref=own_ref,
        dst_ref=other_ref,
        send_sem=swap_send,
        recv_sem=swap_recv,
        device_id={"view": pair},
        device_id_type=MESH,
    )
    swap.start()
    swap.wait()


def render_step(slots, lists, counts, view, back, target_tiles, send_index, send_count):
    smem = pl.BlockSpec(memory_space=pltpu.SMEM)
    vmem = pl.BlockSpec(memory_space=pltpu.VMEM)
    shape = jax.ShapeDtypeStruct((10, 128, 128), jnp.float32)
    f32, bf16 = jnp.float32, jnp.bfloat16
    return pl.pallas_call(
        render_kernel,
        out_shape=(shape, shape),
        in_specs=[vmem, vmem, smem, smem, smem, vmem, vmem, smem],
        out_specs=(vmem, vmem),
        scratch_shapes=[
            pltpu.VMEM((288, 512), bf16),
            pltpu.VMEM((64, 256), bf16),
            pltpu.VMEM((256, 256), bf16),
            pltpu.VMEM((256, 256), bf16),
            pltpu.VMEM((32, 9, 256), f32),
            pltpu.VMEM((32, 256, 256), f32),
            pltpu.VMEM((32, 256, 256), f32),
            pltpu.VMEM((32, 9, 256), f32),
            pltpu.VMEM((256, 128), f32),
            pltpu.VMEM((288, 256), f32),
            pltpu.VMEM((576, 256), f32),
            pltpu.VMEM((128, 256), f32),
            pltpu.VMEM((576, 128), f32),
            pltpu.VMEM((576, 128), f32),
            pltpu.VMEM((128, 256), f32),
            pltpu.VMEM((5, 26, 32, 128), f32),
            pltpu.VMEM((4, 256, 256), bf16),
            pltpu.VMEM((4, 256, 256), bf16),
            *exchange_scratch(10),
            pltpu.SemaphoreType.DMA((4,)),
            pltpu.SemaphoreType.DMA((4,)),
            pltpu.SemaphoreType.DMA,
            pltpu.SemaphoreType.DMA,
        ],
        compiler_params=pltpu.CompilerParams(
            collective_id=1, has_side_effects=True, vmem_limit_bytes=VMEM_LIMIT
        ),
        name="render_step",
    )(slots, lists, counts, view, back, target_tiles, send_index, send_count)


RATES = [0.016] * 3 + [0.005] * 3 + [0.001] * 4 + [0.05] + [0.0025] * 3 + [0.000125] * 45
LOSS_TERMS = 2 * 3 * 1024 * 512


def update_kernel(
    params_ref, first_ref, second_ref, own_ref, other_ref, view_ref, shear_ref, offset_ref, center_ref,
    params_out, first_out, second_out, loss_out, dense,
):
    refs = (shear_ref, offset_ref, center_ref)
    cameras = [camera_of(refs, 0), camera_of(refs, 1)]
    is_first = view_ref[0] == 0
    losses = own_ref[9, 0:1, :] + other_ref[9, 0:1, :]
    loss_out[...] = jnp.sum(losses, axis=1, keepdims=True) / LOSS_TERMS

    def part(sub, carry):
        rows = dense_rows(params_ref, sub)
        _, pull_back = jax.vjp(lambda *values: project_rows(values, cameras), *rows)
        here = pl.ds(pl.multiple_of(8 * sub, 8), 8)
        own = [own_ref[q, here, :] for q in range(9)]
        other = [other_ref[q, here, :] for q in range(9)]
        gradient = pull_back(
            [
                [jnp.where(is_first, a, b) for a, b in zip(own, other)],
                [jnp.where(is_first, b, a) for a, b in zip(own, other)],
            ]
        )
        for r in range(59):
            dense[8 * r : 8 * r + 8, :] = gradient[r]
        for first in range(0, 59, 8):
            size = min(8, 59 - first)
            row_ids = lax.broadcasted_iota(jnp.int32, (size, 128), 0)
            rate = jnp.full((size, 128), RATES[first], jnp.float32)
            for r in range(1, size):
                if RATES[first + r] != RATES[first + r - 1]:
                    rate = jnp.where(row_ids >= r, RATES[first + r], rate)
            rate = rate / (1.0 - 0.9**STEP_COUNT)
            for c in range(8):
                columns = pl.ds(pl.multiple_of(1024 * sub + 128 * c, 128), 128)
                here = (slice(first, first + size), columns)
                grad = dense[pl.ds(8 * first + c, size, stride=8), :]
                new_first = 0.9 * first_ref[here] + 0.1 * grad
                new_second = 0.999 * second_ref[here] + 0.001 * grad * grad
                scale = jnp.sqrt(new_second * (1.0 / (1.0 - 0.999**STEP_COUNT))) + 1e-15
                params_out[here] = params_ref[here] - rate * new_first / scale
                first_out[here] = new_first
                second_out[here] = new_second
        return carry

    lax.fori_loop(0, BLOCK // 1024, part, 0)


def update(params, first_moment, second_moment, own, other, view, shear, offset, center):
    smem = pl.BlockSpec(memory_space=pltpu.SMEM)
    block = pl.BlockSpec((59, BLOCK), lambda i: (0, i))
    grads = pl.BlockSpec((10, BLOCK // 128, 128), lambda i: (0, i, 0))
    shape = jax.ShapeDtypeStruct(params.shape, jnp.float32)
    return pl.pallas_call(
        update_kernel,
        grid=(16384 // BLOCK,),
        out_shape=(shape, shape, shape, jax.ShapeDtypeStruct((1, 1), jnp.float32)),
        in_specs=[block, block, block, grads, grads, smem, smem, smem, smem],
        out_specs=(block, block, block, pl.BlockSpec((1, 1), lambda i: (0, 0))),
        scratch_shapes=[pltpu.VMEM((59 * 8, 128), jnp.float32)],
        compiler_params=pltpu.CompilerParams(vmem_limit_bytes=VMEM_LIMIT),
        name="update",
    )(params, first_moment, second_moment, own, other, view, shear, offset, center)


def shards(
    params,
    first_moment,
    second_moment,
    target,
    view_shear,
    view_offset,
    cam_center,
    background,
    send_index,
    send_count,
    tile_list,
    tile_count,
):
    view_index = lax.axis_index("view")
    view = view_index.astype(jnp.int32).reshape(1)
    incoming = project_and_pick(params, send_index[0], view, view_shear, view_offset, cam_center)
    target_tiles = target[0].reshape(3, 16, 32, 16).transpose(2, 0, 1, 3).reshape(96, 256)
    own_grad, other_grad = render_step(
        incoming, tile_list[0, 0], tile_count, view, background, target_tiles, send_index[0], send_count
    )
    new_params, new_first, new_second, mean_loss = update(
        params, first_moment, second_moment, own_grad, other_grad, view, view_shear, view_offset, cam_center
    )
    return (new_params, new_first, new_second, mean_loss[0, 0])


def solution(mesh):
    placed = (
        P(None, "tile"),
        P(None, "tile"),
        P(None, "tile"),
        P("view", None, "tile", None),
        P(),
        P(),
        P(),
        P(),
        P("tile", None, None),
        P("tile", None),
        P("view", "tile", None, None),
        P("tile", None),
    )
    return jax.shard_map(
        shards,
        mesh=mesh,
        in_specs=placed,
        out_specs=(P(None, "tile"), P(None, "tile"), P(None, "tile"), P()),
        check_vma=False,
    )
```

time: 124 us -> 99.3 us (0.80)
  other arithmetic: 8.02 us -> 0 us
  Pallas kernels: 103 us -> 96.8 us
  starting transfers between devices: 4.17 us -> 0 us
  local copies, waits for them, and re-layouts: 5.85 us -> 1.7 us
  waiting for transfers between devices: 1.93 us -> 0 us
    pallas_call x4 -> x1, Pallas kernels: 64.9 us -> 58.2 us  [render_step(): pl.pallas_call(render_kernel, out_shape=(shape, shape), in_specs=[vmem, v...]
    ppermute x1 -> x0, starting transfers between devices: 4.17 us -> none  [shards(): other_grad = lax.ppermute(own_grad, 'view', [(0, 1), (1, 0)])]
    mul x3 -> x0, other arithmetic: 2.75 us -> none  [the longest x1 1.59 us: ssim_map(): (2.0 * level_x * level_y + 0.0001) * (2.0 * (product_xy - level_x * level...]
    add x8 -> x0, other arithmetic: 2.41 us -> none  [the longest x6 1.51 us: gaussian_blur(): vertical + taps[position] * planes[:, position:position + rows_out]]
    ppermute x1 -> x0, waiting for transfers between devices: 1.93 us -> none  [shards(): other_grad = lax.ppermute(own_grad, 'view', [(0, 1), (1, 0)])]
  transfers between devices with their start and end apart: 1 -> 0, of which waited for: 1 -> 0; matrix products, arithmetic and copies ran while one was open for 0% -> 0% of each run, Pallas kernels for 0% -> 0%
where the time goes in v4:
time: 99.3 us; the launch traced here: 99.2 us
  Pallas kernels  96.8 us (97%)
  local copies, waits for them, and re-layouts  1.7 us (2%)
    pallas_call x1, Pallas kernels, render_step(): pl.pallas_call(render_kernel, out_shape=(shape, shape), in_specs=[vmem, v...  58.2 us
    pallas_call x1, Pallas kernels, project_and_pick(): pl.pallas_call(project_kernel, grid=(16384 // BLOCK,), out_shape=jax.Shap...  25.7 us
    pallas_call x1, Pallas kernels, update(): pl.pallas_call(update_kernel, grid=(16384 // BLOCK,), out_shape=(shape, s...  12.9 us

profile of v4, /device:TPU:1, one launch (start us, length us, event | category | flops | bytes accessed | tf_op | source)
XLA Modules:
  0.0 99.2 jit_solution(714836544313936312)
XLA Ops:
  0.6 0.0 copy-start
  0.6 25.7 %project_and_pick.1.slots_ref = f32[64,9,128]{2,1,0:T(8,128)} custom-call(f32[59,16384]{1,0:T(8,128)} %params_ref.3, s32[64,128]{1,0:T(8,128)} %bitcast.10, s32[1]{0:T(128)} %bitcast.1.view_ref, f32[2,2]{1,0:T(2,128)} %shear_ref.3, f32[2,2]{1,0:T(2,128)} %offset_ref.3, f32[2,3]{1,0:T(2,128)} %center_ref.3), custom_call_target="tpu_custom_call" | custom-call | tf_op jit(solution)/shard_map/project_and_pick/pallas_call | solution.py:309
  26.3 0.0 copy-done
  26.3 0.3 reshape_squeeze.3
  26.6 0.5 copy.17
  27.1 1.0 reshape.15.target_ref
  28.0 58.2 %render_step.1 = (f32[10,128,128]{2,1,0:T(8,128)}, f32[10,128,128]{2,1,0:T(8,128)}) custom-call(f32[64,9,128]{2,1,0:T(8,128)} %project_and_pick.1.slots_ref, s32[32,256]{1,0:T(8,128)} %bitcast.12, s32[1,32]{1,0:T(1,128)} %count_ref.1, s32[1]{0:T(128)} %bitcast.1.view_ref, f32[2,3]{1,0:T(2,128)} %back_ref.1, f32[96,256]{1,0:T(8,128)} %reshape.15.target_ref, ...), custom_call_target="tpu_custom_call" | custom-call | tf_op jit(solution)/shard_map/render_step/pallas_call | solution.py:687
  86.3 12.9 %update.1 = (f32[59,16384]{1,0:T(8,128)}, f32[59,16384]{1,0:T(8,128)}, f32[59,16384]{1,0:T(8,128)}, f32[1,1]{1,0:T(1,128)}) custom-call(f32[59,16384]{1,0:T(8,128)} %params_ref.3, f32[59,16384]{1,0:T(8,128)} %first_ref.1, f32[59,16384]{1,0:T(8,128)} %second_ref.1, f32[10,128,128]{2,1,0:T(8,128)} %get-tuple-element.10.own_ref, ...), custom_call_target="tpu_custom_call" | custom-call | tf_op jit(solution)/shard_map/update/pallas_call | solution.py:780
Async XLA Ops:
  0.6 25.7 %copy-start = (f32[1,3,16,512]{3,2,1,0:T(8,128)S(1)}, f32[1,3,16,512]{3,2,1,0:T(8,128)}, u32[]{:S(2)}) copy-start(f32[1,3,16,512]{3,2,1,0:T(8,128)} %param.15) | copy-start | bytes 294916

commit v5 on v4

--- a/solution.py
+++ b/solution.py
@@ -50,7 +50,7 @@
 
 
 MESH = pl.DeviceIdType.MESH
-VMEM_LIMIT = 56 * 1024 * 1024
+MIB = 1024 * 1024
 NN = (((1,), (0,)), ((), ()))
 NT = (((1,), (1,)), ((), ()))
 TN = (((0,), (0,)), ((), ()))
@@ -201,8 +201,8 @@
     return pltpu.make_async_remote_copy(
         src_ref=outgoing.at[peer],
         dst_ref=incoming.at[me],
-        send_sem=send_sem.at[peer],
-        recv_sem=recv_sem.at[me],
+        send_sem=send_sem,
+        recv_sem=recv_sem,
         device_id={"tile": peer},
         device_id_type=MESH,
     )
@@ -216,30 +216,23 @@
 
 def finish_blocks(outgoing, incoming, send_sem, recv_sem):
     me = lax.axis_index("tile")
+    pltpu.make_async_remote_copy(
+        src_ref=outgoing.at[0:63],
+        dst_ref=incoming.at[0:63],
+        send_sem=send_sem,
+        recv_sem=recv_sem,
+        device_id={"tile": lax.rem(me + 1, 64)},
+        device_id_type=MESH,
+    ).wait()
     incoming[me] = outgoing[me]
-
-    def finish(p, carry):
-        peer = lax.rem(me + p, 64)
-        block_copy(outgoing, incoming, send_sem, recv_sem, peer).wait_send()
-        pltpu.make_async_remote_copy(
-            src_ref=outgoing.at[peer],
-            dst_ref=incoming.at[peer],
-            send_sem=send_sem.at[peer],
-            recv_sem=recv_sem.at[peer],
-            device_id={"tile": peer},
-            device_id_type=MESH,
-        ).wait_recv()
-        return carry
-
-    lax.fori_loop(1, 64, finish, 0)
 
 
 def exchange_scratch(rows):
     return [
         pltpu.VMEM((64, rows, 128), jnp.float32),
         pltpu.VMEM((64, rows, 128), jnp.float32),
-        pltpu.SemaphoreType.DMA((64,)),
-        pltpu.SemaphoreType.DMA((64,)),
+        pltpu.SemaphoreType.DMA,
+        pltpu.SemaphoreType.DMA,
         pltpu.SemaphoreType.REGULAR,
         pltpu.SemaphoreType.REGULAR,
     ]
@@ -326,7 +319,7 @@
             *exchange_scratch(9),
         ],
         compiler_params=pltpu.CompilerParams(
-            collective_id=0, has_side_effects=True, vmem_limit_bytes=VMEM_LIMIT
+            collective_id=0, has_side_effects=True, vmem_limit_bytes=56 * MIB
         ),
         name="project_and_pick",
     )(params, send_index, view, shear, offset, center)
@@ -407,11 +400,11 @@
     keep = jnp.exp(both_parts(jnp.log(1.0 - cover), before[...], NN))
     cover_ref[tile] = cover
     keep_ref[tile] = keep
-    shown = mxu(jnp.concatenate(split2(cover * keep), axis=0), colors, NT)
-    total[...] += shown[0:256, 0:128] + shown[0:256, 128:256] + shown[256:512, 0:128]
-
-
-def backward_tile(tile, slot, band, picked, after, cover_ref, keep_ref, grad_ref, results, high_weights, low_weights):
+    shown = mxu((cover * keep).astype(jnp.bfloat16), colors, NT)
+    total[...] += shown[:, 0:128] + shown[:, 128:256]
+
+
+def backward_tile(tile, band, picked, after, cover_ref, keep_ref, grad_ref, results):
     rows = [picked[tile, q : q + 1, :] for q in range(9)]
     grads = jnp.concatenate([grad_ref[pl.ds(3 * tile + c, 1), :] for c in range(3)], axis=0)
     colors = jnp.concatenate(rows[6:9], axis=0)
@@ -425,14 +418,10 @@
     both = jnp.concatenate([grads_high, grads_low, blank, blank[0:3]], axis=0).astype(jnp.bfloat16)
     delta_x, delta_y = tile_deltas(tile, band, rows[0], rows[1])
     shade = mxu(left, right, TN)
-    cover = cover_ref[tile]
-    weight = cover * keep_ref[tile]
-    weight_high, weight_low = split2(weight)
-    high_weights[slot] = weight_high
-    low_weights[slot] = weight_low
+    weight = keep_ref[tile]
     lit = weight * shade
-    behind = both_parts(lit, after[...], NN)
-    pull = lit - behind * (cover / (1.0 - cover))
+    behind = mxu(lit.astype(jnp.bfloat16), after[...], NN)
+    pull = lit - behind * cover_ref[tile]
     sum_0 = jnp.zeros((16, 256), jnp.float32)
     sum_y = sum_0
     sum_yy = sum_0
@@ -443,8 +432,8 @@
         sum_0 = sum_0 + piece
         sum_y = sum_y + piece_y
         sum_yy = sum_yy + piece_y * level
-    color_grad = mxu(both, high_weights[slot], NN)
-    color_grad = color_grad[0:3] + color_grad[3:6] + mxu(both, low_weights[slot], NN)[0:3]
+    color_grad = mxu(both, weight.astype(jnp.bfloat16), NN)
+    color_grad = color_grad[0:3] + color_grad[3:6]
     sum_x = sum_0 * delta_x
 
     def fold(value):
@@ -487,17 +476,29 @@
     return result
 
 
-def window_step(band, last_band, image_ref, truth_ref, grad_ref, spread):
-    image = image_ref[...].reshape(36, 16, 128)
-    truth = truth_ref[...].reshape(36, 16, 128)
-    stage = lax.broadcasted_iota(jnp.int32, (36, 16, 128), 0) - 10 + 16 * band
-    within = (stage >= 0) & (stage < 16 * (last_band + 1))
-    image = jnp.where(within, image, 0.0)
-    truth = jnp.where(within, truth, 0.0)
-    stats = []
-    for k, plane in enumerate((image, truth, image * image, truth * truth, image * truth)):
-        stats.append(blurred_across(blurred_down(plane, 26), spread.at[k]))
-    mean_x, mean_y, power_x, power_y, cross_xy = stats
+def rows_within(field_ref, band, last_band):
+    rows = lax.broadcasted_iota(jnp.int32, (36, 16, 128), 0) - 10 + 16 * band
+    within = (rows >= 0) & (rows < 16 * (last_band + 1))
+    return jnp.where(within, field_ref[...].reshape(36, 16, 128), 0.0), within
+
+
+def window_of(plane, spread):
+    return blurred_across(blurred_down(plane, 26), spread)
+
+
+def truth_step(band, last_band, truth_ref, spread, truth_stats):
+    truth, _ = rows_within(truth_ref, band, last_band)
+    truth_stats[0] = window_of(truth, spread.at[0])
+    truth_stats[1] = window_of(truth * truth, spread.at[1])
+
+
+def window_step(band, last_band, image_ref, truth_ref, grad_ref, spread, truth_stats):
+    image, within = rows_within(image_ref, band, last_band)
+    truth, _ = rows_within(truth_ref, band, last_band)
+    mean_x = window_of(image, spread.at[0])
+    power_x = window_of(image * image, spread.at[1])
+    cross_xy = window_of(image * truth, spread.at[2])
+    mean_y, power_y = truth_stats[0], truth_stats[1]
     similarity, ssim_back = jax.vjp(
         lambda level_x, energy_x, product_xy: ssim_map(
             level_x, mean_y, energy_x, power_y, product_xy
@@ -525,7 +526,7 @@
     slots_ref, list_ref, count_ref, view_ref, back_ref, target_ref, index_ref, sent_ref,
     own_ref, other_ref,
     high_parts, low_parts, before, after, picked, cover_ref, keep_ref, results, total, slot_total, owner_total,
-    target_rows, image_ref, truth_ref, grad_ref, spread, high_weights, low_weights,
+    target_rows, image_ref, truth_ref, grad_ref, spread, truth_stats,
     outgoing, incoming, send_sem, recv_sem, plane_sem, cube_sem, halo_send, halo_recv, swap_send, swap_recv,
 ):
     me = lax.axis_index("tile")
@@ -606,29 +607,44 @@
     shown = [halo(image_ref, 2, following, 256, 0), halo(image_ref, 3, previous, 160, 416)]
     for copy in shown:
         copy.start()
-    for copy in copies + shown:
+    for copy in copies:
         copy.wait()
-    loss = window_step(band, last_band, image_ref, truth_ref, grad_ref, spread)
+    truth_step(band, last_band, truth_ref, spread, truth_stats)
+
+    def prepare(tile, carry):
+        cover = cover_ref[tile]
+        keep_ref[tile] = cover * keep_ref[tile]
+        cover_ref[tile] = cover / (1.0 - cover)
+        return carry
+
+    lax.fori_loop(0, 32, prepare, 0, unroll=2)
+    for copy in shown:
+        copy.wait()
+    loss = window_step(band, last_band, image_ref, truth_ref, grad_ref, spread, truth_stats)
 
     def backward(group, carry):
         for slot in range(4):
             backward_tile(
-                4 * group + slot, slot, band, picked, after, cover_ref, keep_ref, grad_ref, results,
-                high_weights, low_weights,
+                4 * group + slot, band, picked, after, cover_ref, keep_ref, grad_ref, results
             )
         return carry
 
     lax.fori_loop(0, 8, backward, 0)
     slot_total[...] = jnp.zeros_like(slot_total)
 
+    def joined(values):
+        return jnp.concatenate(values, axis=1)
+
     def place_slots(tile, carry):
-        high, low = slot_place(list_ref[pl.ds(tile, 1), :])
-        low_ids = lax.broadcasted_iota(jnp.int32, (256, 256), 0)
-        rows = [results[tile, q : q + 1, :] for q in range(9)]
-        place_rows(rows, slot_total, one_hot(low_ids, low), high_ids == high)
+        tiles = (tile, tile + 16)
+        high, low = slot_place(joined([list_ref[pl.ds(t, 1), :] for t in tiles]))
+        low_ids = lax.broadcasted_iota(jnp.int32, (256, 512), 0)
+        slot_ids = lax.broadcasted_iota(jnp.int32, (32, 512), 0)
+        rows = [joined([results[t, q : q + 1, :] for t in tiles]) for q in range(9)]
+        place_rows(rows, slot_total, one_hot(low_ids, low), slot_ids == high)
         return carry
 
-    lax.fori_loop(0, 32, place_slots, 0, unroll=4)
+    lax.fori_loop(0, 16, place_slots, 0, unroll=4)
     for q in range(9):
         for half in range(2):
             outgoing[32 * half : 32 * half + 32, q, :] = slot_total[
@@ -642,24 +658,21 @@
 
     lax.fori_loop(1, 64, send, 0)
     owner_total[...] = jnp.zeros_like(owner_total)
-    owner_ids = lax.broadcasted_iota(jnp.int32, (64, 256), 0)
+    owner_ids = lax.broadcasted_iota(jnp.int32, (64, 512), 0)
     finish_blocks(outgoing, incoming, send_sem, recv_sem)
 
     def place_owned(first, carry):
-        def joined(values):
-            return jnp.concatenate(values, axis=1)
-
-        bands = (first, first + 32)
+        bands = (first, first + 16, first + 32, first + 48)
         index = joined([index_ref[pl.ds(d, 1), :] for d in bands])
         live = joined([(color_lanes < sent_ref[0, d]).astype(jnp.int32) for d in bands])
         high = jnp.where(live > 0, (index >> 7) & 63, -1)
         low = (index & 127) + ((index >> 13) << 7)
-        low_ids = lax.broadcasted_iota(jnp.int32, (256, 256), 0)
+        low_ids = lax.broadcasted_iota(jnp.int32, (256, 512), 0)
         rows = [joined([incoming[d, q : q + 1, :] for d in bands]) for q in range(9)]
         place_rows(rows, owner_total, one_hot(low_ids, low), owner_ids == high)
         return carry
 
-    lax.fori_loop(0, 32, place_owned, 0, unroll=4)
+    lax.fori_loop(0, 16, place_owned, 0, unroll=4)
     for q in range(9):
         for half in range(2):
             own_ref[q, 64 * half : 64 * half + 64, :] = owner_total[
@@ -705,9 +718,8 @@
             pltpu.VMEM((576, 128), f32),
             pltpu.VMEM((576, 128), f32),
             pltpu.VMEM((128, 256), f32),
-            pltpu.VMEM((5, 26, 32, 128), f32),
-            pltpu.VMEM((4, 256, 256), bf16),
-            pltpu.VMEM((4, 256, 256), bf16),
+            pltpu.VMEM((3, 26, 32, 128), f32),
+            pltpu.VMEM((2, 26, 16, 128), f32),
             *exchange_scratch(10),
             pltpu.SemaphoreType.DMA((4,)),
             pltpu.SemaphoreType.DMA((4,)),
@@ -715,8 +727,9 @@
             pltpu.SemaphoreType.DMA,
         ],
         compiler_params=pltpu.CompilerParams(
-            collective_id=1, has_side_effects=True, vmem_limit_bytes=VMEM_LIMIT
+            collective_id=1, has_side_effects=True, vmem_limit_bytes=34 * MIB
         ),
+        cost_estimate=pl.CostEstimate(flops=20_000_000_000, bytes_accessed=4_000_000, transcendentals=7_000_000),
         name="render_step",
     )(slots, lists, counts, view, back, target_tiles, send_index, send_count)
 
@@ -784,7 +797,7 @@
         in_specs=[block, block, block, grads, grads, smem, smem, smem, smem],
         out_specs=(block, block, block, pl.BlockSpec((1, 1), lambda i: (0, 0))),
         scratch_shapes=[pltpu.VMEM((59 * 8, 128), jnp.float32)],
-        compiler_params=pltpu.CompilerParams(vmem_limit_bytes=VMEM_LIMIT),
+        compiler_params=pltpu.CompilerParams(vmem_limit_bytes=16 * MIB),
         name="update",
     )(params, first_moment, second_moment, own, other, view, shear, offset, center)
 

time: 99.3 us -> 89.2 us (0.90)
  Pallas kernels: 96.8 us -> 86.1 us
    pallas_call x1, Pallas kernels: 58.2 us -> 51.5 us  [render_step(): pl.pallas_call(render_kernel, out_shape=(shape, shape), in_specs=[vmem, v...]
    pallas_call x1, Pallas kernels: 12.9 us -> 10.1 us  [update(): pl.pallas_call(update_kernel, grid=(16384 // BLOCK,), out_shape=(shape, s...]
    pallas_call x1, Pallas kernels: 25.7 us -> 24.4 us  [project_and_pick(): pl.pallas_call(project_kernel, grid=(16384 // BLOCK,), out_shape=jax.Shap...]
    unnamed x2 -> x26, local copies, waits for them, and re-layouts: 0.01 us -> 1.09 us
where the time goes in v5:
time: 89.2 us; the launch traced here: 89.1 us
  Pallas kernels  86.1 us (97%)
  local copies, waits for them, and re-layouts  2.15 us (2%)
    pallas_call x1, Pallas kernels, render_step(): pl.pallas_call(render_kernel, out_shape=(shape, shape), in_specs=[vmem, v...  51.5 us
    pallas_call x1, Pallas kernels, project_and_pick(): pl.pallas_call(project_kernel, grid=(16384 // BLOCK,), out_shape=jax.Shap...  24.4 us
    pallas_call x1, Pallas kernels, update(): pl.pallas_call(update_kernel, grid=(16384 // BLOCK,), out_shape=(shape, s...  10.1 us

profile of v5, /device:TPU:1, one launch (start us, length us, event | category | flops | bytes accessed | tf_op | source)
XLA Modules:
  0.0 89.1 jit_solution(2909935528252196165)
XLA Ops:
  0.6 0.0 copy-start.10
  0.6 0.0 copy-start.8
  0.7 0.0 copy-start.11
  0.7 0.0 copy-start.4
  0.7 0.0 copy-start.9
  0.7 0.0 copy-start.12
  0.7 24.4 %project_and_pick.1.slots_ref = f32[64,9,128]{2,1,0:T(8,128)} custom-call(f32[59,16384]{1,0:T(8,128)} %params_ref.3, s32[64,128]{1,0:T(8,128)} %bitcast.9, s32[1]{0:T(128)} %bitcast.1.view_ref, f32[2,2]{1,0:T(2,128)} %shear_ref.3, f32[2,2]{1,0:T(2,128)} %offset_ref.3, f32[2,3]{1,0:T(2,128)} %center_ref.3), custom_call_target="tpu_custom_call" | custom-call | tf_op jit(solution)/shard_map/project_and_pick/pallas_call | solution.py:302
  25.1 0.0 copy-done.12
  25.1 0.3 reshape_squeeze.3
  25.4 0.5 copy.17
  25.9 0.3 reshape.15.target_ref
  26.2 0.0 copy-done.10
  26.2 0.0 copy-done.8
  26.2 0.0 copy-done.11
  26.3 0.0 copy-done.4
  26.3 0.0 copy-done.9
  26.3 0.0 copy-start.3
  26.3 1.0 %copy-done.3 = f32[64,9,128]{2,1,0:T(8,128)S(1)} copy-done((f32[64,9,128]{2,1,0:T(8,128)S(1)}, f32[64,9,128]{2,1,0:T(8,128)}, u32[]{:S(2)}) %copy-start.3) | copy-done | bytes 294936
  27.3 0.0 copy-start
  27.3 0.0 copy-start.1
  27.3 0.0 copy-start.2
  27.3 0.0 copy-start.5
  27.3 0.0 copy-start.6
  27.3 0.0 copy-start.7
  27.4 51.5 %render_step.1 = (f32[10,128,128]{2,1,0:T(8,128)S(1)}, f32[10,128,128]{2,1,0:T(8,128)S(1)}) custom-call(f32[64,9,128]{2,1,0:T(8,128)S(1)} %copy-done.3, s32[32,256]{1,0:T(8,128)S(1)} %bitcast.11, s32[1,32]{1,0:T(1,128)S(1)} %copy-done.10, s32[1]{0:T(128)} %bitcast.1.view_ref, f32[2,3]{1,0:T(2,128)S(1)} %copy-done.9, f32[96,256]{1,0:T(8,128)S(1)} %reshape.15.target_ref, ...), custom_call_target="tpu_custom_call" | custom-call | flops 20000000000 | bytes 4000000 | tf_op jit(solution)/shard_map/render_step/pallas_call | solution.py:700
  78.9 0.0 copy-done
  78.9 0.0 copy-done.1
  78.9 0.0 copy-done.2
  78.9 0.0 copy-done.5
  78.9 0.0 copy-done.6
  78.9 0.0 copy-done.7
  78.9 10.1 %update.1 = (f32[59,16384]{1,0:T(8,128)}, f32[59,16384]{1,0:T(8,128)}, f32[59,16384]{1,0:T(8,128)}, f32[1,1]{1,0:T(1,128)}) custom-call(f32[59,16384]{1,0:T(8,128)S(1)} %copy-done, f32[59,16384]{1,0:T(8,128)S(1)} %copy-done.1, f32[59,16384]{1,0:T(8,128)S(1)} %copy-done.2, f32[10,128,128]{2,1,0:T(8,128)S(1)} %get-tuple-element.10.own_ref, ...), custom_call_target="tpu_custom_call" | custom-call | tf_op jit(solution)/shard_map/update/pallas_call | solution.py:793
Async XLA Ops:
  0.6 25.6 %copy-start.10 = (s32[1,32]{1,0:T(1,128)S(1)}, s32[1,32]{1,0:T(1,128)}, u32[]{:S(2)}) copy-start(s32[1,32]{1,0:T(1,128)} %count_ref.1) | copy-start | bytes 388
  0.6 25.6 %copy-start.8 = (s32[1,1,32,256]{3,2,1,0:T(8,128)S(1)}, s32[1,1,32,256]{3,2,1,0:T(8,128)}, u32[]{:S(2)}) copy-start(s32[1,1,32,256]{3,2,1,0:T(8,128)} %param.22) | copy-start | bytes 98308
  0.7 25.6 %copy-start.11 = (s32[1,64]{1,0:T(1,128)S(1)}, s32[1,64]{1,0:T(1,128)}, u32[]{:S(2)}) copy-start(s32[1,64]{1,0:T(1,128)} %sent_ref.1) | copy-start | bytes 772
  0.7 25.6 %copy-start.4 = (s32[1,64,128]{2,1,0:T(8,128)S(1)}, s32[1,64,128]{2,1,0:T(8,128)}, u32[]{:S(2)}) copy-start(s32[1,64,128]{2,1,0:T(8,128)} %param.20) | copy-start | bytes 98308
  0.7 25.6 %copy-start.9 = (f32[2,3]{1,0:T(2,128)S(1)}, f32[2,3]{1,0:T(2,128)}, u32[]{:S(2)}) copy-start(f32[2,3]{1,0:T(2,128)} %back_ref.1) | copy-start | bytes 76
  0.7 24.5 %copy-start.12 = (f32[1,3,16,512]{3,2,1,0:T(8,128)S(1)}, f32[1,3,16,512]{3,2,1,0:T(8,128)}, u32[]{:S(2)}) copy-start(f32[1,3,16,512]{3,2,1,0:T(8,128)} %param.15) | copy-start | bytes 294916
  26.3 1.0 %copy-start.3 = (f32[64,9,128]{2,1,0:T(8,128)S(1)}, f32[64,9,128]{2,1,0:T(8,128)}, u32[]{:S(2)}) copy-start(f32[64,9,128]{2,1,0:T(8,128)} %project_and_pick.1.slots_ref) | copy-start | bytes 884740
  27.3 51.5 %copy-start = (f32[59,16384]{1,0:T(8,128)S(1)}, f32[59,16384]{1,0:T(8,128)}, u32[]{:S(2)}) copy-start(f32[59,16384]{1,0:T(8,128)} %params_ref.3) | copy-start | bytes 11599876
  27.3 51.6 %copy-start.1 = (f32[59,16384]{1,0:T(8,128)S(1)}, f32[59,16384]{1,0:T(8,128)}, u32[]{:S(2)}) copy-start(f32[59,16384]{1,0:T(8,128)} %first_ref.1) | copy-start | bytes 11599876
  27.3 51.6 %copy-start.2 = (f32[59,16384]{1,0:T(8,128)S(1)}, f32[59,16384]{1,0:T(8,128)}, u32[]{:S(2)}) copy-start(f32[59,16384]{1,0:T(8,128)} %second_ref.1) | copy-start | bytes 11599876
  27.3 51.6 %copy-start.5 = (f32[2,2]{1,0:T(2,128)S(1)}, f32[2,2]{1,0:T(2,128)}, u32[]{:S(2)}) copy-start(f32[2,2]{1,0:T(2,128)} %shear_ref.3) | copy-start | bytes 52
  27.3 51.6 %copy-start.6 = (f32[2,2]{1,0:T(2,128)S(1)}, f32[2,2]{1,0:T(2,128)}, u32[]{:S(2)}) copy-start(f32[2,2]{1,0:T(2,128)} %offset_ref.3) | copy-start | bytes 52
  27.3 51.6 %copy-start.7 = (f32[2,3]{1,0:T(2,128)S(1)}, f32[2,3]{1,0:T(2,128)}, u32[]{:S(2)}) copy-start(f32[2,3]{1,0:T(2,128)} %center_ref.3) | copy-start | bytes 76

commit v6 on v5

--- a/solution.py
+++ b/solution.py
@@ -400,8 +400,8 @@
     keep = jnp.exp(both_parts(jnp.log(1.0 - cover), before[...], NN))
     cover_ref[tile] = cover
     keep_ref[tile] = keep
-    shown = mxu((cover * keep).astype(jnp.bfloat16), colors, NT)
-    total[...] += shown[:, 0:128] + shown[:, 128:256]
+    shown = mxu(jnp.concatenate(split2(cover * keep), axis=0), colors, NT)
+    total[...] += shown[0:256, 0:128] + shown[0:256, 128:256] + shown[256:512, 0:128]
 
 
 def backward_tile(tile, band, picked, after, cover_ref, keep_ref, grad_ref, results):
@@ -432,8 +432,9 @@
         sum_0 = sum_0 + piece
         sum_y = sum_y + piece_y
         sum_yy = sum_yy + piece_y * level
-    color_grad = mxu(both, weight.astype(jnp.bfloat16), NN)
-    color_grad = color_grad[0:3] + color_grad[3:6]
+    weight_high, weight_low = split2(weight)
+    color_grad = mxu(both, weight_high, NN)
+    color_grad = color_grad[0:3] + color_grad[3:6] + mxu(both, weight_low, NN)[0:3]
     sum_x = sum_0 * delta_x
 
     def fold(value):
@@ -738,9 +739,12 @@
 LOSS_TERMS = 2 * 3 * 1024 * 512
 
 
+STAGES = 4
+
+
 def update_kernel(
     params_ref, first_ref, second_ref, own_ref, other_ref, view_ref, shear_ref, offset_ref, center_ref,
-    params_out, first_out, second_out, loss_out, dense,
+    params_out, first_out, second_out, loss_out, dense, staged, copy_sem,
 ):
     refs = (shear_ref, offset_ref, center_ref)
     cameras = [camera_of(refs, 0), camera_of(refs, 1)]
@@ -748,7 +752,21 @@
     losses = own_ref[9, 0:1, :] + other_ref[9, 0:1, :]
     loss_out[...] = jnp.sum(losses, axis=1, keepdims=True) / LOSS_TERMS
 
+    def copies(slot, sub):
+        columns = pl.ds(pl.multiple_of(1024 * sub, 1024), 1024)
+        return [
+            pltpu.make_async_copy(staged.at[slot, k], out.at[:, columns], copy_sem.at[slot, k])
+            for k, out in enumerate((params_out, first_out, second_out))
+        ]
+
     def part(sub, carry):
+        slot = lax.rem(sub, STAGES)
+
+        @pl.when(sub >= STAGES)
+        def _():
+            for copy in copies(slot, sub - STAGES):
+                copy.wait()
+
         rows = dense_rows(params_ref, sub)
         _, pull_back = jax.vjp(lambda *values: project_rows(values, cameras), *rows)
         here = pl.ds(pl.multiple_of(8 * sub, 8), 8)
@@ -777,27 +795,36 @@
                 new_first = 0.9 * first_ref[here] + 0.1 * grad
                 new_second = 0.999 * second_ref[here] + 0.001 * grad * grad
                 scale = jnp.sqrt(new_second * (1.0 / (1.0 - 0.999**STEP_COUNT))) + 1e-15
-                params_out[here] = params_ref[here] - rate * new_first / scale
-                first_out[here] = new_first
-                second_out[here] = new_second
+                there = (slice(first, first + size), slice(128 * c, 128 * c + 128))
+                staged.at[slot, 0][there] = params_ref[here] - rate * new_first / scale
+                staged.at[slot, 1][there] = new_first
+                staged.at[slot, 2][there] = new_second
+        for copy in copies(slot, sub):
+            copy.start()
         return carry
 
-    lax.fori_loop(0, BLOCK // 1024, part, 0)
+    lax.fori_loop(0, 16, part, 0)
+    for sub in range(16 - STAGES, 16):
+        for copy in copies(sub % STAGES, sub):
+            copy.wait()
 
 
 def update(params, first_moment, second_moment, own, other, view, shear, offset, center):
     smem = pl.BlockSpec(memory_space=pltpu.SMEM)
-    block = pl.BlockSpec((59, BLOCK), lambda i: (0, i))
-    grads = pl.BlockSpec((10, BLOCK // 128, 128), lambda i: (0, i, 0))
+    vmem = pl.BlockSpec(memory_space=pltpu.VMEM)
+    anywhere = pl.BlockSpec(memory_space=pl.ANY)
     shape = jax.ShapeDtypeStruct(params.shape, jnp.float32)
     return pl.pallas_call(
         update_kernel,
-        grid=(16384 // BLOCK,),
         out_shape=(shape, shape, shape, jax.ShapeDtypeStruct((1, 1), jnp.float32)),
-        in_specs=[block, block, block, grads, grads, smem, smem, smem, smem],
-        out_specs=(block, block, block, pl.BlockSpec((1, 1), lambda i: (0, 0))),
-        scratch_shapes=[pltpu.VMEM((59 * 8, 128), jnp.float32)],
-        compiler_params=pltpu.CompilerParams(vmem_limit_bytes=16 * MIB),
+        in_specs=[vmem, vmem, vmem, vmem, vmem, smem, smem, smem, smem],
+        out_specs=(anywhere, anywhere, anywhere, vmem),
+        scratch_shapes=[
+            pltpu.VMEM((59 * 8, 128), jnp.float32),
+            pltpu.VMEM((STAGES, 3, 59, 1024), jnp.float32),
+            pltpu.SemaphoreType.DMA((STAGES, 3)),
+        ],
+        compiler_params=pltpu.CompilerParams(vmem_limit_bytes=24 * MIB),
         name="update",
     )(params, first_moment, second_moment, own, other, view, shear, offset, center)
 

time: 89.2 us -> 87.8 us (0.984)
  Pallas kernels: 86.1 us -> 84.6 us
    pallas_call x1, Pallas kernels: 10.1 us -> 8.86 us  [update(): pl.pallas_call(update_kernel, out_shape=(shape, shape, shape, jax.ShapeDt...]
where the time goes in v6:
time: 87.8 us; the launch traced here: 87.6 us
  Pallas kernels  84.6 us (96%)
  local copies, waits for them, and re-layouts  2.15 us (2%)
    pallas_call x1, Pallas kernels, render_step(): pl.pallas_call(render_kernel, out_shape=(shape, shape), in_specs=[vmem, v...  51.3 us
    pallas_call x1, Pallas kernels, project_and_pick(): pl.pallas_call(project_kernel, grid=(16384 // BLOCK,), out_shape=jax.Shap...  24.4 us
    pallas_call x1, Pallas kernels, update(): pl.pallas_call(update_kernel, out_shape=(shape, shape, shape, jax.ShapeDt...  8.86 us

profile of v6, /device:TPU:1, one launch (start us, length us, event | category | flops | bytes accessed | tf_op | source)
XLA Modules:
  0.0 87.6 jit_solution(12297771822327766769)
XLA Ops:
  0.6 0.0 copy-start.10
  0.6 0.0 copy-start.8
  0.7 0.0 copy-start.11
  0.7 0.0 copy-start.4
  0.7 0.0 copy-start.9
  0.7 0.0 copy-start.12
  0.7 24.4 %project_and_pick.1.slots_ref = f32[64,9,128]{2,1,0:T(8,128)} custom-call(f32[59,16384]{1,0:T(8,128)} %params_ref.3, s32[64,128]{1,0:T(8,128)} %bitcast.9, s32[1]{0:T(128)} %bitcast.1.view_ref, f32[2,2]{1,0:T(2,128)} %shear_ref.3, f32[2,2]{1,0:T(2,128)} %offset_ref.3, f32[2,3]{1,0:T(2,128)} %center_ref.3), custom_call_target="tpu_custom_call" | custom-call | tf_op jit(solution)/shard_map/project_and_pick/pallas_call | solution.py:302
  25.1 0.0 copy-done.12
  25.1 0.3 reshape_squeeze.3
  25.4 0.5 copy.17
  25.9 0.3 reshape.15.target_ref
  26.2 0.0 copy-done.10
  26.2 0.0 copy-done.8
  26.2 0.0 copy-done.11
  26.3 0.0 copy-done.4
  26.3 0.0 copy-done.9
  26.3 0.0 copy-start.3
  26.3 1.0 %copy-done.3 = f32[64,9,128]{2,1,0:T(8,128)S(1)} copy-done((f32[64,9,128]{2,1,0:T(8,128)S(1)}, f32[64,9,128]{2,1,0:T(8,128)}, u32[]{:S(2)}) %copy-start.3) | copy-done | bytes 294936
  27.3 0.0 copy-start
  27.3 0.0 copy-start.1
  27.3 0.0 copy-start.2
  27.3 0.0 copy-start.5
  27.3 0.0 copy-start.6
  27.3 0.0 copy-start.7
  27.4 51.3 %render_step.1 = (f32[10,128,128]{2,1,0:T(8,128)S(1)}, f32[10,128,128]{2,1,0:T(8,128)S(1)}) custom-call(f32[64,9,128]{2,1,0:T(8,128)S(1)} %copy-done.3, s32[32,256]{1,0:T(8,128)S(1)} %bitcast.11, s32[1,32]{1,0:T(1,128)S(1)} %copy-done.10, s32[1]{0:T(128)} %bitcast.1.view_ref, f32[2,3]{1,0:T(2,128)S(1)} %copy-done.9, f32[96,256]{1,0:T(8,128)S(1)} %reshape.15.target_ref, ...), custom_call_target="tpu_custom_call" | custom-call | flops 20000000000 | bytes 4000000 | tf_op jit(solution)/shard_map/render_step/pallas_call | solution.py:701
  78.7 0.0 copy-done
  78.7 0.0 copy-done.1
  78.7 0.0 copy-done.2
  78.7 0.0 copy-done.5
  78.7 0.0 copy-done.6
  78.7 0.0 copy-done.7
  78.7 8.9 %update.1 = (f32[59,16384]{1,0:T(8,128)}, f32[59,16384]{1,0:T(8,128)}, f32[59,16384]{1,0:T(8,128)}, f32[1,1]{1,0:T(1,128)}) custom-call(f32[59,16384]{1,0:T(8,128)S(1)} %copy-done, f32[59,16384]{1,0:T(8,128)S(1)} %copy-done.1, f32[59,16384]{1,0:T(8,128)S(1)} %copy-done.2, f32[10,128,128]{2,1,0:T(8,128)S(1)} %get-tuple-element.10.own_ref, ...), custom_call_target="tpu_custom_call" | custom-call | tf_op jit(solution)/shard_map/update/pallas_call | solution.py:817
Async XLA Ops:
  0.6 25.6 %copy-start.10 = (s32[1,32]{1,0:T(1,128)S(1)}, s32[1,32]{1,0:T(1,128)}, u32[]{:S(2)}) copy-start(s32[1,32]{1,0:T(1,128)} %count_ref.1) | copy-start | bytes 388
  0.6 25.6 %copy-start.8 = (s32[1,1,32,256]{3,2,1,0:T(8,128)S(1)}, s32[1,1,32,256]{3,2,1,0:T(8,128)}, u32[]{:S(2)}) copy-start(s32[1,1,32,256]{3,2,1,0:T(8,128)} %param.22) | copy-start | bytes 98308
  0.7 25.6 %copy-start.11 = (s32[1,64]{1,0:T(1,128)S(1)}, s32[1,64]{1,0:T(1,128)}, u32[]{:S(2)}) copy-start(s32[1,64]{1,0:T(1,128)} %sent_ref.1) | copy-start | bytes 772
  0.7 25.6 %copy-start.4 = (s32[1,64,128]{2,1,0:T(8,128)S(1)}, s32[1,64,128]{2,1,0:T(8,128)}, u32[]{:S(2)}) copy-start(s32[1,64,128]{2,1,0:T(8,128)} %param.20) | copy-start | bytes 98308
  0.7 25.6 %copy-start.9 = (f32[2,3]{1,0:T(2,128)S(1)}, f32[2,3]{1,0:T(2,128)}, u32[]{:S(2)}) copy-start(f32[2,3]{1,0:T(2,128)} %back_ref.1) | copy-start | bytes 76
  0.7 24.5 %copy-start.12 = (f32[1,3,16,512]{3,2,1,0:T(8,128)S(1)}, f32[1,3,16,512]{3,2,1,0:T(8,128)}, u32[]{:S(2)}) copy-start(f32[1,3,16,512]{3,2,1,0:T(8,128)} %param.15) | copy-start | bytes 294916
  26.3 1.0 %copy-start.3 = (f32[64,9,128]{2,1,0:T(8,128)S(1)}, f32[64,9,128]{2,1,0:T(8,128)}, u32[]{:S(2)}) copy-start(f32[64,9,128]{2,1,0:T(8,128)} %project_and_pick.1.slots_ref) | copy-start | bytes 884740
  27.3 51.4 %copy-start = (f32[59,16384]{1,0:T(8,128)S(1)}, f32[59,16384]{1,0:T(8,128)}, u32[]{:S(2)}) copy-start(f32[59,16384]{1,0:T(8,128)} %params_ref.3) | copy-start | bytes 11599876
  27.3 51.4 %copy-start.1 = (f32[59,16384]{1,0:T(8,128)S(1)}, f32[59,16384]{1,0:T(8,128)}, u32[]{:S(2)}) copy-start(f32[59,16384]{1,0:T(8,128)} %first_ref.1) | copy-start | bytes 11599876
  27.3 51.4 %copy-start.2 = (f32[59,16384]{1,0:T(8,128)S(1)}, f32[59,16384]{1,0:T(8,128)}, u32[]{:S(2)}) copy-start(f32[59,16384]{1,0:T(8,128)} %second_ref.1) | copy-start | bytes 11599876
  27.3 51.4 %copy-start.5 = (f32[2,2]{1,0:T(2,128)S(1)}, f32[2,2]{1,0:T(2,128)}, u32[]{:S(2)}) copy-start(f32[2,2]{1,0:T(2,128)} %shear_ref.3) | copy-start | bytes 52
  27.3 51.4 %copy-start.6 = (f32[2,2]{1,0:T(2,128)S(1)}, f32[2,2]{1,0:T(2,128)}, u32[]{:S(2)}) copy-start(f32[2,2]{1,0:T(2,128)} %offset_ref.3) | copy-start | bytes 52
  27.3 51.4 %copy-start.7 = (f32[2,3]{1,0:T(2,128)S(1)}, f32[2,3]{1,0:T(2,128)}, u32[]{:S(2)}) copy-start(f32[2,3]{1,0:T(2,128)} %center_ref.3) | copy-start | bytes 76

commit v7 on v6

--- a/solution.py
+++ b/solution.py
@@ -170,29 +170,21 @@
         pl.semaphore_signal(semaphore, inc=1, device_id={"tile": peer}, device_id_type=MESH)
 
 
-def greet_all(step, semaphores):
+def greet_all(stage, semaphores):
     plane_sem, cube_sem = semaphores
     me = lax.axis_index("tile")
     lines = [axis_peers(me, stride) for stride in (1, 4, 16)]
     barrier = pltpu.get_barrier_semaphore()
-
-    @pl.when(step == 0)
-    def _():
+    if stage == 0:
         for line in lines:
             signal_all(barrier, line)
-
-    @pl.when(step == 1)
-    def _():
+    elif stage == 1:
         pl.semaphore_wait(barrier, 9)
         signal_all(plane_sem, lines[1])
-
-    @pl.when(step == 2)
-    def _():
+    elif stage == 2:
         pl.semaphore_wait(plane_sem, 3)
         signal_all(cube_sem, lines[2])
-
-    @pl.when(step == 3)
-    def _():
+    else:
         pl.semaphore_wait(cube_sem, 3)
 
 
@@ -239,84 +231,102 @@
 
 
 def project_kernel(
-    params_ref, index_ref, view_ref, shear_ref, offset_ref, center_ref, out_ref,
-    table, high_parts, low_parts, outgoing, incoming, send_sem, recv_sem, *greetings,
+    source_ref, index_ref, view_ref, shear_ref, offset_ref, center_ref, incoming,
+    params_ref, table, high_parts, low_parts, outgoing, send_sem, recv_sem, plane_sem, cube_sem, load_sem,
 ):
-    step = pl.program_id(0)
-    greet_all(step, greetings)
+    greetings = (plane_sem, cube_sem)
+    loads = [
+        pltpu.make_async_copy(
+            source_ref.at[:, pl.ds(BLOCK * k, BLOCK)], params_ref.at[:, pl.ds(BLOCK * k, BLOCK)], load_sem.at[k]
+        )
+        for k in range(16384 // BLOCK)
+    ]
+    for load in loads:
+        load.start()
+    greet_all(0, greetings)
     camera = camera_of((shear_ref, offset_ref, center_ref), view_ref[0])
 
     def part(sub, carry):
         record = project_rows(dense_rows(params_ref, sub), [camera])[0]
-        first = pl.multiple_of(step * (BLOCK // 128) + 8 * sub, 8)
+        first = pl.multiple_of(8 * sub, 8)
         for q in range(9):
             table[q, pl.ds(first, 8), :] = record[q]
         return carry
 
-    lax.fori_loop(0, BLOCK // 1024, part, 0, unroll=2)
-
-    @pl.when(step == pl.num_programs(0) - 1)
-    def _():
+    for k, load in enumerate(loads):
+        load.wait()
+        lax.fori_loop(k * BLOCK // 1024, (k + 1) * BLOCK // 1024, part, 0, unroll=2)
+        if k == 1:
+            greet_all(1, greetings)
+    greet_all(2, greetings)
+    for q in range(9):
+        for half in range(2):
+            store_parts(
+                table[q, 64 * half : 64 * half + 64, :],
+                high_parts, low_parts, q, pl.ds(128 * half, 128),
+            )
+    low_ids = lax.broadcasted_iota(jnp.int32, (256, 256), 0)
+    high_ids = lax.broadcasted_iota(jnp.int32, (64, 256), 0)
+
+    def pick(pair, carry):
+        index = jnp.concatenate(
+            [index_ref[pl.ds(pair, 1), :], index_ref[pl.ds(pair + 32, 1), :]], axis=1
+        )
+        high = (index >> 7) & 63
+        low = (index & 127) + ((index >> 13) << 7)
+        rows = pick_rows(high_parts, low_parts, one_hot(low_ids, low), high_ids == high)
         for q in range(9):
-            for half in range(2):
-                store_parts(
-                    table[q, 64 * half : 64 * half + 64, :],
-                    high_parts, low_parts, q, pl.ds(128 * half, 128),
-                )
-        low_ids = lax.broadcasted_iota(jnp.int32, (256, 256), 0)
-        high_ids = lax.broadcasted_iota(jnp.int32, (64, 256), 0)
-
-        def pick(pair, carry):
-            index = jnp.concatenate(
-                [index_ref[pl.ds(pair, 1), :], index_ref[pl.ds(pair + 32, 1), :]], axis=1
-            )
-            high = (index >> 7) & 63
-            low = (index & 127) + ((index >> 13) << 7)
-            rows = pick_rows(high_parts, low_parts, one_hot(low_ids, low), high_ids == high)
-            for q in range(9):
-                outgoing[pair, q : q + 1, :] = rows[q][:, 0:128]
-                outgoing[pair + 32, q : q + 1, :] = rows[q][:, 128:256]
+            outgoing[pair, q : q + 1, :] = rows[q][:, 0:128]
+            outgoing[pair + 32, q : q + 1, :] = rows[q][:, 128:256]
+        return carry
+
+    me = lax.axis_index("tile")
+
+    def group(part, carry):
+        first = lax.rem(part + me, 4) * 8
+        lax.fori_loop(0, 8, lambda k, carry: pick(first + k, carry), 0, unroll=4)
+
+        @pl.when(part == 0)
+        def _():
+            greet_all(3, greetings)
+
+        def send(k, carry):
+            for peer in (first + k, first + k + 32):
+                send_block(outgoing, incoming, send_sem, recv_sem, peer)
             return carry
 
-        me = lax.axis_index("tile")
-
-        def group(part, carry):
-            first = lax.rem(part + me, 4) * 8
-            lax.fori_loop(0, 8, lambda k, carry: pick(first + k, carry), 0, unroll=4)
-
-            def send(k, carry):
-                for peer in (first + k, first + k + 32):
-                    send_block(outgoing, incoming, send_sem, recv_sem, peer)
-                return carry
-
-            lax.fori_loop(0, 8, send, 0)
-            return carry
-
-        lax.fori_loop(0, 4, group, 0)
-        finish_blocks(outgoing, incoming, send_sem, recv_sem)
-        out_ref[...] = incoming[...]
+        lax.fori_loop(0, 8, send, 0)
+        return carry
+
+    lax.fori_loop(0, 4, group, 0)
+    finish_blocks(outgoing, incoming, send_sem, recv_sem)
 
 
 def project_and_pick(params, send_index, view, shear, offset, center):
     smem = pl.BlockSpec(memory_space=pltpu.SMEM)
     return pl.pallas_call(
         project_kernel,
-        grid=(16384 // BLOCK,),
         out_shape=jax.ShapeDtypeStruct((64, 9, 128), jnp.float32),
         in_specs=[
-            pl.BlockSpec((59, BLOCK), lambda i: (0, i)),
-            pl.BlockSpec((64, 128), lambda i: (0, 0)),
+            pl.BlockSpec(memory_space=pl.ANY),
+            pl.BlockSpec(memory_space=pltpu.VMEM),
             smem,
             smem,
             smem,
             smem,
         ],
-        out_specs=pl.BlockSpec((64, 9, 128), lambda i: (0, 0, 0)),
+        out_specs=pl.BlockSpec(memory_space=pltpu.VMEM),
         scratch_shapes=[
+            pltpu.VMEM((59, 16384), jnp.float32),
             pltpu.VMEM((9, 128, 128), jnp.float32),
             pltpu.VMEM((576, 512), jnp.bfloat16),
             pltpu.VMEM((128, 256), jnp.bfloat16),
-            *exchange_scratch(9),
+            pltpu.VMEM((64, 9, 128), jnp.float32),
+            pltpu.SemaphoreType.DMA,
+            pltpu.SemaphoreType.DMA,
+            pltpu.SemaphoreType.REGULAR,
+            pltpu.SemaphoreType.REGULAR,
+            pltpu.SemaphoreType.DMA((16384 // BLOCK,)),
         ],
         compiler_params=pltpu.CompilerParams(
             collective_id=0, has_side_effects=True, vmem_limit_bytes=56 * MIB

time: 87.8 us -> 84.9 us (0.967)
  Pallas kernels: 84.6 us -> 81.7 us
    pallas_call x1, Pallas kernels: 24.4 us -> 22.5 us  [project_and_pick(): pl.pallas_call(project_kernel, out_shape=jax.ShapeDtypeStruct((64, 9, 128...]
    pallas_call x1, Pallas kernels: 51.3 us -> 50.4 us  [render_step(): pl.pallas_call(render_kernel, out_shape=(shape, shape), in_specs=[vmem, v...]
where the time goes in v7:
time: 84.9 us; the launch traced here: 84.7 us
  Pallas kernels  81.7 us (96%)
  local copies, waits for them, and re-layouts  2.15 us (3%)
    pallas_call x1, Pallas kernels, render_step(): pl.pallas_call(render_kernel, out_shape=(shape, shape), in_specs=[vmem, v...  50.4 us
    pallas_call x1, Pallas kernels, project_and_pick(): pl.pallas_call(project_kernel, out_shape=jax.ShapeDtypeStruct((64, 9, 128...  22.5 us
    pallas_call x1, Pallas kernels, update(): pl.pallas_call(update_kernel, out_shape=(shape, shape, shape, jax.ShapeDt...  8.86 us

profile of v7, /device:TPU:1, one launch (start us, length us, event | category | flops | bytes accessed | tf_op | source)
XLA Modules:
  0.0 84.7 jit_solution(5477505113942160915)
XLA Ops:
  0.6 0.0 copy-start.10
  0.6 0.0 copy-start.8
  0.7 0.0 copy-start.11
  0.7 0.0 copy-start.4
  0.7 0.0 copy-start.9
  0.7 0.0 copy-start.12
  0.7 22.5 %project_and_pick.1.slots_ref = f32[64,9,128]{2,1,0:T(8,128)} custom-call(f32[59,16384]{1,0:T(8,128)} %params_ref.1, s32[64,128]{1,0:T(8,128)} %bitcast.9, s32[1]{0:T(128)} %bitcast.1.view_ref, f32[2,2]{1,0:T(2,128)} %shear_ref.3, f32[2,2]{1,0:T(2,128)} %offset_ref.3, f32[2,3]{1,0:T(2,128)} %center_ref.3), custom_call_target="tpu_custom_call" | custom-call | tf_op jit(solution)/shard_map/project_and_pick/pallas_call | solution.py:307
  23.2 0.0 copy-done.12
  23.2 0.3 reshape_squeeze.3
  23.5 0.5 copy.17
  23.9 0.3 reshape.15.target_ref
  24.3 0.0 copy-done.10
  24.3 0.0 copy-done.8
  24.3 0.0 copy-done.11
  24.3 0.0 copy-done.4
  24.3 0.0 copy-done.9
  24.3 0.0 copy-start.3
  24.3 1.0 %copy-done.3 = f32[64,9,128]{2,1,0:T(8,128)S(1)} copy-done((f32[64,9,128]{2,1,0:T(8,128)S(1)}, f32[64,9,128]{2,1,0:T(8,128)}, u32[]{:S(2)}) %copy-start.3) | copy-done | bytes 294936
  25.3 0.0 copy-start
  25.3 0.0 copy-start.1
  25.4 0.0 copy-start.2
  25.4 0.0 copy-start.5
  25.4 0.0 copy-start.6
  25.4 0.0 copy-start.7
  25.4 50.4 %render_step.1 = (f32[10,128,128]{2,1,0:T(8,128)S(1)}, f32[10,128,128]{2,1,0:T(8,128)S(1)}) custom-call(f32[64,9,128]{2,1,0:T(8,128)S(1)} %copy-done.3, s32[32,256]{1,0:T(8,128)S(1)} %bitcast.11, s32[1,32]{1,0:T(1,128)S(1)} %copy-done.10, s32[1]{0:T(128)} %bitcast.1.view_ref, f32[2,3]{1,0:T(2,128)S(1)} %copy-done.9, f32[96,256]{1,0:T(8,128)S(1)} %reshape.15.target_ref, ...), custom_call_target="tpu_custom_call" | custom-call | flops 20000000000 | bytes 4000000 | tf_op jit(solution)/shard_map/render_step/pallas_call | solution.py:711
  75.8 0.0 copy-done
  75.8 0.0 copy-done.1
  75.8 0.0 copy-done.2
  75.8 0.0 copy-done.5
  75.8 0.0 copy-done.6
  75.8 0.0 copy-done.7
  75.8 8.9 %update.1 = (f32[59,16384]{1,0:T(8,128)}, f32[59,16384]{1,0:T(8,128)}, f32[59,16384]{1,0:T(8,128)}, f32[1,1]{1,0:T(1,128)}) custom-call(f32[59,16384]{1,0:T(8,128)S(1)} %copy-done, f32[59,16384]{1,0:T(8,128)S(1)} %copy-done.1, f32[59,16384]{1,0:T(8,128)S(1)} %copy-done.2, f32[10,128,128]{2,1,0:T(8,128)S(1)} %get-tuple-element.10.own_ref, ...), custom_call_target="tpu_custom_call" | custom-call | tf_op jit(solution)/shard_map/update/pallas_call | solution.py:827
Async XLA Ops:
  0.6 23.6 %copy-start.10 = (s32[1,32]{1,0:T(1,128)S(1)}, s32[1,32]{1,0:T(1,128)}, u32[]{:S(2)}) copy-start(s32[1,32]{1,0:T(1,128)} %count_ref.1) | copy-start | bytes 388
  0.6 23.6 %copy-start.8 = (s32[1,1,32,256]{3,2,1,0:T(8,128)S(1)}, s32[1,1,32,256]{3,2,1,0:T(8,128)}, u32[]{:S(2)}) copy-start(s32[1,1,32,256]{3,2,1,0:T(8,128)} %param.22) | copy-start | bytes 98308
  0.7 23.6 %copy-start.11 = (s32[1,64]{1,0:T(1,128)S(1)}, s32[1,64]{1,0:T(1,128)}, u32[]{:S(2)}) copy-start(s32[1,64]{1,0:T(1,128)} %sent_ref.1) | copy-start | bytes 772
  0.7 23.6 %copy-start.4 = (s32[1,64,128]{2,1,0:T(8,128)S(1)}, s32[1,64,128]{2,1,0:T(8,128)}, u32[]{:S(2)}) copy-start(s32[1,64,128]{2,1,0:T(8,128)} %param.20) | copy-start | bytes 98308
  0.7 23.6 %copy-start.9 = (f32[2,3]{1,0:T(2,128)S(1)}, f32[2,3]{1,0:T(2,128)}, u32[]{:S(2)}) copy-start(f32[2,3]{1,0:T(2,128)} %back_ref.1) | copy-start | bytes 76
  0.7 22.5 %copy-start.12 = (f32[1,3,16,512]{3,2,1,0:T(8,128)S(1)}, f32[1,3,16,512]{3,2,1,0:T(8,128)}, u32[]{:S(2)}) copy-start(f32[1,3,16,512]{3,2,1,0:T(8,128)} %param.15) | copy-start | bytes 294916
  24.3 1.0 %copy-start.3 = (f32[64,9,128]{2,1,0:T(8,128)S(1)}, f32[64,9,128]{2,1,0:T(8,128)}, u32[]{:S(2)}) copy-start(f32[64,9,128]{2,1,0:T(8,128)} %project_and_pick.1.slots_ref) | copy-start | bytes 884740
  25.3 50.4 %copy-start = (f32[59,16384]{1,0:T(8,128)S(1)}, f32[59,16384]{1,0:T(8,128)}, u32[]{:S(2)}) copy-start(f32[59,16384]{1,0:T(8,128)} %params_ref.1) | copy-start | bytes 11599876
  25.3 50.4 %copy-start.1 = (f32[59,16384]{1,0:T(8,128)S(1)}, f32[59,16384]{1,0:T(8,128)}, u32[]{:S(2)}) copy-start(f32[59,16384]{1,0:T(8,128)} %first_ref.1) | copy-start | bytes 11599876
  25.4 50.5 %copy-start.2 = (f32[59,16384]{1,0:T(8,128)S(1)}, f32[59,16384]{1,0:T(8,128)}, u32[]{:S(2)}) copy-start(f32[59,16384]{1,0:T(8,128)} %second_ref.1) | copy-start | bytes 11599876
  25.4 50.5 %copy-start.5 = (f32[2,2]{1,0:T(2,128)S(1)}, f32[2,2]{1,0:T(2,128)}, u32[]{:S(2)}) copy-start(f32[2,2]{1,0:T(2,128)} %shear_ref.3) | copy-start | bytes 52
  25.4 50.5 %copy-start.6 = (f32[2,2]{1,0:T(2,128)S(1)}, f32[2,2]{1,0:T(2,128)}, u32[]{:S(2)}) copy-start(f32[2,2]{1,0:T(2,128)} %offset_ref.3) | copy-start | bytes 52
  25.4 50.5 %copy-start.7 = (f32[2,3]{1,0:T(2,128)S(1)}, f32[2,3]{1,0:T(2,128)}, u32[]{:S(2)}) copy-start(f32[2,3]{1,0:T(2,128)} %center_ref.3) | copy-start | bytes 76
